TPU v7x, 256 devices: a whole 4x4x8 slice. The times are simulated.
256 devices in a mesh: row: 16 (over z, x_lo), col: 16 (over x_hi, y, core).
Axes of the slice: x: 4 (x_hi: 2, x_lo: 2; x = x_hi * 2 + x_lo), y: 4, z: 8, core: 2. Of those that a mesh axis runs over, the one named last changes fastest.
Arguments:
- p_values: bfloat16 [192, 2048, 128], P('row', 'col'), may hold values from -0.8984375 to 0.8984375
- p_where: int32 [192, 32], P('row', 'col'), may hold values from 0 to 127, as said below
- p_count: int32 [16, 16], P('row', 'col'), may hold values from 6 to 12, as said below
- h_values: bfloat16 [192, 2048, 128], P('row', 'col'), may hold values from -3 to 3
- h_where: int32 [192, 32], P('row', 'col'), may hold values from 0 to 127, as said below
- h_count: int32 [16, 16], P('row', 'col'), may hold values from 6 to 12, as said below
Outputs:
- ph_values: bfloat16 [192, 2048, 128], P('row', 'col')
- php_values: bfloat16 [192, 2048, 128], P('row', 'col')
- energy: float32 [], replicated
Inputs may be any that keep to these rules, and one draw needn't show every extreme that they name: `p_where`: the 12 slots of the device of row index i and column index j name distinct blocks of its own tile: block rows i * 8 to i * 8 + 7 and the j-th of 16 equal ranges of block columns. `h_where`: as for p_where. `p_count`: some device has all 12 slots live. `h_count`: some device has all 12 slots live.
All inputs are finite; a program needn't handle non-finite values.
Results may differ from a plain program's by a relative error of at most 0.0049.
Values may be sent and summed in bfloat16 or wider, within the bound.
No kernel may reach another device: no remote copies, remote signals or barrier semaphores. Data moves between devices by JAX's collectives and lax.ppermute only.
A program may use at most 64 MiB of HBM per device.

v0:
```python
import functools

import jax
import jax.numpy as jnp
from jax import lax
from jax.sharding import Mesh
from jax.sharding import PartitionSpec as P

TILE = 8
ROW = ("row_0", "row_1")
COL = ("col_0", "col_1", "col_2")
ROW_COL = ("row_0", "row_1", "col_0", "col_1", "col_2")


def whole_of(shard, axes, dim):
    for axis in reversed(axes):
        shard = lax.all_gather(shard, axis, axis=dim, tiled=True)
    return shard


def by_axis(shard, axes):
    return functools.reduce(lax.psum, axes, shard)


def contribute(total_sum, left_tile, right_tile, band_index, out_where):
    left_vals, left_where, left_count = left_tile
    right_vals, right_where, right_count = right_tile
    slot_count = left_vals.shape[0]
    inner_blocks = band_index * TILE + jnp.arange(TILE, dtype=jnp.int32)
    left_live = jnp.arange(slot_count, dtype=jnp.int32) < left_count[0, 0]
    right_live = jnp.arange(slot_count, dtype=jnp.int32) < right_count[0, 0]
    match_left = (
        (left_where[None, None, :, 0] == out_where[:, None, None, 0])
        & (left_where[None, None, :, 1] == inner_blocks[None, :, None])
        & left_live[None, None, :]
    )
    match_right = (
        (right_where[None, None, :, 1] == out_where[:, None, None, 1])
        & (right_where[None, None, :, 0] == inner_blocks[None, :, None])
        & right_live[None, None, :]
    )
    pick_left = jnp.argmax(match_left.astype(jnp.int32), axis=2)
    pick_right = jnp.argmax(match_right.astype(jnp.int32), axis=2)
    has_left = jnp.any(match_left, axis=2)
    has_right = jnp.any(match_right, axis=2)
    nothing = jnp.zeros((), jnp.bfloat16)

    def slot_product(items):
        left_pick, left_has, right_pick, right_has = items
        row_blocks = jnp.where(left_has[:, None, None], left_vals[left_pick], nothing)
        col_blocks = jnp.where(right_has[:, None, None], right_vals[right_pick], nothing)
        return jnp.einsum("kxy,kyz->xz", row_blocks, col_blocks, preferred_element_type=jnp.float32)

    return total_sum + lax.map(slot_product, (pick_left, has_left, pick_right, has_right))


def pick_tile(gathered, owner, slot_count):
    all_vals, all_where, all_count = gathered
    start = (owner * slot_count).astype(jnp.int32)
    vals = lax.dynamic_slice_in_dim(all_vals, start, slot_count, 0)
    where = lax.dynamic_slice_in_dim(all_where, start, slot_count, 0)
    count = lax.dynamic_slice_in_dim(all_count, owner.astype(jnp.int32), 1, 0)
    return (vals, where, count)


def multiply(left_tile, right_tile, out_where):
    rows_count = lax.axis_size(ROW)
    cols_count = lax.axis_size(COL)
    band_ratio = rows_count // cols_count
    slot_count = out_where.shape[0]
    block_size = left_tile[0].shape[1]
    zero_sum = jnp.zeros((slot_count, block_size, block_size), jnp.float32)
    left_all = (
        lax.all_gather(left_tile[0], COL, axis=0, tiled=True),
        lax.all_gather(left_tile[1], COL, axis=0, tiled=True),
        lax.all_gather(left_tile[2], COL, axis=0, tiled=True),
    )
    right_all = (
        whole_of(right_tile[0], ROW, 0),
        whole_of(right_tile[1], ROW, 0),
        whole_of(right_tile[2], ROW, 0),
    )

    def band_step(band_index, total_sum):
        left_here = pick_tile(left_all, band_index // band_ratio, slot_count)
        right_here = pick_tile(right_all, band_index, slot_count)
        return contribute(total_sum, left_here, right_here, band_index, out_where)

    return lax.fori_loop(0, rows_count, band_step, zero_sum)


def per_device(p_values, p_where, p_count, h_values, h_where, h_count):
    slot_count = p_values.shape[0]
    live_slots = jnp.arange(slot_count, dtype=jnp.int32) < p_count[0, 0]
    density_tile = (p_values, p_where, p_count)
    first_sum = multiply(density_tile, (h_values, h_where, h_count), p_where)
    first_sum = jnp.where(live_slots[:, None, None], first_sum, jnp.float32(0.0))
    traces = jnp.trace(first_sum, axis1=1, axis2=2)
    diagonal = live_slots & (p_where[:, 0] == p_where[:, 1])
    local_energy = jnp.sum(jnp.where(diagonal, traces, jnp.float32(0.0)))
    ph_values = first_sum.astype(jnp.bfloat16)
    second_sum = multiply((ph_values, p_where, p_count), density_tile, p_where)
    php_values = jnp.where(live_slots[:, None, None], second_sum, jnp.float32(0.0)).astype(
        jnp.bfloat16
    )
    energy = by_axis(local_energy, ROW_COL)
    return (ph_values, php_values, energy)


def solution(mesh):
    torus = Mesh(mesh.devices.reshape(8, 2, 2, 4, 2), ("row_0", "row_1", "col_0", "col_1", "col_2"))
    in_specs = (
        P(ROW, COL, None),
        P(ROW, COL),
        P(ROW, COL),
        P(ROW, COL, None),
        P(ROW, COL),
        P(ROW, COL),
    )
    out_specs = (P(ROW, COL, None), P(ROW, COL, None), P())
    return jax.shard_map(
        per_device, mesh=torus, in_specs=in_specs, out_specs=out_specs, check_vma=False
    )
```

profile of v0, /device:TPU:2, one launch (start us, length us, event | category | flops | bytes accessed | tf_op | source)
XLA Modules:
  0.0 1091.4 jit_solution(13348728796765932657)
XLA Ops:
  7.2 13.6 %all_gather.57 = bf16[24,128,128]{2,1,0:T(8,128)(2,1)} all-gather(bf16[12,128,128]{2,1,0:T(8,128)(2,1)} %param.17), channel_id=1, replica_groups=mesh['row_0'=8,'row_1'=2,'col_0'=2,'col_1'=4,'col_2'=2] {'row_1'}, dimensions={0}, use_global_device_ids=true | all-gather | bytes 1179648 | tf_op jit(solution)/shard_map/all_gather | solution.py:17
  21.6 15.7 %all_gather.64 = bf16[24,128,128]{2,1,0:T(8,128)(2,1)} all-gather(bf16[12,128,128]{2,1,0:T(8,128)(2,1)} %param.14), channel_id=1, replica_groups=mesh['row_0'=8,'row_1'=2,'col_0'=2,'col_1'=4,'col_2'=2] {'row_1'}, dimensions={0}, use_global_device_ids=true | all-gather | bytes 1179648 | tf_op jit(solution)/shard_map/all_gather | solution.py:17
  43.2 13.2 %all-reduce = s32[16]{0:T(128)S(1)} all-reduce(s32[16]{0:T(128)S(1)} %bitcast_dynamic-update-slice_fusion.2), channel_id=1, replica_groups=mesh['row_0'=8,'row_1'=2,'col_0'=2,'col_1'=4,'col_2'=2] {'col_0','col_1'..., use_global_device_ids=true, to_apply=%add | all-reduce | flops 16 | bytes 128
  56.4 20.6 %all-gather = s32[16,12,2]{1,2,0:T(2,128)S(1)} all-gather(s32[1,12,2]{1,2,0:T(2,128)} %bitcast.156), channel_id=1, replica_groups=mesh['row_0'=8,'row_1'=2,'col_0'=2,'col_1'=4,'col_2'=2] {'col_0','col_1'..., dimensions={0}, use_global_device_ids=true | all-gather | bytes 1632 | tf_op jit(solution)/shard_map/all_gather | solution.py:75
  77.1 4.5 all-gather.1
  81.7 19.1 %all-gather.2 = s32[8,24,2]{1,2,0:T(2,128)S(1)} all-gather(s32[1,24,2]{1,2,0:T(2,128)S(1)} %reshape.550), channel_id=1, replica_groups=mesh['row_0'=8,'row_1'=2,'col_0'=2,'col_1'=4,'col_2'=2] {'row_0'}, dimensions={0}, use_global_device_ids=true | all-gather | bytes 1728 | tf_op jit(solution)/shard_map/all_gather | solution.py:17
  107.6 10.1 all-reduce.5
  117.7 51.9 %all-gather.10.cloned.1.call-done = bf16[192,128,128]{2,1,0:T(8,128)(2,1)} async-done(((bf16[12,128,128]{2,1,0:T(8,128)(2,1)}), bf16[192,128,128]{2,1,0:T(8,128)(2,1)}) %all-gather.10.cloned.1.call-update) | async-done | bytes 6291472 | tf_op jit(solution)/shard_map/all_gather | solution.py:74
  169.6 422.4 %while.103 = (s32[]{:T(128)}, f32[12,128,128]{2,1,0:T(8,128)S(1)}, s32[192,2]{0,1:T(2,128)S(1)}, s32[12,2]{0,1:T(2,128)}, s32[16,1]{0,1:T(1,128)S(1)}, /*index=5...) while((s32[]{:T(128)}, f32[12,128,128]{2,1,0:T(8,128)S(1)}, ...), condition=%wide.region_7.8_spmd.clone.clone, body=%wide.region_0.7_spmd.clone.sunk.clone | while | flops 34240824 | bytes 5585050 | solution.py:89
  176.6 19.1 %while.102 = (s32[]{:T(128)}, f32[12,128,128]{2,1,0:T(8,128)S(1)}, pred[12,8]{1,0:T(8,128)(4,1)S(1)}, s32[12,8]{1,0:T(8,128)S(1)}, bf16[12,128,128]{2,1,0:T(8,12...) while((s32[]{:T(128)}, f32[12,128,128]{2,1,0:T(8,128)S(1)}, ...), condition=%wide.region_6.6_spmd, body=%wide.region_5.5_spmd.sunk | while | flops 33818672 | bytes 1648009 | solution.py:54
  203.0 19.1 %while.102 = (s32[]{:T(128)}, f32[12,128,128]{2,1,0:T(8,128)S(1)}, pred[12,8]{1,0:T(8,128)(4,1)S(1)}, s32[12,8]{1,0:T(8,128)S(1)}, bf16[12,128,128]{2,1,0:T(8,12...) while((s32[]{:T(128)}, f32[12,128,128]{2,1,0:T(8,128)S(1)}, ...), condition=%wide.region_6.6_spmd, body=%wide.region_5.5_spmd.sunk | while | flops 33818672 | bytes 1648009 | solution.py:54
  229.4 19.1 %while.102 = (s32[]{:T(128)}, f32[12,128,128]{2,1,0:T(8,128)S(1)}, pred[12,8]{1,0:T(8,128)(4,1)S(1)}, s32[12,8]{1,0:T(8,128)S(1)}, bf16[12,128,128]{2,1,0:T(8,12...) while((s32[]{:T(128)}, f32[12,128,128]{2,1,0:T(8,128)S(1)}, ...), condition=%wide.region_6.6_spmd, body=%wide.region_5.5_spmd.sunk | while | flops 33818672 | bytes 1648009 | solution.py:54
  255.8 19.1 %while.102 = (s32[]{:T(128)}, f32[12,128,128]{2,1,0:T(8,128)S(1)}, pred[12,8]{1,0:T(8,128)(4,1)S(1)}, s32[12,8]{1,0:T(8,128)S(1)}, bf16[12,128,128]{2,1,0:T(8,12...) while((s32[]{:T(128)}, f32[12,128,128]{2,1,0:T(8,128)S(1)}, ...), condition=%wide.region_6.6_spmd, body=%wide.region_5.5_spmd.sunk | while | flops 33818672 | bytes 1648009 | solution.py:54
  282.2 19.1 %while.102 = (s32[]{:T(128)}, f32[12,128,128]{2,1,0:T(8,128)S(1)}, pred[12,8]{1,0:T(8,128)(4,1)S(1)}, s32[12,8]{1,0:T(8,128)S(1)}, bf16[12,128,128]{2,1,0:T(8,12...) while((s32[]{:T(128)}, f32[12,128,128]{2,1,0:T(8,128)S(1)}, ...), condition=%wide.region_6.6_spmd, body=%wide.region_5.5_spmd.sunk | while | flops 33818672 | bytes 1648009 | solution.py:54
  308.6 19.1 %while.102 = (s32[]{:T(128)}, f32[12,128,128]{2,1,0:T(8,128)S(1)}, pred[12,8]{1,0:T(8,128)(4,1)S(1)}, s32[12,8]{1,0:T(8,128)S(1)}, bf16[12,128,128]{2,1,0:T(8,12...) while((s32[]{:T(128)}, f32[12,128,128]{2,1,0:T(8,128)S(1)}, ...), condition=%wide.region_6.6_spmd, body=%wide.region_5.5_spmd.sunk | while | flops 33818672 | bytes 1648009 | solution.py:54
  335.0 19.1 %while.102 = (s32[]{:T(128)}, f32[12,128,128]{2,1,0:T(8,128)S(1)}, pred[12,8]{1,0:T(8,128)(4,1)S(1)}, s32[12,8]{1,0:T(8,128)S(1)}, bf16[12,128,128]{2,1,0:T(8,12...) while((s32[]{:T(128)}, f32[12,128,128]{2,1,0:T(8,128)S(1)}, ...), condition=%wide.region_6.6_spmd, body=%wide.region_5.5_spmd.sunk | while | flops 33818672 | bytes 1648009 | solution.py:54
  361.4 19.1 %while.102 = (s32[]{:T(128)}, f32[12,128,128]{2,1,0:T(8,128)S(1)}, pred[12,8]{1,0:T(8,128)(4,1)S(1)}, s32[12,8]{1,0:T(8,128)S(1)}, bf16[12,128,128]{2,1,0:T(8,12...) while((s32[]{:T(128)}, f32[12,128,128]{2,1,0:T(8,128)S(1)}, ...), condition=%wide.region_6.6_spmd, body=%wide.region_5.5_spmd.sunk | while | flops 33818672 | bytes 1648009 | solution.py:54
  387.8 19.1 %while.102 = (s32[]{:T(128)}, f32[12,128,128]{2,1,0:T(8,128)S(1)}, pred[12,8]{1,0:T(8,128)(4,1)S(1)}, s32[12,8]{1,0:T(8,128)S(1)}, bf16[12,128,128]{2,1,0:T(8,12...) while((s32[]{:T(128)}, f32[12,128,128]{2,1,0:T(8,128)S(1)}, ...), condition=%wide.region_6.6_spmd, body=%wide.region_5.5_spmd.sunk | while | flops 33818672 | bytes 1648009 | solution.py:54
  414.2 19.1 %while.102 = (s32[]{:T(128)}, f32[12,128,128]{2,1,0:T(8,128)S(1)}, pred[12,8]{1,0:T(8,128)(4,1)S(1)}, s32[12,8]{1,0:T(8,128)S(1)}, bf16[12,128,128]{2,1,0:T(8,12...) while((s32[]{:T(128)}, f32[12,128,128]{2,1,0:T(8,128)S(1)}, ...), condition=%wide.region_6.6_spmd, body=%wide.region_5.5_spmd.sunk | while | flops 33818672 | bytes 1648009 | solution.py:54
  440.6 19.1 %while.102 = (s32[]{:T(128)}, f32[12,128,128]{2,1,0:T(8,128)S(1)}, pred[12,8]{1,0:T(8,128)(4,1)S(1)}, s32[12,8]{1,0:T(8,128)S(1)}, bf16[12,128,128]{2,1,0:T(8,12...) while((s32[]{:T(128)}, f32[12,128,128]{2,1,0:T(8,128)S(1)}, ...), condition=%wide.region_6.6_spmd, body=%wide.region_5.5_spmd.sunk | while | flops 33818672 | bytes 1648009 | solution.py:54
  467.0 19.1 %while.102 = (s32[]{:T(128)}, f32[12,128,128]{2,1,0:T(8,128)S(1)}, pred[12,8]{1,0:T(8,128)(4,1)S(1)}, s32[12,8]{1,0:T(8,128)S(1)}, bf16[12,128,128]{2,1,0:T(8,12...) while((s32[]{:T(128)}, f32[12,128,128]{2,1,0:T(8,128)S(1)}, ...), condition=%wide.region_6.6_spmd, body=%wide.region_5.5_spmd.sunk | while | flops 33818672 | bytes 1648009 | solution.py:54
  493.4 19.1 %while.102 = (s32[]{:T(128)}, f32[12,128,128]{2,1,0:T(8,128)S(1)}, pred[12,8]{1,0:T(8,128)(4,1)S(1)}, s32[12,8]{1,0:T(8,128)S(1)}, bf16[12,128,128]{2,1,0:T(8,12...) while((s32[]{:T(128)}, f32[12,128,128]{2,1,0:T(8,128)S(1)}, ...), condition=%wide.region_6.6_spmd, body=%wide.region_5.5_spmd.sunk | while | flops 33818672 | bytes 1648009 | solution.py:54
  519.8 19.1 %while.102 = (s32[]{:T(128)}, f32[12,128,128]{2,1,0:T(8,128)S(1)}, pred[12,8]{1,0:T(8,128)(4,1)S(1)}, s32[12,8]{1,0:T(8,128)S(1)}, bf16[12,128,128]{2,1,0:T(8,12...) while((s32[]{:T(128)}, f32[12,128,128]{2,1,0:T(8,128)S(1)}, ...), condition=%wide.region_6.6_spmd, body=%wide.region_5.5_spmd.sunk | while | flops 33818672 | bytes 1648009 | solution.py:54
  546.2 19.1 %while.102 = (s32[]{:T(128)}, f32[12,128,128]{2,1,0:T(8,128)S(1)}, pred[12,8]{1,0:T(8,128)(4,1)S(1)}, s32[12,8]{1,0:T(8,128)S(1)}, bf16[12,128,128]{2,1,0:T(8,12...) while((s32[]{:T(128)}, f32[12,128,128]{2,1,0:T(8,128)S(1)}, ...), condition=%wide.region_6.6_spmd, body=%wide.region_5.5_spmd.sunk | while | flops 33818672 | bytes 1648009 | solution.py:54
  572.6 19.1 %while.102 = (s32[]{:T(128)}, f32[12,128,128]{2,1,0:T(8,128)S(1)}, pred[12,8]{1,0:T(8,128)(4,1)S(1)}, s32[12,8]{1,0:T(8,128)S(1)}, bf16[12,128,128]{2,1,0:T(8,12...) while((s32[]{:T(128)}, f32[12,128,128]{2,1,0:T(8,128)S(1)}, ...), condition=%wide.region_6.6_spmd, body=%wide.region_5.5_spmd.sunk | while | flops 33818672 | bytes 1648009 | solution.py:54
  592.9 4.5 all-gather.3
  597.5 16.6 %all-gather.4 = s32[8,24,2]{1,2,0:T(2,128)S(1)} all-gather(s32[1,24,2]{1,2,0:T(2,128)S(1)} %reshape.554), channel_id=1, replica_groups=mesh['row_0'=8,'row_1'=2,'col_0'=2,'col_1'=4,'col_2'=2] {'row_0'}, dimensions={0}, use_global_device_ids=true | all-gather | bytes 1728 | tf_op jit(solution)/shard_map/all_gather | solution.py:17
  615.7 15.6 %psum.35 = f32[]{:T(128)} all-reduce(f32[]{:T(128)} %fusion.27), channel_id=1, replica_groups=mesh['row_0'=8,'row_1'=2,'col_0'=2,'col_1'=4,'col_2'=2] {'row_0'}, use_global_device_ids=true, to_apply=%region_18.19 | all-reduce | flops 1 | bytes 8 | tf_op jit(solution)/shard_map/psum | solution.py:22
  631.3 5.6 psum.36
  637.0 7.1 psum.37
  644.1 9.2 psum.38
  660.2 423.9 %while.105 = (s32[]{:T(128)}, f32[12,128,128]{2,1,0:T(8,128)S(1)}, s32[192,2]{0,1:T(2,128)S(1)}, s32[12,2]{0,1:T(2,128)}, s32[16,1]{0,1:T(1,128)S(1)}, /*index=5...) while((s32[]{:T(128)}, f32[12,128,128]{2,1,0:T(8,128)S(1)}, ...), condition=%wide.region_15.16_spmd.clone.clone, body=%wide.region_8.15_spmd.clone.sunk.clone | while | flops 34240824 | bytes 5585050 | solution.py:89
  667.2 19.1 %while.104 = (s32[]{:T(128)}, f32[12,128,128]{2,1,0:T(8,128)S(1)}, pred[12,8]{1,0:T(8,128)(4,1)S(1)}, s32[12,8]{1,0:T(8,128)S(1)}, bf16[12,128,128]{2,1,0:T(8,12...) while((s32[]{:T(128)}, f32[12,128,128]{2,1,0:T(8,128)S(1)}, ...), condition=%wide.region_14.14_spmd, body=%wide.region_13.13_spmd.sunk | while | flops 33818672 | bytes 1648009 | solution.py:54
  693.7 19.1 %while.104 = (s32[]{:T(128)}, f32[12,128,128]{2,1,0:T(8,128)S(1)}, pred[12,8]{1,0:T(8,128)(4,1)S(1)}, s32[12,8]{1,0:T(8,128)S(1)}, bf16[12,128,128]{2,1,0:T(8,12...) while((s32[]{:T(128)}, f32[12,128,128]{2,1,0:T(8,128)S(1)}, ...), condition=%wide.region_14.14_spmd, body=%wide.region_13.13_spmd.sunk | while | flops 33818672 | bytes 1648009 | solution.py:54
  720.2 19.1 %while.104 = (s32[]{:T(128)}, f32[12,128,128]{2,1,0:T(8,128)S(1)}, pred[12,8]{1,0:T(8,128)(4,1)S(1)}, s32[12,8]{1,0:T(8,128)S(1)}, bf16[12,128,128]{2,1,0:T(8,12...) while((s32[]{:T(128)}, f32[12,128,128]{2,1,0:T(8,128)S(1)}, ...), condition=%wide.region_14.14_spmd, body=%wide.region_13.13_spmd.sunk | while | flops 33818672 | bytes 1648009 | solution.py:54
  746.7 19.1 %while.104 = (s32[]{:T(128)}, f32[12,128,128]{2,1,0:T(8,128)S(1)}, pred[12,8]{1,0:T(8,128)(4,1)S(1)}, s32[12,8]{1,0:T(8,128)S(1)}, bf16[12,128,128]{2,1,0:T(8,12...) while((s32[]{:T(128)}, f32[12,128,128]{2,1,0:T(8,128)S(1)}, ...), condition=%wide.region_14.14_spmd, body=%wide.region_13.13_spmd.sunk | while | flops 33818672 | bytes 1648009 | solution.py:54
  773.2 19.1 %while.104 = (s32[]{:T(128)}, f32[12,128,128]{2,1,0:T(8,128)S(1)}, pred[12,8]{1,0:T(8,128)(4,1)S(1)}, s32[12,8]{1,0:T(8,128)S(1)}, bf16[12,128,128]{2,1,0:T(8,12...) while((s32[]{:T(128)}, f32[12,128,128]{2,1,0:T(8,128)S(1)}, ...), condition=%wide.region_14.14_spmd, body=%wide.region_13.13_spmd.sunk | while | flops 33818672 | bytes 1648009 | solution.py:54
  799.7 19.1 %while.104 = (s32[]{:T(128)}, f32[12,128,128]{2,1,0:T(8,128)S(1)}, pred[12,8]{1,0:T(8,128)(4,1)S(1)}, s32[12,8]{1,0:T(8,128)S(1)}, bf16[12,128,128]{2,1,0:T(8,12...) while((s32[]{:T(128)}, f32[12,128,128]{2,1,0:T(8,128)S(1)}, ...), condition=%wide.region_14.14_spmd, body=%wide.region_13.13_spmd.sunk | while | flops 33818672 | bytes 1648009 | solution.py:54
  826.2 19.1 %while.104 = (s32[]{:T(128)}, f32[12,128,128]{2,1,0:T(8,128)S(1)}, pred[12,8]{1,0:T(8,128)(4,1)S(1)}, s32[12,8]{1,0:T(8,128)S(1)}, bf16[12,128,128]{2,1,0:T(8,12...) while((s32[]{:T(128)}, f32[12,128,128]{2,1,0:T(8,128)S(1)}, ...), condition=%wide.region_14.14_spmd, body=%wide.region_13.13_spmd.sunk | while | flops 33818672 | bytes 1648009 | solution.py:54
  852.7 19.1 %while.104 = (s32[]{:T(128)}, f32[12,128,128]{2,1,0:T(8,128)S(1)}, pred[12,8]{1,0:T(8,128)(4,1)S(1)}, s32[12,8]{1,0:T(8,128)S(1)}, bf16[12,128,128]{2,1,0:T(8,12...) while((s32[]{:T(128)}, f32[12,128,128]{2,1,0:T(8,128)S(1)}, ...), condition=%wide.region_14.14_spmd, body=%wide.region_13.13_spmd.sunk | while | flops 33818672 | bytes 1648009 | solution.py:54
  879.2 19.1 %while.104 = (s32[]{:T(128)}, f32[12,128,128]{2,1,0:T(8,128)S(1)}, pred[12,8]{1,0:T(8,128)(4,1)S(1)}, s32[12,8]{1,0:T(8,128)S(1)}, bf16[12,128,128]{2,1,0:T(8,12...) while((s32[]{:T(128)}, f32[12,128,128]{2,1,0:T(8,128)S(1)}, ...), condition=%wide.region_14.14_spmd, body=%wide.region_13.13_spmd.sunk | while | flops 33818672 | bytes 1648009 | solution.py:54
  905.7 19.1 %while.104 = (s32[]{:T(128)}, f32[12,128,128]{2,1,0:T(8,128)S(1)}, pred[12,8]{1,0:T(8,128)(4,1)S(1)}, s32[12,8]{1,0:T(8,128)S(1)}, bf16[12,128,128]{2,1,0:T(8,12...) while((s32[]{:T(128)}, f32[12,128,128]{2,1,0:T(8,128)S(1)}, ...), condition=%wide.region_14.14_spmd, body=%wide.region_13.13_spmd.sunk | while | flops 33818672 | bytes 1648009 | solution.py:54
  932.2 19.1 %while.104 = (s32[]{:T(128)}, f32[12,128,128]{2,1,0:T(8,128)S(1)}, pred[12,8]{1,0:T(8,128)(4,1)S(1)}, s32[12,8]{1,0:T(8,128)S(1)}, bf16[12,128,128]{2,1,0:T(8,12...) while((s32[]{:T(128)}, f32[12,128,128]{2,1,0:T(8,128)S(1)}, ...), condition=%wide.region_14.14_spmd, body=%wide.region_13.13_spmd.sunk | while | flops 33818672 | bytes 1648009 | solution.py:54
  958.7 19.1 %while.104 = (s32[]{:T(128)}, f32[12,128,128]{2,1,0:T(8,128)S(1)}, pred[12,8]{1,0:T(8,128)(4,1)S(1)}, s32[12,8]{1,0:T(8,128)S(1)}, bf16[12,128,128]{2,1,0:T(8,12...) while((s32[]{:T(128)}, f32[12,128,128]{2,1,0:T(8,128)S(1)}, ...), condition=%wide.region_14.14_spmd, body=%wide.region_13.13_spmd.sunk | while | flops 33818672 | bytes 1648009 | solution.py:54
  985.2 19.1 %while.104 = (s32[]{:T(128)}, f32[12,128,128]{2,1,0:T(8,128)S(1)}, pred[12,8]{1,0:T(8,128)(4,1)S(1)}, s32[12,8]{1,0:T(8,128)S(1)}, bf16[12,128,128]{2,1,0:T(8,12...) while((s32[]{:T(128)}, f32[12,128,128]{2,1,0:T(8,128)S(1)}, ...), condition=%wide.region_14.14_spmd, body=%wide.region_13.13_spmd.sunk | while | flops 33818672 | bytes 1648009 | solution.py:54
  1011.6 19.1 %while.104 = (s32[]{:T(128)}, f32[12,128,128]{2,1,0:T(8,128)S(1)}, pred[12,8]{1,0:T(8,128)(4,1)S(1)}, s32[12,8]{1,0:T(8,128)S(1)}, bf16[12,128,128]{2,1,0:T(8,12...) while((s32[]{:T(128)}, f32[12,128,128]{2,1,0:T(8,128)S(1)}, ...), condition=%wide.region_14.14_spmd, body=%wide.region_13.13_spmd.sunk | while | flops 33818672 | bytes 1648009 | solution.py:54
  1038.1 19.1 %while.104 = (s32[]{:T(128)}, f32[12,128,128]{2,1,0:T(8,128)S(1)}, pred[12,8]{1,0:T(8,128)(4,1)S(1)}, s32[12,8]{1,0:T(8,128)S(1)}, bf16[12,128,128]{2,1,0:T(8,12...) while((s32[]{:T(128)}, f32[12,128,128]{2,1,0:T(8,128)S(1)}, ...), condition=%wide.region_14.14_spmd, body=%wide.region_13.13_spmd.sunk | while | flops 33818672 | bytes 1648009 | solution.py:54
  1064.6 19.1 %while.104 = (s32[]{:T(128)}, f32[12,128,128]{2,1,0:T(8,128)S(1)}, pred[12,8]{1,0:T(8,128)(4,1)S(1)}, s32[12,8]{1,0:T(8,128)S(1)}, bf16[12,128,128]{2,1,0:T(8,12...) while((s32[]{:T(128)}, f32[12,128,128]{2,1,0:T(8,128)S(1)}, ...), condition=%wide.region_14.14_spmd, body=%wide.region_13.13_spmd.sunk | while | flops 33818672 | bytes 1648009 | solution.py:54
  (3308 shorter events, 839.3 us)
Async XLA Ops:
  7.2 110.5 %all-gather.12.cloned.1.call-start = ((), (), s32[]{:S(2)}) async-start(), calls=%async_computation.1 | async-start | bytes 7077888 | tf_op jit(solution)/shard_map/all_gather | solution.py:17
  20.8 148.8 %all-gather.10.cloned.1.call-start = ((), (), s32[]{:S(2)}) async-start(), calls=%async_computation | async-start | bytes 6684672 | tf_op jit(solution)/shard_map/all_gather | solution.py:74
  21.6 634.8 %all-gather.16.cloned.1.call-start = ((), (), s32[]{:S(2)}) async-start(), calls=%async_computation.3 | async-start | bytes 7077888 | tf_op jit(solution)/shard_map/all_gather | solution.py:17
  37.3 622.8 %all-gather.14.cloned.1.call-start = ((), (), s32[]{:S(2)}) async-start(), calls=%async_computation.2 | async-start | bytes 6684672 | tf_op jit(solution)/shard_map/all_gather | solution.py:74
Sparse Core Ops, SparseCore 0:
  21.0 78.9 all-gather.11
  102.8 66.8 all-gather.9
  171.4 73.2 all-gather.15
  593.0 67.0 all-gather.13
where the time goes:
time: 1100 us; the launch traced here: 1090 us
  local copies, waits for them, and re-layouts  556 us (51%)
  blocking collectives  163 us (15%)
  other arithmetic  161 us (15%)
  matrix products  110 us (10%)
  waiting for transfers between devices  56.4 us (5%)
  loops' own time  29.1 us (3%)
  between operations  15.8 us (1%)
    gather x384, local copies, waits for them, and re-layouts, slot_product(): right_vals[right_pick]  229 us
    gather x384, local copies, waits for them, and re-layouts, slot_product(): left_vals[left_pick]  229 us
    dot_general x384, matrix products, slot_product(): jnp.einsum('kxy,kyz->xz', row_blocks, col_blocks, preferred_element_type=...  110 us
    all_gather x6, blocking collectives, whole_of(): shard = lax.all_gather(shard, axis, axis=dim, tiled=True)  73.9 us
    another operation x64, other arithmetic, contribute(): pick_left = jnp.argmax(match_left.astype(jnp.int32), axis=2)  71.8 us
    all_gather x2, waiting for transfers between devices, multiply(): lax.all_gather(left_tile[0], COL, axis=0, tiled=True)  55.7 us
    psum x5, blocking collectives, by_axis(): return functools.reduce(lax.psum, axes, shard)  40.6 us
    dynamic_slice x32, local copies, waits for them, and re-layouts, pick_tile(): vals = lax.dynamic_slice_in_dim(all_vals, start, slot_count, 0)  37.6 us
  transfers between devices with their start and end apart: 4, of which 2 were waited for; matrix products, arithmetic and copies ran while one was open for 38% of the time, Pallas kernels for 0%

commit v1 on v0

v1 whole, which is shorter than its diff:
```python
import functools

import jax
import jax.numpy as jnp
from jax import lax
from jax.experimental import pallas as pl
from jax.experimental.pallas import tpu as pltpu
from jax.sharding import Mesh
from jax.sharding import PartitionSpec as P

TILE = 8
BLK = 128
CAP = 12
BODY = CAP * BLK
META = 16
PAY = BODY + META
LEFTS = 16
RIGHTS = 8
OUTS = 2
CODE_AT = 64
MASK_AT = 80
NO_SLOT = 255
UNROLL = 4
LIST = LEFTS * CAP * TILE + UNROLL
RING_Y = 4
RING_Z = 8
AXES = ("z", "x_lo", "x_hi", "y", "core")
ROW = ("z", "x_lo")
COL = ("x_hi", "y", "core")
IN_CHIP_X = ("x_lo", "x_hi", "core")


def describe(where, count, row, col):
    slot = lax.broadcasted_iota(jnp.int32, (CAP, BLK), 0)
    lane = lax.broadcasted_iota(jnp.int32, (CAP, BLK), 1)
    live = slot < count[0, 0]
    r = (where[:, 0] - row * TILE)[:, None]
    c = (where[:, 1] - col * TILE)[:, None]
    code = jnp.where(live, r * TILE + c, NO_SLOT)
    here = jnp.where(code == lane, slot + 1, 0)
    names = jnp.where(slot == lane - CODE_AT, code, 0)
    bits = jnp.where(live & (r == lane - MASK_AT), jnp.left_shift(1, c), 0)
    values = jnp.where(lane < CODE_AT, here, jnp.where(lane < MASK_AT, names, bits))
    line = jnp.sum(values, axis=0, keepdims=True).astype(jnp.bfloat16)
    return jnp.broadcast_to(line, (META, BLK))


def x_index(x_lo, x_hi, core):
    return (x_lo * 2 + x_hi) * 2 + core


def x_perms():
    first, second = [], []
    for x in range(4):
        a, b = x % 2, 1 - x % 2
        right, far, left = (x + 1) % 4, (x + 2) % 4, (x + 3) % 4
        at = lambda chip, core: x_index(chip % 2, chip // 2, core)
        first.append((at(x, b), at(right, right % 2)))
        first.append((at(x, a), at(far, 1 - far % 2)))
        second.append((at(x, b), at(left, 1 - left % 2)))
        second.append((at(x, a), at(x, a)))
    return first, second


def ring(n, step):
    return [(i, (i + step) % n) for i in range(n)]


def spread(tile):
    first, second = x_perms()
    far = lax.ppermute(tile, IN_CHIP_X, first)
    near = lax.ppermute(tile, IN_CHIP_X, second)
    near_up = lax.ppermute(near, "y", ring(RING_Y, 1))
    far_down = lax.ppermute(far, "y", ring(RING_Y, -1))
    near_down = lax.ppermute(near, "y", ring(RING_Y, -1))
    far_up = lax.ppermute(far, "y", ring(RING_Y, 1))
    near_two = lax.ppermute(near_up, "y", ring(RING_Y, 1))
    far_two = lax.ppermute(far_down, "y", ring(RING_Y, -1))
    mine = [near, near_up, near_down, near_two, far, far_up, far_down, far_two]
    theirs = [lax.ppermute(t, "core", ring(2, 1)) for t in mine]
    return mine + theirs


def tile_table(x, y, core):
    same = core == x % 2
    dy = jnp.array([0, -1, 1, 2] * 4, jnp.int32)
    if_same = jnp.array([0] * 4 + [-1] * 4 + [1] * 4 + [2] * 4, jnp.int32)
    if_other = jnp.array([1] * 4 + [2] * 4 + [0] * 4 + [-1] * 4, jnp.int32)
    dx = jnp.where(same, if_same, if_other)
    from_x = (x + dx + 4) % 4
    from_y = (y + dy + RING_Y) % RING_Y
    return (from_x // 2) * RING_Y + from_y, (dx + 4) % 2


def product_kernel(trace, info, *refs):
    lefts, metas = refs[:LEFTS], refs[LEFTS : 2 * LEFTS]
    right, outs = refs[2 * LEFTS], refs[2 * LEFTS + 1]
    refs = refs[2 * LEFTS + 2 :]
    own, other = refs[0], refs[1]
    refs = refs[2:]
    energy = None
    if trace:
        energy, refs = refs[0], refs[1:]
    lv, rv, mv, mi, sm, todo, acc, sems, meta_sem = refs

    small, large = [], []
    for t in range(LEFTS):
        small.append((metas[t].at[pl.ds(BODY, META)], mv.at[pl.ds(t * META, META)]))
    for t in range(RIGHTS):
        small.append((right.at[pl.ds(t * PAY + BODY, META)], mv.at[pl.ds((LEFTS + t) * META, META)]))
    for t in range(RIGHTS):
        large.append((right.at[pl.ds(t * PAY, BODY)], rv.at[pl.ds(t * BODY, BODY)]))
    for t in range(LEFTS):
        large.append((lefts[t].at[pl.ds(0, BODY)], lv.at[pl.ds(t * BODY, BODY)]))
    copies = [pltpu.make_async_copy(a, b, sems.at[n]) for n, (a, b) in enumerate(small + large)]
    for copy in copies:
        copy.start()
    acc[...] = jnp.zeros_like(acc)
    for copy in copies[: len(small)]:
        copy.wait()
    for t in range(LEFTS + RIGHTS):
        mi[t : t + 1, :] = mv[t * META : (t + 1) * META, :].astype(jnp.float32)[0:1].astype(jnp.int32)
    for t in range(OUTS):
        mi[LEFTS + RIGHTS + t : LEFTS + RIGHTS + t + 1, :] = (
            outs[t * META : (t + 1) * META, :].astype(jnp.float32)[0:1].astype(jnp.int32)
        )
    to_scalar = pltpu.make_async_copy(mi, sm, meta_sem)
    to_scalar.start()
    to_scalar.wait()

    def each_left(n_tile, count):
        k_tile = info[0, n_tile]
        out_tile = info[1, n_tile]
        r_row = LEFTS + k_tile
        o_row = LEFTS + RIGHTS + out_tile

        def each_slot(slot, count):
            code = sm[n_tile, CODE_AT + slot]
            i, k = code // TILE, code % TILE
            both = sm[r_row, MASK_AT + k] & sm[o_row, MASK_AT + i]

            def hits(count):
                for j in range(TILE):
                    bit = (both // (1 << j)) % 2
                    r = sm[r_row, k * TILE + j] - 1
                    o = sm[o_row, lax.rem(i * TILE + j, BLK)] - 1

                    @pl.when(bit == 1)
                    def _():
                        todo[0, count] = n_tile * CAP + slot
                        todo[1, count] = k_tile * CAP + r
                        todo[2, count] = out_tile * CAP + o

                    count = count + bit
                return count

            return lax.cond(both != 0, hits, lambda count: count, count)

        return lax.fori_loop(0, CAP, each_slot, count)

    count = lax.fori_loop(0, LEFTS, each_left, jnp.int32(0))
    for u in range(UNROLL):
        todo[0, count + u] = 0
        todo[1, count + u] = 0
        todo[2, count + u] = OUTS * CAP
    for copy in copies[len(small) :]:
        copy.wait()

    def block(n):
        return pl.ds(pl.multiple_of(n * BLK, BLK), BLK)

    def step(g, carry):
        parts = []
        for u in range(UNROLL):
            n = g * UNROLL + u
            a, b = lv[block(todo[0, n]), :], rv[block(todo[1, n]), :]
            parts.append(jnp.dot(a, b, preferred_element_type=jnp.float32))
        for u in range(UNROLL):
            o = block(todo[2, g * UNROLL + u])
            acc[o, :] += parts[u]
        return carry

    lax.fori_loop(0, (count + UNROLL - 1) // UNROLL, step, 0)
    own[...] = acc[0:BODY, :]
    other[...] = acc[BODY : 2 * BODY, :].astype(other.dtype)
    if trace:
        energy[...] = jnp.zeros_like(energy)
        for t in range(OUTS):

            @pl.when(info[2, t] == 1)
            def _():
                r = lax.broadcasted_iota(jnp.int32, (BLK, BLK), 0)
                c = lax.broadcasted_iota(jnp.int32, (BLK, BLK), 1)
                for i in range(TILE):
                    slot = sm[LEFTS + RIGHTS + t, i * TILE + i] - 1

                    @pl.when(slot >= 0)
                    def _():
                        held = acc[block(t * CAP + slot), :]
                        diagonal = jnp.where(r == c, held, 0.0)
                        energy[...] += jnp.sum(diagonal.reshape(BLK // 8, 8, BLK), axis=0)


def product(info, lefts, metas, right, outs, send_type, trace):
    shapes = [
        jax.ShapeDtypeStruct((BODY, BLK), jnp.float32),
        jax.ShapeDtypeStruct((BODY, BLK), send_type),
    ]
    if trace:
        shapes.append(jax.ShapeDtypeStruct((8, BLK), jnp.float32))
    vmem = pl.BlockSpec(memory_space=pltpu.VMEM)
    anywhere = pl.BlockSpec(memory_space=pl.ANY)
    n_copies = 2 * (LEFTS + RIGHTS)
    return pl.pallas_call(
        functools.partial(product_kernel, trace),
        out_shape=shapes,
        in_specs=[pl.BlockSpec(memory_space=pltpu.SMEM)] + [anywhere] * (2 * LEFTS + 1) + [vmem],
        out_specs=[vmem] * len(shapes),
        scratch_shapes=[
            pltpu.VMEM((LEFTS * BODY, BLK), jnp.bfloat16),
            pltpu.VMEM((RIGHTS * BODY, BLK), jnp.bfloat16),
            pltpu.VMEM(((LEFTS + RIGHTS) * META, BLK), jnp.bfloat16),
            pltpu.VMEM((32, BLK), jnp.int32),
            pltpu.SMEM((32, BLK), jnp.int32),
            pltpu.SMEM((3, LIST), jnp.int32),
            pltpu.VMEM(((OUTS * CAP + 1) * BLK, BLK), jnp.float32),
            pltpu.SemaphoreType.DMA((n_copies,)),
            pltpu.SemaphoreType.DMA,
        ],
        compiler_params=pltpu.CompilerParams(vmem_limit_bytes=32 * 1024 * 1024),
        cost_estimate=pl.CostEstimate(flops=200_000_000, bytes_accessed=12_000_000, transcendentals=0),
    )(info, *lefts, *metas, right, outs)


def total(part):
    for axis, size, hop in (
        ("core", 2, 1),
        ("x_lo", 2, 1),
        ("x_hi", 2, 1),
        ("y", RING_Y, 1),
        ("y", RING_Y, 2),
        ("z", RING_Z, 1),
        ("z", RING_Z, 2),
        ("z", RING_Z, 4),
    ):
        part = part + lax.ppermute(part, axis, [(i, i ^ hop) for i in range(size)])
    return jnp.sum(part)


def per_device(p_values, p_where, p_count, h_values, h_where, h_count):
    z, x_lo, x_hi, y, core = (lax.axis_index(a) for a in AXES)
    row, col = z * 2 + x_lo, (x_hi * RING_Y + y) * 2 + core
    places, out_tiles = tile_table(x_hi * 2 + x_lo, y, core)
    on_diagonal = jnp.stack([row == col, z * 2 + 1 - x_lo == col]).astype(jnp.int32)
    info = jnp.stack([places, out_tiles, jnp.pad(on_diagonal, (0, LEFTS - 2))]).astype(jnp.int32)

    p_meta = describe(p_where, p_count, row, col)
    h_meta = describe(h_where, h_count, row, col)
    h_pay = jnp.concatenate([h_values.reshape(BODY, BLK), h_meta])
    p_pay = jnp.concatenate([p_values.reshape(BODY, BLK), p_meta])
    h_line = lax.all_gather(h_pay, "z", axis=0, tiled=True)
    p_line = lax.all_gather(p_pay, "z", axis=0, tiled=True)
    partner_meta = lax.ppermute(p_meta, "x_lo", ring(2, 1))
    outs = jnp.concatenate([p_meta, partner_meta])
    p_tiles = spread(p_pay)

    own, other, energy = product(info, p_tiles, p_tiles, h_line, outs, jnp.bfloat16, True)
    came = lax.ppermute(other, "x_lo", ring(2, 1))
    ph = (own + came.astype(jnp.float32)).astype(jnp.bfloat16)

    f_tiles = spread(ph)
    own, other = product(info, f_tiles, p_tiles, p_line, outs, jnp.bfloat16, False)
    came = lax.ppermute(other, "x_lo", ring(2, 1))
    php = (own + came.astype(jnp.float32)).astype(jnp.bfloat16)
    return ph.reshape(CAP, BLK, BLK), php.reshape(CAP, BLK, BLK), total(energy)


def solution(mesh):
    torus = Mesh(mesh.devices.reshape(8, 2, 2, 4, 2), AXES)
    in_specs = (
        P(ROW, COL, None),
        P(ROW, COL),
        P(ROW, COL),
        P(ROW, COL, None),
        P(ROW, COL),
        P(ROW, COL),
    )
    out_specs = (P(ROW, COL, None), P(ROW, COL, None), P())
    return jax.shard_map(
        per_device, mesh=torus, in_specs=in_specs, out_specs=out_specs, check_vma=False
    )
```

time: 1100 us -> 230 us (0.21)
  local copies, waits for them, and re-layouts: 556 us -> 28.2 us
  blocking collectives: 163 us -> 0 us
  other arithmetic: 161 us -> 6.81 us
  matrix products: 110 us -> 0 us
  starting transfers between devices: 0.16 us -> 45.2 us
  waiting for transfers between devices: 56.4 us -> 100 us
  Pallas kernels: 0 us -> 32.4 us
  loops' own time: 29.1 us -> 0 us
    gather x768 -> x0, local copies, waits for them, and re-layouts: 459 us -> none  [the longest x384 229 us: slot_product(): right_vals[right_pick]]
    dot_general x384 -> x0, matrix products: 110 us -> none  [slot_product(): jnp.einsum('kxy,kyz->xz', row_blocks, col_blocks, preferred_element_type=...]
    ppermute x0 -> x43, waiting for transfers between devices: none -> 100 us  [the longest x8 25.2 us: total(): part = part + lax.ppermute(part, axis, [(i, i ^ hop) for i in range(size)])]
    all_gather x7 -> x0, blocking collectives: 94.5 us -> none  [the longest x6 73.9 us: whole_of(): shard = lax.all_gather(shard, axis, axis=dim, tiled=True)]
    another operation x64 -> x4, other arithmetic: 71.8 us -> 0.79 us  [the longest x3 0.71 us: per_device(): jnp.stack([places, out_tiles, jnp.pad(on_diagonal, (0, LEFTS - 2))])]
    dynamic_slice x96 -> x0, local copies, waits for them, and re-layouts: 59.9 us -> none  [the longest x32 37.6 us: pick_tile(): vals = lax.dynamic_slice_in_dim(all_vals, start, slot_count, 0)]
    all_gather x4 -> x2, waiting for transfers between devices: 55.7 us -> 0.01 us  [the longest x1 0.01 us: per_device(): h_line = lax.all_gather(h_pay, 'z', axis=0, tiled=True)]
    ppermute x0 -> x43, starting transfers between devices: none -> 45.1 us  [the longest x8 16.3 us: total(): part = part + lax.ppermute(part, axis, [(i, i ^ hop) for i in range(size)])]
  transfers between devices with their start and end apart: 4 -> 45, of which waited for: 2 -> 23; matrix products, arithmetic and copies ran while one was open for 38% -> 1% of each run, Pallas kernels for 0% -> 7%
where the time goes in v1:
time: 230 us; the launch traced here: 228 us
  waiting for transfers between devices  100 us (43%)
  starting transfers between devices  45.2 us (20%)
  Pallas kernels  32.4 us (14%)
  local copies, waits for them, and re-layouts  28.2 us (12%)
  between operations  15.6 us (7%)
  other arithmetic  6.81 us (3%)
    pallas_call x2, Pallas kernels, product(): pl.pallas_call(functools.partial(product_kernel, trace), out_shape=shapes...  32.4 us
    unnamed x60, local copies, waits for them, and re-layouts  28.2 us
    ppermute x8, waiting for transfers between devices, total(): part = part + lax.ppermute(part, axis, [(i, i ^ hop) for i in range(size)])  25.2 us
    ppermute x8, starting transfers between devices, total(): part = part + lax.ppermute(part, axis, [(i, i ^ hop) for i in range(size)])  16.3 us
    ppermute x2, waiting for transfers between devices, spread(): far = lax.ppermute(tile, IN_CHIP_X, first)  15.6 us
    ppermute x2, waiting for transfers between devices, spread(): near_up = lax.ppermute(near, 'y', ring(RING_Y, 1))  15.1 us
    ppermute x2, waiting for transfers between devices, spread(): near_two = lax.ppermute(near_up, 'y', ring(RING_Y, 1))  11.9 us
    ppermute x2, waiting for transfers between devices, spread(): far_two = lax.ppermute(far_down, 'y', ring(RING_Y, -1))  8.95 us
  transfers between devices with their start and end apart: 45, of which 23 were waited for; matrix products, arithmetic and copies ran while one was open for 1% of the time, Pallas kernels for 7%

profile of v1, /device:TPU:2, one launch (start us, length us, event | category | flops | bytes accessed | tf_op | source)
XLA Modules:
  0.0 228.3 jit_solution(14712319358057911371)
XLA Ops:
  9.5 1.8 pad_maximum_fusion.1
  11.3 1.8 pad_maximum_fusion
  13.2 1.6 collective-permute-start.4
  14.8 1.9 collective-permute-start
  16.7 8.0 %collective-permute-done.4.refs_4_.refs_20_ = bf16[1552,128]{1,0:T(8,128)(2,1)S(1)} collective-permute-done((bf16[1552,128]{1,0:T(8,128)(2,1)}, bf16[1552,128]{1,0:T(8,128)(2,1)S(1)}, u32[]{:S(2)}, u32[]{:S(2)}) %collective-permute-start.4) | collective-permute-done | bytes 397344 | tf_op jit(solution)/shard_map/ppermute | solution.py:71
  24.7 3.0 %collective-permute-start.6 = (bf16[1552,128]{1,0:T(8,128)(2,1)S(1)}, bf16[1552,128]{1,0:T(8,128)(2,1)S(1)}, u32[]{:S(2)}, u32[]{:S(2)}) collective-permute-start(bf16[1552,128]{1,0:T(8,128)(2,1)S(1)} %collective-permute-done.4.refs_4_.refs_20_), channel_id=1, source_target_pairs={{0,6},{2,0},{4,2},{6,4},{1,7},{3,1},{5,3},{7,5},{8,14},{10,8},{12,... | collective-permute-start | bytes 1191944 | tf_op jit(solution)/shard_map/ppermute | solution.py:74
  28.3 2.5 %collective-permute-start.16 = (bf16[16,128]{1,0:T(8,128)(2,1)S(1)}, bf16[16,128]{1,0:T(8,128)(2,1)S(1)}, u32[]{:S(2)}, u32[]{:S(2)}) collective-permute-start(bf16[16,128]{1,0:T(8,128)(2,1)S(1)} %broadcast_in_dim.67), channel_id=1, source_target_pairs={{0,16},{16,0},{1,17},{17,1},{2,18},{18,2},{3,19},{19,3},{4,20},{20... | collective-permute-start | bytes 12296 | tf_op jit(solution)/shard_map/ppermute | solution.py:263
  30.8 1.6 collective-permute-done.16
  32.4 2.7 %collective-permute-start.2 = (bf16[1552,128]{1,0:T(8,128)(2,1)S(1)}, bf16[1552,128]{1,0:T(8,128)(2,1)S(1)}, u32[]{:S(2)}, u32[]{:S(2)}) collective-permute-start(bf16[1552,128]{1,0:T(8,128)(2,1)S(1)} %collective-permute-done.refs_0_.refs_16_), channel_id=1, source_target_pairs={{0,6},{2,0},{4,2},{6,4},{1,7},{3,1},{5,3},{7,5},{8,14},{10,8},{12,... | collective-permute-start | bytes 1191944 | tf_op jit(solution)/shard_map/ppermute | solution.py:75
  35.0 2.2 collective-permute-done.6.refs_6_.refs_22_
  37.2 3.7 %collective-permute-done.5.refs_5_.refs_21_ = bf16[1552,128]{1,0:T(8,128)(2,1)S(1)} collective-permute-done((bf16[1552,128]{1,0:T(8,128)(2,1)S(1)}, bf16[1552,128]{1,0:T(8,128)(2,1)S(1)}, u32[]{:S(2)}, u32[]{:S(2)}) %collective-permute-start.5) | collective-permute-done | bytes 397344 | tf_op jit(solution)/shard_map/ppermute | solution.py:76
  40.9 7.8 %collective-permute-done.1.refs_1_.refs_17_ = bf16[1552,128]{1,0:T(8,128)(2,1)S(1)} collective-permute-done((bf16[1552,128]{1,0:T(8,128)(2,1)S(1)}, bf16[1552,128]{1,0:T(8,128)(2,1)S(1)}, u32[]{:S(2)}, u32[]{:S(2)}) %collective-permute-start.1) | collective-permute-done | bytes 397344 | tf_op jit(solution)/shard_map/ppermute | solution.py:73
  49.5 4.3 %collective-permute-done.7.refs_7_.refs_23_ = bf16[1552,128]{1,0:T(8,128)(2,1)} collective-permute-done((bf16[1552,128]{1,0:T(8,128)(2,1)S(1)}, bf16[1552,128]{1,0:T(8,128)(2,1)}, u32[]{:S(2)}, u32[]{:S(2)}) %collective-permute-start.7) | collective-permute-done | bytes 397344 | tf_op jit(solution)/shard_map/ppermute | solution.py:78
  53.9 6.8 %collective-permute-done.3.refs_3_.refs_19_ = bf16[1552,128]{1,0:T(8,128)(2,1)} collective-permute-done((bf16[1552,128]{1,0:T(8,128)(2,1)S(1)}, bf16[1552,128]{1,0:T(8,128)(2,1)}, u32[]{:S(2)}, u32[]{:S(2)}) %collective-permute-start.3) | collective-permute-done | bytes 397344 | tf_op jit(solution)/shard_map/ppermute | solution.py:77
  65.2 1.0 copy-done.1
  66.2 1.0 copy-done.4
  67.2 1.0 copy-done.7
  70.2 2.0 copy-done.16
  72.3 17.1 %shard_map.112 = (f32[1536,128]{1,0:T(8,128)S(1)}, bf16[1536,128]{1,0:T(8,128)(2,1)S(1)}, f32[8,128]{1,0:T(8,128)S(1)}) custom-call(s32[3,16]{1,0:T(4,128)S(1)} %pad_add_fusion.info, bf16[1552,128]{1,0:T(8,128)(2,1)S(1)} %collective-permute-done.refs_0_.refs_16_, bf16[1552,128]{1,0:T(8,128)(2,1)S(1)} %collective-permute-done.1.refs_1_.refs_17_, ...), custom_call_target="tpu_custom_call" | custom-call | flops 200000000 | bytes 12000000 | tf_op jit(solution)/shard_map/pallas_call | solution.py:214
  89.3 2.1 collective-permute-start.17
  91.5 8.2 %collective-permute-done.17 = bf16[1536,128]{1,0:T(8,128)(2,1)S(1)} collective-permute-done((bf16[1536,128]{1,0:T(8,128)(2,1)S(1)}, bf16[1536,128]{1,0:T(8,128)(2,1)S(1)}, u32[]{:S(2)}, u32[]{:S(2)}) %collective-permute-start.17) | collective-permute-done | bytes 393248 | tf_op jit(solution)/shard_map/ppermute | solution.py:268
  99.8 2.3 collective-permute-start.22
  102.0 1.9 collective-permute-start.18
  104.0 7.6 %collective-permute-done.22.refs_4_ = bf16[1536,128]{1,0:T(8,128)(2,1)S(1)} collective-permute-done((bf16[1536,128]{1,0:T(8,128)(2,1)S(1)}, bf16[1536,128]{1,0:T(8,128)(2,1)S(1)}, u32[]{:S(2)}, u32[]{:S(2)}) %collective-permute-start.22) | collective-permute-done | bytes 393248 | tf_op jit(solution)/shard_map/ppermute | solution.py:71
  111.6 2.0 collective-permute-start.23
  115.4 2.9 %collective-permute-start.20 = (bf16[1536,128]{1,0:T(8,128)(2,1)S(1)}, bf16[1536,128]{1,0:T(8,128)(2,1)}, u32[]{:S(2)}, u32[]{:S(2)}) collective-permute-start(bf16[1536,128]{1,0:T(8,128)(2,1)S(1)} %collective-permute-done.18.refs_0_), channel_id=1, source_target_pairs={{0,6},{2,0},{4,2},{6,4},{1,7},{3,1},{5,3},{7,5},{8,14},{10,8},{12,... | collective-permute-start | bytes 1179656 | tf_op jit(solution)/shard_map/ppermute | solution.py:75
  119.1 4.4 %collective-permute-done.24.refs_6_ = bf16[1536,128]{1,0:T(8,128)(2,1)S(1)} collective-permute-done((bf16[1536,128]{1,0:T(8,128)(2,1)S(1)}, bf16[1536,128]{1,0:T(8,128)(2,1)S(1)}, u32[]{:S(2)}, u32[]{:S(2)}) %collective-permute-start.24) | collective-permute-done | bytes 393248 | tf_op jit(solution)/shard_map/ppermute | solution.py:74
  123.5 1.3 collective-permute-done.23.refs_5_
  125.6 7.3 %collective-permute-done.19.refs_1_ = bf16[1536,128]{1,0:T(8,128)(2,1)} collective-permute-done((bf16[1536,128]{1,0:T(8,128)(2,1)S(1)}, bf16[1536,128]{1,0:T(8,128)(2,1)}, u32[]{:S(2)}, u32[]{:S(2)}) %collective-permute-start.19) | collective-permute-done | bytes 393248 | tf_op jit(solution)/shard_map/ppermute | solution.py:73
  135.4 4.6 %collective-permute-done.25.refs_7_ = bf16[1536,128]{1,0:T(8,128)(2,1)} collective-permute-done((bf16[1536,128]{1,0:T(8,128)(2,1)S(1)}, bf16[1536,128]{1,0:T(8,128)(2,1)}, u32[]{:S(2)}, u32[]{:S(2)}) %collective-permute-start.25) | collective-permute-done | bytes 393248 | tf_op jit(solution)/shard_map/ppermute | solution.py:78
  140.0 5.1 %collective-permute-done.21.refs_3_ = bf16[1536,128]{1,0:T(8,128)(2,1)} collective-permute-done((bf16[1536,128]{1,0:T(8,128)(2,1)}, bf16[1536,128]{1,0:T(8,128)(2,1)}, u32[]{:S(2)}, u32[]{:S(2)}) %collective-permute-start.21) | collective-permute-done | bytes 393248 | tf_op jit(solution)/shard_map/ppermute | solution.py:77
  145.1 2.0 collective-permute-done.29.refs_11_
  147.2 1.0 copy-done.2
  152.2 1.9 copy-done.15
  160.0 15.3 %shard_map.113 = (f32[1536,128]{1,0:T(8,128)S(1)}, bf16[1536,128]{1,0:T(8,128)(2,1)S(1)}) custom-call(s32[3,16]{1,0:T(4,128)S(1)} %pad_add_fusion.info, bf16[1536,128]{1,0:T(8,128)(2,1)S(1)} %copy-done.20, bf16[1536,128]{1,0:T(8,128)(2,1)} %collective-permute-done.19.refs_1_, bf16[1536,128]{1,0:T(8,128)(2,1)} %collective-permute-done.20.refs_2_, ...), custom_call_target="tpu_custom_call" | custom-call | flops 200000000 | bytes 12000000 | tf_op jit(solution)/shard_map/pallas_call | solution.py:214
  175.4 3.2 %collective-permute-start.34 = (bf16[1536,128]{1,0:T(8,128)(2,1)S(1)}, bf16[1536,128]{1,0:T(8,128)(2,1)S(1)}, u32[]{:S(2)}, u32[]{:S(2)}) collective-permute-start(bf16[1536,128]{1,0:T(8,128)(2,1)S(1)} %get-tuple-element.11), channel_id=1, source_target_pairs={{0,16},{16,0},{1,17},{17,1},{2,18},{18,2},{3,19},{19,3},{4,20},{20... | collective-permute-start | bytes 1179656 | tf_op jit(solution)/shard_map/ppermute | solution.py:273
  178.5 1.2 collective-permute-done.35
  179.8 6.7 %collective-permute-done.36 = f32[8,128]{1,0:T(8,128)S(1)} collective-permute-done((f32[8,128]{1,0:T(8,128)S(1)}, f32[8,128]{1,0:T(8,128)S(1)}, u32[]{:S(2)}, u32[]{:S(2)}) %collective-permute-start.36) | collective-permute-done | bytes 4128 | tf_op jit(solution)/shard_map/ppermute | solution.py:246
  186.5 1.0 collective-permute-start.37
  187.5 4.1 %collective-permute-done.37 = f32[8,128]{1,0:T(8,128)S(1)} collective-permute-done((f32[8,128]{1,0:T(8,128)S(1)}, f32[8,128]{1,0:T(8,128)S(1)}, u32[]{:S(2)}, u32[]{:S(2)}) %collective-permute-start.37) | collective-permute-done | bytes 4128 | tf_op jit(solution)/shard_map/ppermute | solution.py:246
  191.9 3.3 %collective-permute-done.38 = f32[8,128]{1,0:T(8,128)S(1)} collective-permute-done((f32[8,128]{1,0:T(8,128)S(1)}, f32[8,128]{1,0:T(8,128)S(1)}, u32[]{:S(2)}, u32[]{:S(2)}) %collective-permute-start.38) | collective-permute-done | bytes 4128 | tf_op jit(solution)/shard_map/ppermute | solution.py:246
  195.4 5.0 %collective-permute-done.39 = f32[8,128]{1,0:T(8,128)S(1)} collective-permute-done((f32[8,128]{1,0:T(8,128)S(1)}, f32[8,128]{1,0:T(8,128)S(1)}, u32[]{:S(2)}, u32[]{:S(2)}) %collective-permute-start.39) | collective-permute-done | bytes 4128 | tf_op jit(solution)/shard_map/ppermute | solution.py:246
  200.3 1.7 collective-permute-start.40
  202.1 1.9 collective-permute-done.40
  203.9 5.0 %collective-permute-start.41 = (f32[8,128]{1,0:T(8,128)S(1)}, f32[8,128]{1,0:T(8,128)S(1)}, u32[]{:S(2)}, u32[]{:S(2)}) collective-permute-start(f32[8,128]{1,0:T(8,128)S(1)} %add.134), channel_id=1, source_target_pairs={{0,64},{32,96},{64,0},{96,32},{128,192},{160,224},{192,128},{224,1... | collective-permute-start | bytes 12296 | tf_op jit(solution)/shard_map/ppermute | solution.py:246
  208.9 1.6 collective-permute-done.41
  210.5 8.0 %collective-permute-start.42 = (f32[8,128]{1,0:T(8,128)S(1)}, f32[8,128]{1,0:T(8,128)S(1)}, u32[]{:S(2)}, u32[]{:S(2)}) collective-permute-start(f32[8,128]{1,0:T(8,128)S(1)} %add.135), channel_id=1, source_target_pairs={{0,128},{32,160},{64,192},{96,224},{128,0},{160,32},{192,64},{224,... | collective-permute-start | bytes 12296 | tf_op jit(solution)/shard_map/ppermute | solution.py:246
  218.5 1.6 collective-permute-done.42
  (133 shorter events, 27.0 us)
Async XLA Ops:
  7.2 58.1 %all-gather.3.cloned.1.call-start = ((), (), s32[]{:S(2)}) async-start(), calls=%async_computation | async-start | bytes 3575808 | tf_op jit(solution)/shard_map/all_gather | solution.py:261
  11.2 133.9 %all-gather.5.cloned.1.call-start = ((), (), s32[]{:S(2)}) async-start(), calls=%async_computation.1 | async-start | bytes 3575808 | tf_op jit(solution)/shard_map/all_gather | solution.py:262
  13.2 11.5 %collective-permute-start.4 = (bf16[1552,128]{1,0:T(8,128)(2,1)}, bf16[1552,128]{1,0:T(8,128)(2,1)S(1)}, u32[]{:S(2)}, u32[]{:S(2)}) collective-permute-start(bf16[1552,128]{1,0:T(8,128)(2,1)} %pad_maximum_fusion), channel_id=1, source_target_pairs={{1,17},{0,9},{16,8},{17,24},{9,25},{8,1},{24,0},{25,16},{3,19},{2,... | collective-permute-start | bytes 1191944 | tf_op jit(solution)/shard_map/ppermute | solution.py:71
  14.8 12.9 %collective-permute-start = (bf16[1552,128]{1,0:T(8,128)(2,1)}, bf16[1552,128]{1,0:T(8,128)(2,1)S(1)}, u32[]{:S(2)}, u32[]{:S(2)}) collective-permute-start(bf16[1552,128]{1,0:T(8,128)(2,1)} %pad_maximum_fusion), channel_id=1, source_target_pairs={{1,24},{0,0},{16,1},{17,17},{9,16},{8,8},{24,9},{25,25},{3,26},{2,... | collective-permute-start | bytes 1191944 | tf_op jit(solution)/shard_map/ppermute | solution.py:72
  24.7 7.7 %collective-permute-start.12 = (bf16[1552,128]{1,0:T(8,128)(2,1)S(1)}, bf16[1552,128]{1,0:T(8,128)(2,1)S(1)}, u32[]{:S(2)}, u32[]{:S(2)}) collective-permute-start(bf16[1552,128]{1,0:T(8,128)(2,1)S(1)} %collective-permute-done.4.refs_4_.refs_20_), channel_id=1, source_target_pairs={{0,1},{1,0},{2,3},{3,2},{4,5},{5,4},{6,7},{7,6},{8,9},{9,8},{10,11... | collective-permute-start | bytes 1191944 | tf_op jit(solution)/shard_map/ppermute | solution.py:80
  24.7 12.5 %collective-permute-start.6 = (bf16[1552,128]{1,0:T(8,128)(2,1)S(1)}, bf16[1552,128]{1,0:T(8,128)(2,1)S(1)}, u32[]{:S(2)}, u32[]{:S(2)}) collective-permute-start(bf16[1552,128]{1,0:T(8,128)(2,1)S(1)} %collective-permute-done.4.refs_4_.refs_20_), channel_id=1, source_target_pairs={{0,6},{2,0},{4,2},{6,4},{1,7},{3,1},{5,3},{7,5},{8,14},{10,8},{12,... | collective-permute-start | bytes 1191944 | tf_op jit(solution)/shard_map/ppermute | solution.py:74
  27.7 13.2 %collective-permute-start.5 = (bf16[1552,128]{1,0:T(8,128)(2,1)S(1)}, bf16[1552,128]{1,0:T(8,128)(2,1)S(1)}, u32[]{:S(2)}, u32[]{:S(2)}) collective-permute-start(bf16[1552,128]{1,0:T(8,128)(2,1)S(1)} %collective-permute-done.4.refs_4_.refs_20_), channel_id=1, source_target_pairs={{0,2},{2,4},{4,6},{6,0},{1,3},{3,5},{5,7},{7,1},{8,10},{10,12},{12... | collective-permute-start | bytes 1191944 | tf_op jit(solution)/shard_map/ppermute | solution.py:76
  27.7 21.1 %collective-permute-start.1 = (bf16[1552,128]{1,0:T(8,128)(2,1)S(1)}, bf16[1552,128]{1,0:T(8,128)(2,1)S(1)}, u32[]{:S(2)}, u32[]{:S(2)}) collective-permute-start(bf16[1552,128]{1,0:T(8,128)(2,1)S(1)} %collective-permute-done.refs_0_.refs_16_), channel_id=1, source_target_pairs={{0,2},{2,4},{4,6},{6,0},{1,3},{3,5},{5,7},{7,1},{8,10},{10,12},{12... | collective-permute-start | bytes 1191944 | tf_op jit(solution)/shard_map/ppermute | solution.py:73
  28.3 4.1 %collective-permute-start.16 = (bf16[16,128]{1,0:T(8,128)(2,1)S(1)}, bf16[16,128]{1,0:T(8,128)(2,1)S(1)}, u32[]{:S(2)}, u32[]{:S(2)}) collective-permute-start(bf16[16,128]{1,0:T(8,128)(2,1)S(1)} %broadcast_in_dim.67), channel_id=1, source_target_pairs={{0,16},{16,0},{1,17},{17,1},{2,18},{18,2},{3,19},{19,3},{4,20},{20... | collective-permute-start | bytes 12296 | tf_op jit(solution)/shard_map/ppermute | solution.py:263
  32.4 16.5 %collective-permute-start.8 = (bf16[1552,128]{1,0:T(8,128)(2,1)S(1)}, bf16[1552,128]{1,0:T(8,128)(2,1)S(1)}, u32[]{:S(2)}, u32[]{:S(2)}) collective-permute-start(bf16[1552,128]{1,0:T(8,128)(2,1)S(1)} %collective-permute-done.refs_0_.refs_16_), channel_id=1, source_target_pairs={{0,1},{1,0},{2,3},{3,2},{4,5},{5,4},{6,7},{7,6},{8,9},{9,8},{10,11... | collective-permute-start | bytes 1191944 | tf_op jit(solution)/shard_map/ppermute | solution.py:80
  32.4 16.6 %collective-permute-start.2 = (bf16[1552,128]{1,0:T(8,128)(2,1)S(1)}, bf16[1552,128]{1,0:T(8,128)(2,1)S(1)}, u32[]{:S(2)}, u32[]{:S(2)}) collective-permute-start(bf16[1552,128]{1,0:T(8,128)(2,1)S(1)} %collective-permute-done.refs_0_.refs_16_), channel_id=1, source_target_pairs={{0,6},{2,0},{4,2},{6,4},{1,7},{3,1},{5,3},{7,5},{8,14},{10,8},{12,... | collective-permute-start | bytes 1191944 | tf_op jit(solution)/shard_map/ppermute | solution.py:75
  37.2 12.2 %collective-permute-start.14 = (bf16[1552,128]{1,0:T(8,128)(2,1)S(1)}, bf16[1552,128]{1,0:T(8,128)(2,1)}, u32[]{:S(2)}, u32[]{:S(2)}) collective-permute-start(bf16[1552,128]{1,0:T(8,128)(2,1)S(1)} %collective-permute-done.6.refs_6_.refs_22_), channel_id=1, source_target_pairs={{0,1},{1,0},{2,3},{3,2},{4,5},{5,4},{6,7},{7,6},{8,9},{9,8},{10,11... | collective-permute-start | bytes 1191944 | tf_op jit(solution)/shard_map/ppermute | solution.py:80
  40.9 12.9 %collective-permute-start.7 = (bf16[1552,128]{1,0:T(8,128)(2,1)S(1)}, bf16[1552,128]{1,0:T(8,128)(2,1)}, u32[]{:S(2)}, u32[]{:S(2)}) collective-permute-start(bf16[1552,128]{1,0:T(8,128)(2,1)S(1)} %collective-permute-done.6.refs_6_.refs_22_), channel_id=1, source_target_pairs={{0,6},{2,0},{4,2},{6,4},{1,7},{3,1},{5,3},{7,5},{8,14},{10,8},{12,... | collective-permute-start | bytes 1191944 | tf_op jit(solution)/shard_map/ppermute | solution.py:78
  48.7 11.9 %collective-permute-start.3 = (bf16[1552,128]{1,0:T(8,128)(2,1)S(1)}, bf16[1552,128]{1,0:T(8,128)(2,1)}, u32[]{:S(2)}, u32[]{:S(2)}) collective-permute-start(bf16[1552,128]{1,0:T(8,128)(2,1)S(1)} %collective-permute-done.1.refs_1_.refs_17_), channel_id=1, source_target_pairs={{0,2},{2,4},{4,6},{6,0},{1,3},{3,5},{5,7},{7,1},{8,10},{10,12},{12... | collective-permute-start | bytes 1191944 | tf_op jit(solution)/shard_map/ppermute | solution.py:77
  48.8 14.1 %collective-permute-start.9 = (bf16[1552,128]{1,0:T(8,128)(2,1)S(1)}, bf16[1552,128]{1,0:T(8,128)(2,1)S(1)}, u32[]{:S(2)}, u32[]{:S(2)}) collective-permute-start(bf16[1552,128]{1,0:T(8,128)(2,1)S(1)} %collective-permute-done.1.refs_1_.refs_17_), channel_id=1, source_target_pairs={{0,1},{1,0},{2,3},{3,2},{4,5},{5,4},{6,7},{7,6},{8,9},{9,8},{10,11... | collective-permute-start | bytes 1191944 | tf_op jit(solution)/shard_map/ppermute | solution.py:80
  48.9 12.5 %collective-permute-start.13 = (bf16[1552,128]{1,0:T(8,128)(2,1)S(1)}, bf16[1552,128]{1,0:T(8,128)(2,1)S(1)}, u32[]{:S(2)}, u32[]{:S(2)}) collective-permute-start(bf16[1552,128]{1,0:T(8,128)(2,1)S(1)} %collective-permute-done.5.refs_5_.refs_21_), channel_id=1, source_target_pairs={{0,1},{1,0},{2,3},{3,2},{4,5},{5,4},{6,7},{7,6},{8,9},{9,8},{10,11... | collective-permute-start | bytes 1191944 | tf_op jit(solution)/shard_map/ppermute | solution.py:80
  49.4 12.7 %collective-permute-start.10 = (bf16[1552,128]{1,0:T(8,128)(2,1)S(1)}, bf16[1552,128]{1,0:T(8,128)(2,1)S(1)}, u32[]{:S(2)}, u32[]{:S(2)}) collective-permute-start(bf16[1552,128]{1,0:T(8,128)(2,1)S(1)} %collective-permute-done.2.refs_2_.refs_18_), channel_id=1, source_target_pairs={{0,1},{1,0},{2,3},{3,2},{4,5},{5,4},{6,7},{7,6},{8,9},{9,8},{10,11... | collective-permute-start | bytes 1191944 | tf_op jit(solution)/shard_map/ppermute | solution.py:80
  53.8 9.9 %collective-permute-start.15 = (bf16[1552,128]{1,0:T(8,128)(2,1)}, bf16[1552,128]{1,0:T(8,128)(2,1)S(1)}, u32[]{:S(2)}, u32[]{:S(2)}) collective-permute-start(bf16[1552,128]{1,0:T(8,128)(2,1)} %collective-permute-done.7.refs_7_.refs_23_), channel_id=1, source_target_pairs={{0,1},{1,0},{2,3},{3,2},{4,5},{5,4},{6,7},{7,6},{8,9},{9,8},{10,11... | collective-permute-start | bytes 1191944 | tf_op jit(solution)/shard_map/ppermute | solution.py:80
  60.7 3.8 %collective-permute-start.11 = (bf16[1552,128]{1,0:T(8,128)(2,1)}, bf16[1552,128]{1,0:T(8,128)(2,1)S(1)}, u32[]{:S(2)}, u32[]{:S(2)}) collective-permute-start(bf16[1552,128]{1,0:T(8,128)(2,1)} %collective-permute-done.3.refs_3_.refs_19_), channel_id=1, source_target_pairs={{0,1},{1,0},{2,3},{3,2},{4,5},{5,4},{6,7},{7,6},{8,9},{9,8},{10,11... | collective-permute-start | bytes 1191944 | tf_op jit(solution)/shard_map/ppermute | solution.py:80
  70.2 2.0 copy-start.16
  89.3 10.3 %collective-permute-start.17 = (bf16[1536,128]{1,0:T(8,128)(2,1)S(1)}, bf16[1536,128]{1,0:T(8,128)(2,1)S(1)}, u32[]{:S(2)}, u32[]{:S(2)}) collective-permute-start(bf16[1536,128]{1,0:T(8,128)(2,1)S(1)} %get-tuple-element.9), channel_id=1, source_target_pairs={{0,16},{16,0},{1,17},{17,1},{2,18},{18,2},{3,19},{19,3},{4,20},{20... | collective-permute-start | bytes 1179656 | tf_op jit(solution)/shard_map/ppermute | solution.py:268
  99.8 40.3 %copy-start.29 = (bf16[1536,128]{1,0:T(8,128)(2,1)}, bf16[1536,128]{1,0:T(8,128)(2,1)S(1)}, u32[]{:S(2)}) copy-start(bf16[1536,128]{1,0:T(8,128)(2,1)S(1)} %add_convert_fusion.1) | copy-start | bytes 1179652
  99.8 11.8 %collective-permute-start.22 = (bf16[1536,128]{1,0:T(8,128)(2,1)S(1)}, bf16[1536,128]{1,0:T(8,128)(2,1)S(1)}, u32[]{:S(2)}, u32[]{:S(2)}) collective-permute-start(bf16[1536,128]{1,0:T(8,128)(2,1)S(1)} %add_convert_fusion.1), channel_id=1, source_target_pairs={{1,17},{0,9},{16,8},{17,24},{9,25},{8,1},{24,0},{25,16},{3,19},{2,... | collective-permute-start | bytes 1179656 | tf_op jit(solution)/shard_map/ppermute | solution.py:71
  102.0 12.3 %collective-permute-start.18 = (bf16[1536,128]{1,0:T(8,128)(2,1)S(1)}, bf16[1536,128]{1,0:T(8,128)(2,1)S(1)}, u32[]{:S(2)}, u32[]{:S(2)}) collective-permute-start(bf16[1536,128]{1,0:T(8,128)(2,1)S(1)} %add_convert_fusion.1), channel_id=1, source_target_pairs={{1,24},{0,0},{16,1},{17,17},{9,16},{8,8},{24,9},{25,25},{3,26},{2,... | collective-permute-start | bytes 1179656 | tf_op jit(solution)/shard_map/ppermute | solution.py:72
  111.5 3.1 %collective-permute-start.30 = (bf16[1536,128]{1,0:T(8,128)(2,1)S(1)}, bf16[1536,128]{1,0:T(8,128)(2,1)S(1)}, u32[]{:S(2)}, u32[]{:S(2)}) collective-permute-start(bf16[1536,128]{1,0:T(8,128)(2,1)S(1)} %collective-permute-done.22.refs_4_), channel_id=1, source_target_pairs={{0,1},{1,0},{2,3},{3,2},{4,5},{5,4},{6,7},{7,6},{8,9},{9,8},{10,11... | collective-permute-start | bytes 1179656 | tf_op jit(solution)/shard_map/ppermute | solution.py:80
  111.5 11.9 %collective-permute-start.24 = (bf16[1536,128]{1,0:T(8,128)(2,1)S(1)}, bf16[1536,128]{1,0:T(8,128)(2,1)S(1)}, u32[]{:S(2)}, u32[]{:S(2)}) collective-permute-start(bf16[1536,128]{1,0:T(8,128)(2,1)S(1)} %collective-permute-done.22.refs_4_), channel_id=1, source_target_pairs={{0,6},{2,0},{4,2},{6,4},{1,7},{3,1},{5,3},{7,5},{8,14},{10,8},{12,... | collective-permute-start | bytes 1179656 | tf_op jit(solution)/shard_map/ppermute | solution.py:74
  111.6 13.2 %collective-permute-start.23 = (bf16[1536,128]{1,0:T(8,128)(2,1)S(1)}, bf16[1536,128]{1,0:T(8,128)(2,1)}, u32[]{:S(2)}, u32[]{:S(2)}) collective-permute-start(bf16[1536,128]{1,0:T(8,128)(2,1)S(1)} %collective-permute-done.22.refs_4_), channel_id=1, source_target_pairs={{0,2},{2,4},{4,6},{6,0},{1,3},{3,5},{5,7},{7,1},{8,10},{10,12},{12... | collective-permute-start | bytes 1179656 | tf_op jit(solution)/shard_map/ppermute | solution.py:76
  114.3 18.5 %collective-permute-start.19 = (bf16[1536,128]{1,0:T(8,128)(2,1)S(1)}, bf16[1536,128]{1,0:T(8,128)(2,1)}, u32[]{:S(2)}, u32[]{:S(2)}) collective-permute-start(bf16[1536,128]{1,0:T(8,128)(2,1)S(1)} %collective-permute-done.18.refs_0_), channel_id=1, source_target_pairs={{0,2},{2,4},{4,6},{6,0},{1,3},{3,5},{5,7},{7,1},{8,10},{10,12},{12... | collective-permute-start | bytes 1179656 | tf_op jit(solution)/shard_map/ppermute | solution.py:73
  114.7 18.7 %collective-permute-start.26 = (bf16[1536,128]{1,0:T(8,128)(2,1)S(1)}, bf16[1536,128]{1,0:T(8,128)(2,1)S(1)}, u32[]{:S(2)}, u32[]{:S(2)}) collective-permute-start(bf16[1536,128]{1,0:T(8,128)(2,1)S(1)} %collective-permute-done.18.refs_0_), channel_id=1, source_target_pairs={{0,1},{1,0},{2,3},{3,2},{4,5},{5,4},{6,7},{7,6},{8,9},{9,8},{10,11... | collective-permute-start | bytes 1179656 | tf_op jit(solution)/shard_map/ppermute | solution.py:80
  115.4 18.7 %collective-permute-start.20 = (bf16[1536,128]{1,0:T(8,128)(2,1)S(1)}, bf16[1536,128]{1,0:T(8,128)(2,1)}, u32[]{:S(2)}, u32[]{:S(2)}) collective-permute-start(bf16[1536,128]{1,0:T(8,128)(2,1)S(1)} %collective-permute-done.18.refs_0_), channel_id=1, source_target_pairs={{0,6},{2,0},{4,2},{6,4},{1,7},{3,1},{5,3},{7,5},{8,14},{10,8},{12,... | collective-permute-start | bytes 1179656 | tf_op jit(solution)/shard_map/ppermute | solution.py:75
  123.5 11.2 %collective-permute-start.32 = (bf16[1536,128]{1,0:T(8,128)(2,1)S(1)}, bf16[1536,128]{1,0:T(8,128)(2,1)S(1)}, u32[]{:S(2)}, u32[]{:S(2)}) collective-permute-start(bf16[1536,128]{1,0:T(8,128)(2,1)S(1)} %collective-permute-done.24.refs_6_), channel_id=1, source_target_pairs={{0,1},{1,0},{2,3},{3,2},{4,5},{5,4},{6,7},{7,6},{8,9},{9,8},{10,11... | collective-permute-start | bytes 1179656 | tf_op jit(solution)/shard_map/ppermute | solution.py:80
  124.8 15.3 %collective-permute-start.25 = (bf16[1536,128]{1,0:T(8,128)(2,1)S(1)}, bf16[1536,128]{1,0:T(8,128)(2,1)}, u32[]{:S(2)}, u32[]{:S(2)}) collective-permute-start(bf16[1536,128]{1,0:T(8,128)(2,1)S(1)} %collective-permute-done.24.refs_6_), channel_id=1, source_target_pairs={{0,6},{2,0},{4,2},{6,4},{1,7},{3,1},{5,3},{7,5},{8,14},{10,8},{12,... | collective-permute-start | bytes 1179656 | tf_op jit(solution)/shard_map/ppermute | solution.py:78
  132.8 12.3 %collective-permute-start.21 = (bf16[1536,128]{1,0:T(8,128)(2,1)}, bf16[1536,128]{1,0:T(8,128)(2,1)}, u32[]{:S(2)}, u32[]{:S(2)}) collective-permute-start(bf16[1536,128]{1,0:T(8,128)(2,1)} %collective-permute-done.19.refs_1_), channel_id=1, source_target_pairs={{0,2},{2,4},{4,6},{6,0},{1,3},{3,5},{5,7},{7,1},{8,10},{10,12},{12... | collective-permute-start | bytes 1179656 | tf_op jit(solution)/shard_map/ppermute | solution.py:77
  134.1 11.0 %collective-permute-start.27 = (bf16[1536,128]{1,0:T(8,128)(2,1)}, bf16[1536,128]{1,0:T(8,128)(2,1)}, u32[]{:S(2)}, u32[]{:S(2)}) collective-permute-start(bf16[1536,128]{1,0:T(8,128)(2,1)} %collective-permute-done.19.refs_1_), channel_id=1, source_target_pairs={{0,1},{1,0},{2,3},{3,2},{4,5},{5,4},{6,7},{7,6},{8,9},{9,8},{10,11... | collective-permute-start | bytes 1179656 | tf_op jit(solution)/shard_map/ppermute | solution.py:80
  134.1 11.0 %collective-permute-start.31 = (bf16[1536,128]{1,0:T(8,128)(2,1)}, bf16[1536,128]{1,0:T(8,128)(2,1)}, u32[]{:S(2)}, u32[]{:S(2)}) collective-permute-start(bf16[1536,128]{1,0:T(8,128)(2,1)} %collective-permute-done.23.refs_5_), channel_id=1, source_target_pairs={{0,1},{1,0},{2,3},{3,2},{4,5},{5,4},{6,7},{7,6},{8,9},{9,8},{10,11... | collective-permute-start | bytes 1179656 | tf_op jit(solution)/shard_map/ppermute | solution.py:80
  135.4 9.7 %collective-permute-start.28 = (bf16[1536,128]{1,0:T(8,128)(2,1)}, bf16[1536,128]{1,0:T(8,128)(2,1)}, u32[]{:S(2)}, u32[]{:S(2)}) collective-permute-start(bf16[1536,128]{1,0:T(8,128)(2,1)} %collective-permute-done.20.refs_2_), channel_id=1, source_target_pairs={{0,1},{1,0},{2,3},{3,2},{4,5},{5,4},{6,7},{7,6},{8,9},{9,8},{10,11... | collective-permute-start | bytes 1179656 | tf_op jit(solution)/shard_map/ppermute | solution.py:80
  140.0 5.1 %collective-permute-start.33 = (bf16[1536,128]{1,0:T(8,128)(2,1)}, bf16[1536,128]{1,0:T(8,128)(2,1)}, u32[]{:S(2)}, u32[]{:S(2)}) collective-permute-start(bf16[1536,128]{1,0:T(8,128)(2,1)} %collective-permute-done.25.refs_7_), channel_id=1, source_target_pairs={{0,1},{1,0},{2,3},{3,2},{4,5},{5,4},{6,7},{7,6},{8,9},{9,8},{10,11... | collective-permute-start | bytes 1179656 | tf_op jit(solution)/shard_map/ppermute | solution.py:80
  145.1 2.1 collective-permute-start.29
  152.2 1.9 copy-start.15
  175.4 45.3 %collective-permute-start.34 = (bf16[1536,128]{1,0:T(8,128)(2,1)S(1)}, bf16[1536,128]{1,0:T(8,128)(2,1)S(1)}, u32[]{:S(2)}, u32[]{:S(2)}) collective-permute-start(bf16[1536,128]{1,0:T(8,128)(2,1)S(1)} %get-tuple-element.11), channel_id=1, source_target_pairs={{0,16},{16,0},{1,17},{17,1},{2,18},{18,2},{3,19},{19,3},{4,20},{20... | collective-permute-start | bytes 1179656 | tf_op jit(solution)/shard_map/ppermute | solution.py:273
  178.5 1.2 collective-permute-start.35
  179.7 6.8 %collective-permute-start.36 = (f32[8,128]{1,0:T(8,128)S(1)}, f32[8,128]{1,0:T(8,128)S(1)}, u32[]{:S(2)}, u32[]{:S(2)}) collective-permute-start(f32[8,128]{1,0:T(8,128)S(1)} %add.129), channel_id=1, source_target_pairs={{0,16},{16,0},{1,17},{17,1},{2,18},{18,2},{3,19},{19,3},{4,20},{20... | collective-permute-start | bytes 12296 | tf_op jit(solution)/shard_map/ppermute | solution.py:246
  186.5 5.1 %collective-permute-start.37 = (f32[8,128]{1,0:T(8,128)S(1)}, f32[8,128]{1,0:T(8,128)S(1)}, u32[]{:S(2)}, u32[]{:S(2)}) collective-permute-start(f32[8,128]{1,0:T(8,128)S(1)} %add.130), channel_id=1, source_target_pairs={{0,8},{8,0},{1,9},{9,1},{2,10},{10,2},{3,11},{11,3},{4,12},{12,4},... | collective-permute-start | bytes 12296 | tf_op jit(solution)/shard_map/ppermute | solution.py:246
  191.6 3.6 %collective-permute-start.38 = (f32[8,128]{1,0:T(8,128)S(1)}, f32[8,128]{1,0:T(8,128)S(1)}, u32[]{:S(2)}, u32[]{:S(2)}) collective-permute-start(f32[8,128]{1,0:T(8,128)S(1)} %add.131), channel_id=1, source_target_pairs={{0,2},{2,0},{4,6},{6,4},{1,3},{3,1},{5,7},{7,5},{8,10},{10,8},{12,... | collective-permute-start | bytes 12296 | tf_op jit(solution)/shard_map/ppermute | solution.py:246
  195.2 5.1 %collective-permute-start.39 = (f32[8,128]{1,0:T(8,128)S(1)}, f32[8,128]{1,0:T(8,128)S(1)}, u32[]{:S(2)}, u32[]{:S(2)}) collective-permute-start(f32[8,128]{1,0:T(8,128)S(1)} %add.132), channel_id=1, source_target_pairs={{0,4},{2,6},{4,0},{6,2},{1,5},{3,7},{5,1},{7,3},{8,12},{10,14},{12... | collective-permute-start | bytes 12296 | tf_op jit(solution)/shard_map/ppermute | solution.py:246
  200.3 3.6 %collective-permute-start.40 = (f32[8,128]{1,0:T(8,128)S(1)}, f32[8,128]{1,0:T(8,128)S(1)}, u32[]{:S(2)}, u32[]{:S(2)}) collective-permute-start(f32[8,128]{1,0:T(8,128)S(1)} %add.133), channel_id=1, source_target_pairs={{0,32},{32,0},{64,96},{96,64},{128,160},{160,128},{192,224},{224,1... | collective-permute-start | bytes 12296 | tf_op jit(solution)/shard_map/ppermute | solution.py:246
  203.9 6.6 %collective-permute-start.41 = (f32[8,128]{1,0:T(8,128)S(1)}, f32[8,128]{1,0:T(8,128)S(1)}, u32[]{:S(2)}, u32[]{:S(2)}) collective-permute-start(f32[8,128]{1,0:T(8,128)S(1)} %add.134), channel_id=1, source_target_pairs={{0,64},{32,96},{64,0},{96,32},{128,192},{160,224},{192,128},{224,1... | collective-permute-start | bytes 12296 | tf_op jit(solution)/shard_map/ppermute | solution.py:246
  210.5 9.6 %collective-permute-start.42 = (f32[8,128]{1,0:T(8,128)S(1)}, f32[8,128]{1,0:T(8,128)S(1)}, u32[]{:S(2)}, u32[]{:S(2)}) collective-permute-start(f32[8,128]{1,0:T(8,128)S(1)} %add.135), channel_id=1, source_target_pairs={{0,128},{32,160},{64,192},{96,224},{128,0},{160,32},{192,64},{224,... | collective-permute-start | bytes 12296 | tf_op jit(solution)/shard_map/ppermute | solution.py:246
  (27 other events, 24.3 us)
Sparse Core Ops, SparseCore 0:
  11.4 48.2 all-gather.2
  61.4 43.8 all-gather.4

commit v2 on v1

v2 whole, which is shorter than its diff:
```python
import functools

import jax
import jax.numpy as jnp
from jax import lax
from jax.experimental import pallas as pl
from jax.experimental.pallas import tpu as pltpu
from jax.sharding import Mesh
from jax.sharding import PartitionSpec as P

TILE = 8
BLK = 128
CAP = 12
BODY = CAP * BLK
META = 16
PAY = BODY + META
LEFTS = 16
RIGHTS = 8
OUTS = 2
CODE_AT = 64
MASK_AT = 80
COLUMN_AT = 88
NO_SLOT = 255
UNROLL = 4
HALF = LEFTS // 2
ROWS = LEFTS + RIGHTS + OUTS
QUAD = 4
COUNT_AT = HALF * CAP * TILE + UNROLL
LIST = COUNT_AT + 4
RING_Y = 4
RING_Z = 8
WIDE = 256
AXES = ("z", "x_lo", "x_hi", "y", "core")
ROW = ("z", "x_lo")
COL = ("x_hi", "y", "core")
IN_CHIP_X = ("x_lo", "x_hi", "core")


def describe(where, count, row, col):
    slot = lax.broadcasted_iota(jnp.int32, (CAP, BLK), 0)
    lane = lax.broadcasted_iota(jnp.int32, (CAP, BLK), 1)
    live = slot < count[0, 0]
    r = (where[:, 0] - row * TILE)[:, None]
    c = (where[:, 1] - col * TILE)[:, None]
    code = jnp.where(live, r * TILE + c, NO_SLOT)
    here = jnp.where(code == lane, slot + 1, 0)
    names = jnp.where(slot == lane - CODE_AT, code, 0)
    bits = jnp.where(live & (r == lane - MASK_AT), jnp.left_shift(1, c), 0)
    column_bits = jnp.where(live & (c == lane - COLUMN_AT), jnp.left_shift(1, r), 0)
    masks = jnp.where(lane < COLUMN_AT, bits, column_bits)
    values = jnp.where(lane < CODE_AT, here, jnp.where(lane < MASK_AT, names, masks))
    line = jnp.sum(values, axis=0, keepdims=True).astype(jnp.bfloat16)
    return jnp.broadcast_to(line, (META, BLK))


def x_index(x_lo, x_hi, core):
    return (x_lo * 2 + x_hi) * 2 + core


def x_perms():
    first, second = [], []
    for x in range(4):
        a, b = x % 2, 1 - x % 2
        right, far, left = (x + 1) % 4, (x + 2) % 4, (x + 3) % 4
        at = lambda chip, core: x_index(chip % 2, chip // 2, core)
        first.append((at(x, b), at(right, right % 2)))
        first.append((at(x, a), at(far, 1 - far % 2)))
        second.append((at(x, b), at(left, 1 - left % 2)))
        second.append((at(x, a), at(x, a)))
    return first, second


def ring(n, step):
    return [(i, (i + step) % n) for i in range(n)]


def spread(tile, beside=lambda stage, *tiles: tiles):
    first, second = x_perms()
    far = lax.ppermute(tile, IN_CHIP_X, first)
    near = lax.ppermute(tile, IN_CHIP_X, second)
    far, near = beside(0, far, near)
    near_up = lax.ppermute(near, "y", ring(RING_Y, 1))
    far_down = lax.ppermute(far, "y", ring(RING_Y, -1))
    near_down = lax.ppermute(near, "y", ring(RING_Y, -1))
    far_up = lax.ppermute(far, "y", ring(RING_Y, 1))
    near_up, near_down, far_up, far_down = beside(1, near_up, near_down, far_up, far_down)
    near_two = lax.ppermute(near_up, "y", ring(RING_Y, 1))
    far_two = lax.ppermute(far_down, "y", ring(RING_Y, -1))
    near_two, far_two = beside(2, near_two, far_two)
    mine = [near, near_up, near_down, near_two, far, far_up, far_down, far_two]
    theirs = [lax.ppermute(t, "core", ring(2, 1)) for t in mine]
    return mine + theirs


IF_SAME = (4, 5, 6, 7, 8, 9, 10, 11, 0, 1, 2, 3, 12, 13, 14, 15)
IF_OTHER = (0, 1, 2, 3, 12, 13, 14, 15, 4, 5, 6, 7, 8, 9, 10, 11)


def tile_table(x, y, core):
    same = core == x % 2
    dy = jnp.array([0, -1, 1, 2] * 4, jnp.int32)
    if_same = jnp.array([0] * 4 + [-1] * 4 + [1] * 4 + [2] * 4, jnp.int32)
    if_other = jnp.array([1] * 4 + [2] * 4 + [0] * 4 + [-1] * 4, jnp.int32)
    from_x = (x + jnp.where(same, if_same, if_other) + 4) % 4
    from_y = (y + dy + RING_Y) % RING_Y
    order = jnp.where(same, jnp.array(IF_SAME, jnp.int32), jnp.array(IF_OTHER, jnp.int32))
    return (from_x // 2) * RING_Y + from_y, order, same


def block(n):
    return pl.ds(pl.multiple_of(n * BLK, BLK), BLK)


def start_metas(metas, right, mv, sems):
    copies = [(metas[t].at[pl.ds(BODY, META)], mv.at[pl.ds(t * META, META)]) for t in range(LEFTS)]
    for t in range(RIGHTS):
        copies.append((right.at[pl.ds(t * PAY + BODY, META)], mv.at[pl.ds((LEFTS + t) * META, META)]))
    copies = [pltpu.make_async_copy(a, b, sems.at[n]) for n, (a, b) in enumerate(copies)]
    for copy in copies:
        copy.start()
    return copies


def plan(copies, info, outs, mv, mi, sm, meta_sem, lists):
    for copy in copies:
        copy.wait()
    for t in range(LEFTS + RIGHTS):
        mi[t : t + 1, :] = mv[t * META : (t + 1) * META, :].astype(jnp.float32)[0:1].astype(jnp.int32)
    for t in range(OUTS):
        at = LEFTS + RIGHTS + t
        mi[at : at + 1, :] = outs[t * META : (t + 1) * META, :].astype(jnp.float32)[0:1].astype(jnp.int32)
    for half in range(2):
        for g in range(HALF // QUAD):
            rows, columns = 0, 0
            for q in range(QUAD):
                tile = info[1, half * HALF + g * QUAD + q]
                rows = rows | (mi[pl.ds(tile, 1), :] << (8 * q))
                columns = columns | (mi[pl.ds(LEFTS + info[0, tile], 1), :] << (8 * q))
            at = ROWS + half * 2 + g
            mi[at : at + 1, :] = rows
            mi[at + QUAD : at + QUAD + 1, :] = columns
    to_scalar = pltpu.make_async_copy(mi, sm, meta_sem)
    to_scalar.start()
    to_scalar.wait()

    for half, todo in enumerate(lists):
        o_row = LEFTS + RIGHTS + 1 - half

        def each_out(o, count):
            code = sm[o_row, CODE_AT + o]
            i, j = code >> 3, code & 7
            for g in range(HALF // QUAD):
                at = ROWS + half * 2 + g
                word = sm[at, MASK_AT + i] & sm[at + QUAD, COLUMN_AT + j]

                def hits(count):
                    for q in range(QUAD):
                        n = g * QUAD + q
                        tile = info[1, half * HALF + n]
                        k_tile = info[0, tile]
                        base = ((n * CAP - 1) << 16) + ((k_tile * CAP - 1) << 8) + o

                        def one(state):
                            bits, count = state
                            low = bits & -bits
                            k = (
                                ((low & 0xAA) != 0).astype(jnp.int32)
                                + 2 * ((low & 0xCC) != 0).astype(jnp.int32)
                                + 4 * ((low & 0xF0) != 0).astype(jnp.int32)
                            )
                            left = sm[tile, (i & 7) * TILE + k]
                            right = sm[LEFTS + k_tile, k * TILE + j]
                            todo[count] = base + (left << 16) + (right << 8)
                            return bits - low, count + 1

                        byte = (word >> (8 * q)) & 255
                        count = lax.while_loop(lambda state: state[0] != 0, one, (byte, count))[1]
                    return count

                count = lax.cond(word != 0, hits, lambda count: count, count)
            return count

        count = lax.fori_loop(0, CAP, each_out, jnp.int32(0))
        for u in range(UNROLL):
            todo[count + u] = CAP
        todo[COUNT_AT] = count


def load(half, info, lefts, right, lv, rv, sems, wait):
    for t in range(RIGHTS):
        copy = pltpu.make_async_copy(
            right.at[pl.ds(t * PAY, BODY)], rv.at[pl.ds(t * BODY, BODY)], sems.at[t]
        )
        copy.wait() if wait else copy.start()
    for n in range(HALF):
        to, sem = lv.at[pl.ds(n * BODY, BODY)], sems.at[RIGHTS + n]
        if wait:
            pltpu.make_async_copy(lefts[n].at[pl.ds(0, BODY)], to, sem).wait()
            continue
        for name, order in enumerate((IF_OTHER, IF_SAME)):
            source = lefts[order[half * HALF + n]].at[pl.ds(0, BODY)]

            @pl.when(info[2, 2] == name)
            def _():
                pltpu.make_async_copy(source, to, sem).start()


def multiply(todo, lv, rv, acc):
    def step(g, carry):
        entries = [todo[g * UNROLL + u] for u in range(UNROLL)]
        parts = [
            jnp.dot(lv[block(e >> 16), :], rv[block((e >> 8) & 255), :], preferred_element_type=jnp.float32)
            for e in entries
        ]
        for e, part in zip(entries, parts):
            acc[block(e & 255), :] += part
        return carry

    lax.fori_loop(0, (todo[COUNT_AT] + UNROLL - 1) // UNROLL, step, 0)


def add_trace(info, slots, row, flag, acc, energy):
    @pl.when(info[2, flag] == 1)
    def _():
        r = lax.broadcasted_iota(jnp.int32, (BLK, BLK), 0)
        c = lax.broadcasted_iota(jnp.int32, (BLK, BLK), 1)
        for i in range(TILE):
            slot = slots[row, i * TILE + i] - 1

            @pl.when(slot >= 0)
            def _():
                diagonal = jnp.where(r == c, acc[block(slot), :], 0.0)
                energy[...] += jnp.sum(diagonal.reshape(BLK // 8, 8, BLK), axis=0)


def plan_kernel(info, *refs):
    metas, right, outs = refs[:LEFTS], refs[LEFTS], refs[LEFTS + 1]
    list_a, list_b, mv, mi, sm, sems, meta_sem = refs[LEFTS + 2 :]
    copies = start_metas(metas, right, mv, sems)
    plan(copies, info, outs, mv, mi, sm, meta_sem, (list_a, list_b))


def first_kernel(info, *refs):
    lefts, right, outs = refs[:LEFTS], refs[LEFTS], refs[LEFTS + 1]
    other, list_b, energy, places, list_a, lv, rv, acc, sems, mv, mi, sm, small_sems, meta_sem = refs[LEFTS + 2 :]
    copies = start_metas(lefts, right, mv, small_sems)
    load(0, info, lefts, right, lv, rv, sems, False)
    acc[...] = jnp.zeros_like(acc)
    energy[...] = jnp.zeros_like(energy)
    plan(copies, info, outs, mv, mi, sm, meta_sem, (list_a, list_b))
    places[...] = mi[LEFTS + RIGHTS : LEFTS + RIGHTS + 8, :]
    load(0, info, lefts, right, lv, rv, sems, True)
    multiply(list_a, lv, rv, acc)
    other[...] = acc[0:BODY, :].astype(other.dtype)
    add_trace(info, sm, LEFTS + RIGHTS + 1, 1, acc, energy)


def half_kernel(half, trace, info, todo, *refs):
    lefts, right = refs[:LEFTS], refs[LEFTS]
    refs = refs[LEFTS + 1 :]
    if trace:
        places, energy_in, result, energy, lv, rv, acc, sems = refs
    else:
        result, lv, rv, acc, sems = refs
    load(half, info, lefts, right, lv, rv, sems, False)
    acc[...] = jnp.zeros_like(acc)
    load(half, info, lefts, right, lv, rv, sems, True)
    multiply(todo, lv, rv, acc)
    result[...] = acc[0:BODY, :].astype(result.dtype)
    if trace:
        energy[...] = energy_in[...]
        add_trace(info, places, 0, 0, acc, energy)


VMEM = pl.BlockSpec(memory_space=pltpu.VMEM)
SMEM = pl.BlockSpec(memory_space=pltpu.SMEM)
FAR = pl.BlockSpec(memory_space=pltpu.HBM)
LIST_SHAPE = jax.ShapeDtypeStruct((LIST,), jnp.int32)
TRACE_SHAPE = jax.ShapeDtypeStruct((8, BLK), jnp.float32)
PLACES_SHAPE = jax.ShapeDtypeStruct((8, BLK), jnp.int32)
PARAMS = pltpu.CompilerParams(vmem_limit_bytes=60 * 1024 * 1024)
BLOCKS = [
    pltpu.VMEM((HALF * BODY, BLK), jnp.bfloat16),
    pltpu.VMEM((RIGHTS * BODY, BLK), jnp.bfloat16),
    pltpu.VMEM(((CAP + 1) * BLK, BLK), jnp.float32),
    pltpu.SemaphoreType.DMA((RIGHTS + HALF,)),
]
METAS = [
    pltpu.VMEM(((LEFTS + RIGHTS) * META, BLK), jnp.bfloat16),
    pltpu.VMEM((ROWS + 14, BLK), jnp.int32),
    pltpu.SMEM((ROWS + 14, BLK), jnp.int32),
    pltpu.SemaphoreType.DMA((LEFTS + RIGHTS,)),
    pltpu.SemaphoreType.DMA,
]


def cost(flops, moved):
    return pl.CostEstimate(flops=flops, bytes_accessed=moved, transcendentals=0)


def plan_lists(info, metas, right, outs):
    return pl.pallas_call(
        plan_kernel,
        out_shape=[LIST_SHAPE, LIST_SHAPE],
        in_specs=[SMEM] + [FAR] * (LEFTS + 1) + [VMEM],
        out_specs=[SMEM, SMEM],
        scratch_shapes=METAS,
        compiler_params=PARAMS,
        cost_estimate=cost(1_000_000, 10_000_000),
    )(info, *metas, right, outs)


def first_half(info, lefts, right, outs):
    return pl.pallas_call(
        first_kernel,
        out_shape=[jax.ShapeDtypeStruct((BODY, BLK), jnp.bfloat16), LIST_SHAPE, TRACE_SHAPE, PLACES_SHAPE],
        in_specs=[SMEM] + [FAR] * (LEFTS + 1) + [VMEM],
        out_specs=[VMEM, SMEM, VMEM, VMEM],
        scratch_shapes=[pltpu.SMEM((LIST,), jnp.int32)] + BLOCKS + METAS,
        compiler_params=PARAMS,
        cost_estimate=cost(100_000_000, 20_000_000),
    )(info, *lefts, right, outs)


def later_half(half, kind, info, todo, lefts, right, *trace):
    shapes = [jax.ShapeDtypeStruct((BODY, BLK), kind)] + [TRACE_SHAPE] * bool(trace)
    out = pl.pallas_call(
        functools.partial(half_kernel, half, bool(trace)),
        out_shape=shapes,
        in_specs=[SMEM, SMEM] + [FAR] * (LEFTS + 1) + [SMEM, VMEM] * bool(trace),
        out_specs=[VMEM] * len(shapes),
        scratch_shapes=BLOCKS,
        compiler_params=PARAMS,
        cost_estimate=cost(100_000_000, 15_000_000),
    )(info, todo, *lefts, right, *trace)
    return out if trace else out[0]


class Total:
    steps = (
        ("core", 2, 1),
        ("y", RING_Y, 1),
        ("y", RING_Y, 2),
        ("x_lo", 2, 1),
        ("x_hi", 2, 1),
    )

    def __init__(self, part):
        self.part, self.done = part, 0

    def advance(self, n):
        for axis, size, hop in self.steps[self.done : self.done + n]:
            self.part += lax.ppermute(self.part, axis, [(i, i ^ hop) for i in range(size)])
        self.done += n

    def finish(self):
        wide = jnp.pad(self.part, ((0, WIDE - 8), (0, 0)))
        planes = lax.all_gather(wide, "z", axis=0)
        return jnp.sum(planes[:, :8])


def per_device(p_values, p_where, p_count, h_values, h_where, h_count):
    z, x_lo, x_hi, y, core = (lax.axis_index(a) for a in AXES)
    row, col = z * 2 + x_lo, (x_hi * RING_Y + y) * 2 + core
    places, order, same = tile_table(x_hi * 2 + x_lo, y, core)
    flags = jnp.stack([row == col, z * 2 + 1 - x_lo == col, same])
    info = jnp.stack([places, order, jnp.pad(flags.astype(jnp.int32), (0, LEFTS - 3))]).astype(jnp.int32)

    p_meta = describe(p_where, p_count, row, col)
    h_meta = describe(h_where, h_count, row, col)
    h_pay = jnp.concatenate([h_values.reshape(BODY, BLK), h_meta])
    p_pay = jnp.concatenate([p_values.reshape(BODY, BLK), p_meta])
    h_line = lax.all_gather(h_pay, "z", axis=0, tiled=True)
    p_line = lax.all_gather(p_pay, "z", axis=0, tiled=True)
    partner_meta = lax.ppermute(p_meta, "x_lo", ring(2, 1))
    outs = jnp.concatenate([p_meta, partner_meta])
    p_tiles = spread(p_pay)

    other, todo, energy, out_slots = first_half(info, p_tiles, h_line, outs)
    came = lax.ppermute(other, "x_lo", ring(2, 1))
    own, energy = later_half(1, jnp.float32, info, todo, p_tiles, h_line, out_slots, energy)
    running = Total(energy)
    running.advance(2)
    came, running.part = lax.optimization_barrier((came, running.part))
    ph = (own + came.astype(jnp.float32)).astype(jnp.bfloat16)

    plans = []

    def beside(stage, *tiles):
        if stage == 2:
            plans.extend(plan_lists(info, p_tiles, p_line, outs))
            *tiles, plans[:] = lax.optimization_barrier((*tiles, plans))
            return tiles
        running.advance(stage + 1)
        *tiles, running.part = lax.optimization_barrier((*tiles, running.part))
        return tiles

    f_tiles = spread(ph, beside)
    other = later_half(0, jnp.bfloat16, info, plans[0], f_tiles, p_line)
    came = lax.ppermute(other, "x_lo", ring(2, 1))
    own = later_half(1, jnp.float32, info, plans[1], f_tiles, p_line)
    php = (own + came.astype(jnp.float32)).astype(jnp.bfloat16)
    return ph.reshape(CAP, BLK, BLK), php.reshape(CAP, BLK, BLK), running.finish()


def solution(mesh):
    torus = Mesh(mesh.devices.reshape(8, 2, 2, 4, 2), AXES)
    in_specs = (
        P(ROW, COL, None),
        P(ROW, COL),
        P(ROW, COL),
        P(ROW, COL, None),
        P(ROW, COL),
        P(ROW, COL),
    )
    out_specs = (P(ROW, COL, None), P(ROW, COL, None), P())
    return jax.shard_map(
        per_device, mesh=torus, in_specs=in_specs, out_specs=out_specs, check_vma=False
    )
```

time: 230 us -> 164 us (0.71)
  waiting for transfers between devices: 100 us -> 56 us
  local copies, waits for them, and re-layouts: 28.2 us -> 3.43 us
  Pallas kernels: 32.4 us -> 27.4 us
  other arithmetic: 6.81 us -> 11.7 us
  starting transfers between devices: 45.2 us -> 49.2 us
    unnamed x60 -> x54, local copies, waits for them, and re-layouts: 28.2 us -> 2.73 us
    ppermute x8 -> x5, waiting for transfers between devices: 25.2 us -> 9.32 us  [advance(): lax.ppermute(self.part, axis, [(i, i ^ hop) for i in range(size)])]
    ppermute x2, waiting for transfers between devices: 15.1 us -> 0.32 us  [spread(): near_up = lax.ppermute(near, 'y', ring(RING_Y, 1))]
    ppermute x2, waiting for transfers between devices: 15.6 us -> 2.39 us  [spread(): far = lax.ppermute(tile, IN_CHIP_X, first)]
    ppermute x2, waiting for transfers between devices: 0.01 us -> 11 us  [spread(): near = lax.ppermute(tile, IN_CHIP_X, second)]
    ppermute x2, waiting for transfers between devices: 8.95 us -> 0.52 us  [spread(): far_two = lax.ppermute(far_down, 'y', ring(RING_Y, -1))]
    ppermute x2, waiting for transfers between devices: 11.9 us -> 4.89 us  [spread(): near_two = lax.ppermute(near_up, 'y', ring(RING_Y, 1))]
    all_gather x0 -> x1, waiting for transfers between devices: none -> 6.07 us  [finish(): planes = lax.all_gather(wide, 'z', axis=0)]
  transfers between devices with their start and end apart: 45 -> 43, of which waited for: 23 -> 24; matrix products, arithmetic and copies ran while one was open for 1% -> 5% of each run, Pallas kernels for 7% -> 17%
where the time goes in v2:
time: 164 us; the launch traced here: 163 us
  waiting for transfers between devices  56 us (34%)
  starting transfers between devices  49.2 us (30%)
  Pallas kernels  27.4 us (17%)
  between operations  15.4 us (9%)
  other arithmetic  11.7 us (7%)
  local copies, waits for them, and re-layouts  3.43 us (2%)
    pallas_call x3, Pallas kernels, later_half(): pl.pallas_call(functools.partial(half_kernel, half, bool(trace)), out_sha...  15.1 us
    ppermute x2, waiting for transfers between devices, spread(): near = lax.ppermute(tile, IN_CHIP_X, second)  11 us
    ppermute x5, starting transfers between devices, advance(): lax.ppermute(self.part, axis, [(i, i ^ hop) for i in range(size)])  10.9 us
    ppermute x5, waiting for transfers between devices, advance(): lax.ppermute(self.part, axis, [(i, i ^ hop) for i in range(size)])  9.32 us
    pallas_call x1, Pallas kernels, first_half(): pl.pallas_call(first_kernel, out_shape=[jax.ShapeDtypeStruct((BODY, BLK),...  7.44 us
    all_gather x1, waiting for transfers between devices, finish(): planes = lax.all_gather(wide, 'z', axis=0)  6.07 us
    ppermute x2, starting transfers between devices, per_device(): came = lax.ppermute(other, 'x_lo', ring(2, 1))  6.06 us
    ppermute x2, waiting for transfers between devices, spread(): near_two = lax.ppermute(near_up, 'y', ring(RING_Y, 1))  4.89 us
  transfers between devices with their start and end apart: 43, of which 24 were waited for; matrix products, arithmetic and copies ran while one was open for 5% of the time, Pallas kernels for 17%

profile of v2, /device:TPU:2, one launch (start us, length us, event | category | flops | bytes accessed | tf_op | source)
XLA Modules:
  0.0 163.2 jit_solution(7774177053799861002)
XLA Ops:
  9.5 1.8 %pad_maximum_fusion.1 = bf16[1552,128]{1,0:T(8,128)(2,1)} fusion(bf16[16,128]{1,0:T(8,128)(2,1)S(1)} %broadcast_in_dim.92, bf16[1536,128]{1,0:T(8,128)(2,1)} %bitcast.38), kind=kLoop, calls=%fused_computation.3 | loop fusion | flops 794624 | bytes 794624 | tf_op jit(solution)/shard_map/concatenate | solution.py:371
  11.4 1.8 %pad_maximum_fusion = bf16[1552,128]{1,0:T(8,128)(2,1)} fusion(bf16[16,128]{1,0:T(8,128)(2,1)S(1)} %broadcast_in_dim.85, bf16[1536,128]{1,0:T(8,128)(2,1)} %bitcast.39), kind=kLoop, calls=%fused_computation.2 | loop fusion | flops 794624 | bytes 794624 | tf_op jit(solution)/shard_map/concatenate | solution.py:372
  13.2 1.9 %collective-permute-start = (bf16[1552,128]{1,0:T(8,128)(2,1)}, bf16[1552,128]{1,0:T(8,128)(2,1)S(1)}, u32[]{:S(2)}, u32[]{:S(2)}) collective-permute-start(bf16[1552,128]{1,0:T(8,128)(2,1)} %pad_maximum_fusion), channel_id=1, source_target_pairs={{1,24},{0,0},{16,1},{17,17},{9,16},{8,8},{24,9},{25,25},{3,26},{2,... | collective-permute-start | bytes 1191944 | tf_op jit(solution)/shard_map/ppermute | solution.py:80
  15.2 1.2 collective-permute-start.4
  16.4 8.9 %collective-permute-done.refs_0_ = bf16[1552,128]{1,0:T(8,128)(2,1)S(1)} collective-permute-done((bf16[1552,128]{1,0:T(8,128)(2,1)}, bf16[1552,128]{1,0:T(8,128)(2,1)S(1)}, u32[]{:S(2)}, u32[]{:S(2)}) %collective-permute-start) | collective-permute-done | bytes 397344 | tf_op jit(solution)/shard_map/ppermute | solution.py:80
  25.3 1.6 collective-permute-start.1
  26.8 1.7 %collective-permute-start.2 = (bf16[1552,128]{1,0:T(8,128)(2,1)S(1)}, bf16[1552,128]{1,0:T(8,128)(2,1)S(1)}, u32[]{:S(2)}, u32[]{:S(2)}) collective-permute-start(bf16[1552,128]{1,0:T(8,128)(2,1)S(1)} %collective-permute-done.refs_0_), channel_id=1, source_target_pairs={{0,6},{2,0},{4,2},{6,4},{1,7},{3,1},{5,3},{7,5},{8,14},{10,8},{12,... | collective-permute-start | bytes 1191944 | tf_op jit(solution)/shard_map/ppermute | solution.py:84
  28.5 2.3 %collective-permute-start.6 = (bf16[1552,128]{1,0:T(8,128)(2,1)S(1)}, bf16[1552,128]{1,0:T(8,128)(2,1)S(1)}, u32[]{:S(2)}, u32[]{:S(2)}) collective-permute-start(bf16[1552,128]{1,0:T(8,128)(2,1)S(1)} %collective-permute-done.4.refs_4_), channel_id=1, source_target_pairs={{0,6},{2,0},{4,2},{6,4},{1,7},{3,1},{5,3},{7,5},{8,14},{10,8},{12,... | collective-permute-start | bytes 1191944 | tf_op jit(solution)/shard_map/ppermute | solution.py:83
  30.8 1.9 %collective-permute-start.16 = (bf16[16,128]{1,0:T(8,128)(2,1)S(1)}, bf16[16,128]{1,0:T(8,128)(2,1)S(1)}, u32[]{:S(2)}, u32[]{:S(2)}) collective-permute-start(bf16[16,128]{1,0:T(8,128)(2,1)S(1)} %broadcast_in_dim.85), channel_id=1, source_target_pairs={{0,16},{16,0},{1,17},{17,1},{2,18},{18,2},{3,19},{19,3},{4,20},{20... | collective-permute-start | bytes 12296 | tf_op jit(solution)/shard_map/ppermute | solution.py:375
  32.7 1.7 %collective-permute-done.16 = bf16[16,128]{1,0:T(8,128)(2,1)S(1)} collective-permute-done((bf16[16,128]{1,0:T(8,128)(2,1)S(1)}, bf16[16,128]{1,0:T(8,128)(2,1)S(1)}, u32[]{:S(2)}, u32[]{:S(2)}) %collective-permute-start.16) | collective-permute-done | bytes 4128 | tf_op jit(solution)/shard_map/ppermute | solution.py:375
  34.9 3.4 %collective-permute-done.2.refs_2_ = bf16[1552,128]{1,0:T(8,128)(2,1)S(1)} collective-permute-done((bf16[1552,128]{1,0:T(8,128)(2,1)S(1)}, bf16[1552,128]{1,0:T(8,128)(2,1)S(1)}, u32[]{:S(2)}, u32[]{:S(2)}) %collective-permute-start.2) | collective-permute-done | bytes 397344 | tf_op jit(solution)/shard_map/ppermute | solution.py:84
  38.4 1.6 collective-permute-start.3
  40.0 3.7 %collective-permute-done.6.refs_6_ = bf16[1552,128]{1,0:T(8,128)(2,1)S(1)} collective-permute-done((bf16[1552,128]{1,0:T(8,128)(2,1)S(1)}, bf16[1552,128]{1,0:T(8,128)(2,1)S(1)}, u32[]{:S(2)}, u32[]{:S(2)}) %collective-permute-start.6) | collective-permute-done | bytes 397344 | tf_op jit(solution)/shard_map/ppermute | solution.py:83
  43.6 2.4 %collective-permute-start.7 = (bf16[1552,128]{1,0:T(8,128)(2,1)S(1)}, bf16[1552,128]{1,0:T(8,128)(2,1)}, u32[]{:S(2)}, u32[]{:S(2)}) collective-permute-start(bf16[1552,128]{1,0:T(8,128)(2,1)S(1)} %collective-permute-done.6.refs_6_), channel_id=1, source_target_pairs={{0,6},{2,0},{4,2},{6,4},{1,7},{3,1},{5,3},{7,5},{8,14},{10,8},{12,... | collective-permute-start | bytes 1191944 | tf_op jit(solution)/shard_map/ppermute | solution.py:88
  46.9 4.6 %collective-permute-done.3.refs_3_ = bf16[1552,128]{1,0:T(8,128)(2,1)} collective-permute-done((bf16[1552,128]{1,0:T(8,128)(2,1)S(1)}, bf16[1552,128]{1,0:T(8,128)(2,1)}, u32[]{:S(2)}, u32[]{:S(2)}) %collective-permute-start.3) | collective-permute-done | bytes 397344 | tf_op jit(solution)/shard_map/ppermute | solution.py:87
  56.1 3.6 %all-gather.5.cloned.1.call-done.refs_16_ = bf16[12416,128]{1,0:T(8,128)(2,1)} async-done(((bf16[1552,128]{1,0:T(8,128)(2,1)}), bf16[12416,128]{1,0:T(8,128)(2,1)}) %all-gather.5.cloned.1.call-update) | async-done | bytes 3178512 | tf_op jit(solution)/shard_map/all_gather | solution.py:373
  59.8 7.4 %shard_map.130 = (bf16[1536,128]{1,0:T(8,128)(2,1)}, s32[776]{0:T(1024)}, f32[8,128]{1,0:T(8,128)}, s32[8,128]{1,0:T(8,128)}) custom-call(s32[3,16]{1,0:T(4,128)} %pad_add_fusion.info, bf16[1552,128]{1,0:T(8,128)(2,1)} %copy-done, bf16[1552,128]{1,0:T(8,128)(2,1)} %copy-done.2, bf16[1552,128]{1,0:T(8,128)(2,1)} %copy-done.3, ...), custom_call_target="tpu_custom_call" | custom-call | flops 100000000 | bytes 20000000 | tf_op jit(solution)/shard_map/pallas_call | solution.py:314
  68.2 5.3 %shard_map.131 = (f32[1536,128]{1,0:T(8,128)}, f32[8,128]{1,0:T(8,128)}) custom-call(s32[3,16]{1,0:T(4,128)} %pad_add_fusion.info, s32[776]{0:T(1024)} %get-tuple-element.25.todo, bf16[1552,128]{1,0:T(8,128)(2,1)} %copy-done, bf16[1552,128]{1,0:T(8,128)(2,1)} %copy-done.2, bf16[1552,128]{1,0:T(8,128)(2,1)} %copy-done.3, ...), custom_call_target="tpu_custom_call" | custom-call | flops 100000000 | bytes 15000000 | tf_op jit(solution)/shard_map/pallas_call | solution.py:327
  73.5 1.2 collective-permute-start.18
  74.7 1.0 collective-permute-done.18
  76.4 2.6 %collective-permute-start.19 = (f32[8,128]{1,0:T(8,128)S(1)}, f32[8,128]{1,0:T(8,128)S(1)}, u32[]{:S(2)}, u32[]{:S(2)}) collective-permute-start(f32[8,128]{1,0:T(8,128)S(1)} %add.112), channel_id=1, source_target_pairs={{0,2},{2,0},{4,6},{6,4},{1,3},{3,1},{5,7},{7,5},{8,10},{10,8},{12,... | collective-permute-start | bytes 12296 | tf_op jit(solution)/shard_map/ppermute | solution.py:353
  79.0 1.6 collective-permute-done.19
  80.5 1.2 add_convert_fusion.1
  81.8 1.4 collective-permute-start.20
  83.2 1.9 %collective-permute-start.21 = (bf16[1536,128]{1,0:T(8,128)(2,1)S(1)}, bf16[1536,128]{1,0:T(8,128)(2,1)S(1)}, u32[]{:S(2)}, u32[]{:S(2)}) collective-permute-start(bf16[1536,128]{1,0:T(8,128)(2,1)S(1)} %add_convert_fusion.1), channel_id=1, source_target_pairs={{1,24},{0,0},{16,1},{17,17},{9,16},{8,8},{24,9},{25,25},{3,26},{2,... | collective-permute-start | bytes 1179656 | tf_op jit(solution)/shard_map/ppermute | solution.py:80
  85.1 3.5 %collective-permute-start.22 = (f32[8,128]{1,0:T(8,128)S(1)}, f32[8,128]{1,0:T(8,128)S(1)}, u32[]{:S(2)}, u32[]{:S(2)}) collective-permute-start(f32[8,128]{1,0:T(8,128)S(1)} %add.113), channel_id=1, source_target_pairs={{0,4},{2,6},{4,0},{6,2},{1,5},{3,7},{5,1},{7,3},{8,12},{10,14},{12... | collective-permute-start | bytes 12296 | tf_op jit(solution)/shard_map/ppermute | solution.py:353
  88.6 1.7 %collective-permute-done.22 = f32[8,128]{1,0:T(8,128)S(1)} collective-permute-done((f32[8,128]{1,0:T(8,128)S(1)}, f32[8,128]{1,0:T(8,128)S(1)}, u32[]{:S(2)}, u32[]{:S(2)}) %collective-permute-start.22) | collective-permute-done | bytes 4128 | tf_op jit(solution)/shard_map/ppermute | solution.py:353
  90.3 2.4 %collective-permute-done.20.refs_4_ = bf16[1536,128]{1,0:T(8,128)(2,1)S(1)} collective-permute-done((bf16[1536,128]{1,0:T(8,128)(2,1)S(1)}, bf16[1536,128]{1,0:T(8,128)(2,1)S(1)}, u32[]{:S(2)}, u32[]{:S(2)}) %collective-permute-start.20) | collective-permute-done | bytes 393248 | tf_op jit(solution)/shard_map/ppermute | solution.py:79
  92.7 2.1 %collective-permute-done.21.refs_0_ = bf16[1536,128]{1,0:T(8,128)(2,1)S(1)} collective-permute-done((bf16[1536,128]{1,0:T(8,128)(2,1)S(1)}, bf16[1536,128]{1,0:T(8,128)(2,1)S(1)}, u32[]{:S(2)}, u32[]{:S(2)}) %collective-permute-start.21) | collective-permute-done | bytes 393248 | tf_op jit(solution)/shard_map/ppermute | solution.py:80
  94.8 2.0 %collective-permute-start.23 = (bf16[1536,128]{1,0:T(8,128)(2,1)S(1)}, bf16[1536,128]{1,0:T(8,128)(2,1)S(1)}, u32[]{:S(2)}, u32[]{:S(2)}) collective-permute-start(bf16[1536,128]{1,0:T(8,128)(2,1)S(1)} %collective-permute-done.21.refs_0_), channel_id=1, source_target_pairs={{0,2},{2,4},{4,6},{6,0},{1,3},{3,5},{5,7},{7,1},{8,10},{10,12},{12... | collective-permute-start | bytes 1179656 | tf_op jit(solution)/shard_map/ppermute | solution.py:82
  96.8 1.2 collective-permute-start.24
  98.8 2.4 %collective-permute-start.26 = (bf16[1536,128]{1,0:T(8,128)(2,1)S(1)}, bf16[1536,128]{1,0:T(8,128)(2,1)S(1)}, u32[]{:S(2)}, u32[]{:S(2)}) collective-permute-start(bf16[1536,128]{1,0:T(8,128)(2,1)S(1)} %collective-permute-done.20.refs_4_), channel_id=1, source_target_pairs={{0,6},{2,0},{4,2},{6,4},{1,7},{3,1},{5,3},{7,5},{8,14},{10,8},{12,... | collective-permute-start | bytes 1179656 | tf_op jit(solution)/shard_map/ppermute | solution.py:83
  101.3 1.4 collective-permute-start.27
  102.6 2.2 %collective-permute-done.27 = f32[8,128]{1,0:T(8,128)S(1)} collective-permute-done((f32[8,128]{1,0:T(8,128)S(1)}, f32[8,128]{1,0:T(8,128)S(1)}, u32[]{:S(2)}, u32[]{:S(2)}) %collective-permute-start.27) | collective-permute-done | bytes 4128 | tf_op jit(solution)/shard_map/ppermute | solution.py:353
  104.9 2.3 %collective-permute-start.28 = (f32[8,128]{1,0:T(8,128)S(1)}, f32[8,128]{1,0:T(8,128)S(1)}, u32[]{:S(2)}, u32[]{:S(2)}) collective-permute-start(f32[8,128]{1,0:T(8,128)S(1)} %add.116), channel_id=1, source_target_pairs={{0,8},{8,0},{1,9},{9,1},{2,10},{10,2},{3,11},{11,3},{4,12},{12,4},... | collective-permute-start | bytes 12296 | tf_op jit(solution)/shard_map/ppermute | solution.py:353
  107.2 2.8 %collective-permute-done.28 = f32[8,128]{1,0:T(8,128)S(1)} collective-permute-done((f32[8,128]{1,0:T(8,128)S(1)}, f32[8,128]{1,0:T(8,128)S(1)}, u32[]{:S(2)}, u32[]{:S(2)}) %collective-permute-start.28) | collective-permute-done | bytes 4128 | tf_op jit(solution)/shard_map/ppermute | solution.py:353
  110.0 1.6 collective-permute-done.25.refs_5_
  112.6 1.7 %collective-permute-start.29 = (bf16[1536,128]{1,0:T(8,128)(2,1)S(1)}, bf16[1536,128]{1,0:T(8,128)(2,1)S(1)}, u32[]{:S(2)}, u32[]{:S(2)}) collective-permute-start(bf16[1536,128]{1,0:T(8,128)(2,1)S(1)} %collective-permute-done.23.refs_1_), channel_id=1, source_target_pairs={{0,2},{2,4},{4,6},{6,0},{1,3},{3,5},{5,7},{7,1},{8,10},{10,12},{12... | collective-permute-start | bytes 1179656 | tf_op jit(solution)/shard_map/ppermute | solution.py:87
  114.3 1.6 collective-permute-start.30
  116.4 4.9 %shard_map.132 = (s32[776]{0:T(1024)}, s32[776]{0:T(1024)}) custom-call(s32[3,16]{1,0:T(4,128)} %pad_add_fusion.info, bf16[1552,128]{1,0:T(8,128)(2,1)} %copy-done, bf16[1552,128]{1,0:T(8,128)(2,1)} %copy-done.2, bf16[1552,128]{1,0:T(8,128)(2,1)} %copy-done.3, bf16[1552,128]{1,0:T(8,128)(2,1)} %collective-permute-done.3.refs_3_, ...), custom_call_target="tpu_custom_call" | custom-call | flops 1000000 | bytes 10000000 | tf_op jit(solution)/shard_map/pallas_call | solution.py:302
  121.7 1.4 collective-permute-start.37
  127.6 4.8 %shard_map.134 = bf16[1536,128]{1,0:T(8,128)(2,1)} custom-call(s32[3,16]{1,0:T(4,128)} %pad_add_fusion.info, s32[776]{0:T(1024)} %get-tuple-element.45.todo, bf16[1536,128]{1,0:T(8,128)(2,1)} %copy-done.13, bf16[1536,128]{1,0:T(8,128)(2,1)} %copy-done.14, bf16[1536,128]{1,0:T(8,128)(2,1)} %copy-done.15, bf16[1536,128]{1,0:T(8,128)(2,1)} %copy-done.18, ...), custom_call_target="tpu_custom_call" | custom-call | flops 100000000 | bytes 15000000 | tf_op jit(solution)/shard_map/pallas_call | solution.py:327
  132.4 5.1 %collective-permute-start.39 = (bf16[1536,128]{1,0:T(8,128)(2,1)}, bf16[1536,128]{1,0:T(8,128)(2,1)S(1)}, u32[]{:S(2)}, u32[]{:S(2)}) collective-permute-start(bf16[1536,128]{1,0:T(8,128)(2,1)} %shard_map.134), channel_id=1, source_target_pairs={{0,16},{16,0},{1,17},{17,1},{2,18},{18,2},{3,19},{19,3},{4,20},{20... | collective-permute-start | bytes 1179656 | tf_op jit(solution)/shard_map/ppermute | solution.py:400
  137.5 5.0 %shard_map.133 = f32[1536,128]{1,0:T(8,128)} custom-call(s32[3,16]{1,0:T(4,128)} %pad_add_fusion.info, s32[776]{0:T(1024)} %get-tuple-element.40.todo, bf16[1536,128]{1,0:T(8,128)(2,1)} %copy-done.13, bf16[1536,128]{1,0:T(8,128)(2,1)} %copy-done.14, bf16[1536,128]{1,0:T(8,128)(2,1)} %copy-done.15, bf16[1536,128]{1,0:T(8,128)(2,1)} %copy-done.18, ...), custom_call_target="tpu_custom_call" | custom-call | flops 100000000 | bytes 15000000 | tf_op jit(solution)/shard_map/pallas_call | solution.py:327
  142.5 4.8 %collective-permute-done.39 = bf16[1536,128]{1,0:T(8,128)(2,1)S(1)} collective-permute-done((bf16[1536,128]{1,0:T(8,128)(2,1)}, bf16[1536,128]{1,0:T(8,128)(2,1)S(1)}, u32[]{:S(2)}, u32[]{:S(2)}) %collective-permute-start.39) | collective-permute-done | bytes 393248 | tf_op jit(solution)/shard_map/ppermute | solution.py:400
  147.3 2.0 %add_convert_fusion = bf16[1536,128]{1,0:T(8,128)(2,1)} fusion(f32[1536,128]{1,0:T(8,128)} %shard_map.133, bf16[1536,128]{1,0:T(8,128)(2,1)S(1)} %collective-permute-done.39), kind=kLoop, calls=%fused_computation | loop fusion | flops 589824 | bytes 1572864 | tf_op jit(solution)/shard_map/convert_element_type | solution.py:402
  149.2 6.1 %all-gather.9.cloned.1.call-done = f32[2048,128]{1,0:T(8,128)} async-done(((f32[256,128]{1,0:T(8,128)}), f32[2048,128]{1,0:T(8,128)}) %all-gather.9.cloned.1.call-update) | async-done | bytes 1048592 | tf_op jit(solution)/shard_map/all_gather | solution.py:358
  155.3 1.4 slice_reduce_fusion
  (128 shorter events, 15.9 us)
Async XLA Ops:
  7.2 52.5 %all-gather.5.cloned.1.call-start = ((), (), s32[]{:S(2)}) async-start(), calls=%async_computation | async-start | bytes 3575808 | tf_op jit(solution)/shard_map/all_gather | solution.py:373
  11.3 105.1 %all-gather.7.cloned.1.call-start = ((), (), s32[]{:S(2)}) async-start(), calls=%async_computation.1 | async-start | bytes 3575808 | tf_op jit(solution)/shard_map/all_gather | solution.py:374
  13.2 142.1 %all-gather.9.cloned.1.call-start = ((), (), s32[]{:S(2)}) async-start(), calls=%async_computation.2 | async-start | bytes 1179648 | tf_op jit(solution)/shard_map/all_gather | solution.py:358
  13.2 12.0 %collective-permute-start = (bf16[1552,128]{1,0:T(8,128)(2,1)}, bf16[1552,128]{1,0:T(8,128)(2,1)S(1)}, u32[]{:S(2)}, u32[]{:S(2)}) collective-permute-start(bf16[1552,128]{1,0:T(8,128)(2,1)} %pad_maximum_fusion), channel_id=1, source_target_pairs={{1,24},{0,0},{16,1},{17,17},{9,16},{8,8},{24,9},{25,25},{3,26},{2,... | collective-permute-start | bytes 1191944 | tf_op jit(solution)/shard_map/ppermute | solution.py:80
  15.2 13.3 %collective-permute-start.4 = (bf16[1552,128]{1,0:T(8,128)(2,1)}, bf16[1552,128]{1,0:T(8,128)(2,1)S(1)}, u32[]{:S(2)}, u32[]{:S(2)}) collective-permute-start(bf16[1552,128]{1,0:T(8,128)(2,1)} %pad_maximum_fusion), channel_id=1, source_target_pairs={{1,17},{0,9},{16,8},{17,24},{9,25},{8,1},{24,0},{25,16},{3,19},{2,... | collective-permute-start | bytes 1191944 | tf_op jit(solution)/shard_map/ppermute | solution.py:79
  25.3 34.4 %copy-start = (bf16[1552,128]{1,0:T(8,128)(2,1)}, bf16[1552,128]{1,0:T(8,128)(2,1)S(1)}, u32[]{:S(2)}) copy-start(bf16[1552,128]{1,0:T(8,128)(2,1)S(1)} %collective-permute-done.refs_0_) | copy-start | bytes 1191940
  25.3 9.5 %collective-permute-start.1 = (bf16[1552,128]{1,0:T(8,128)(2,1)S(1)}, bf16[1552,128]{1,0:T(8,128)(2,1)S(1)}, u32[]{:S(2)}, u32[]{:S(2)}) collective-permute-start(bf16[1552,128]{1,0:T(8,128)(2,1)S(1)} %collective-permute-done.refs_0_), channel_id=1, source_target_pairs={{0,2},{2,4},{4,6},{6,0},{1,3},{3,5},{5,7},{7,1},{8,10},{10,12},{12... | collective-permute-start | bytes 1191944 | tf_op jit(solution)/shard_map/ppermute | solution.py:82
  26.8 11.5 %collective-permute-start.2 = (bf16[1552,128]{1,0:T(8,128)(2,1)S(1)}, bf16[1552,128]{1,0:T(8,128)(2,1)S(1)}, u32[]{:S(2)}, u32[]{:S(2)}) collective-permute-start(bf16[1552,128]{1,0:T(8,128)(2,1)S(1)} %collective-permute-done.refs_0_), channel_id=1, source_target_pairs={{0,6},{2,0},{4,2},{6,4},{1,7},{3,1},{5,3},{7,5},{8,14},{10,8},{12,... | collective-permute-start | bytes 1191944 | tf_op jit(solution)/shard_map/ppermute | solution.py:84
  28.5 31.2 %copy-start.1 = (bf16[1552,128]{1,0:T(8,128)(2,1)}, bf16[1552,128]{1,0:T(8,128)(2,1)S(1)}, u32[]{:S(2)}) copy-start(bf16[1552,128]{1,0:T(8,128)(2,1)S(1)} %collective-permute-done.4.refs_4_) | copy-start | bytes 1191940
  28.5 15.1 %collective-permute-start.6 = (bf16[1552,128]{1,0:T(8,128)(2,1)S(1)}, bf16[1552,128]{1,0:T(8,128)(2,1)S(1)}, u32[]{:S(2)}, u32[]{:S(2)}) collective-permute-start(bf16[1552,128]{1,0:T(8,128)(2,1)S(1)} %collective-permute-done.4.refs_4_), channel_id=1, source_target_pairs={{0,6},{2,0},{4,2},{6,4},{1,7},{3,1},{5,3},{7,5},{8,14},{10,8},{12,... | collective-permute-start | bytes 1191944 | tf_op jit(solution)/shard_map/ppermute | solution.py:83
  30.8 15.2 %collective-permute-start.5 = (bf16[1552,128]{1,0:T(8,128)(2,1)S(1)}, bf16[1552,128]{1,0:T(8,128)(2,1)S(1)}, u32[]{:S(2)}, u32[]{:S(2)}) collective-permute-start(bf16[1552,128]{1,0:T(8,128)(2,1)S(1)} %collective-permute-done.4.refs_4_), channel_id=1, source_target_pairs={{0,2},{2,4},{4,6},{6,0},{1,3},{3,5},{5,7},{7,1},{8,10},{10,12},{12... | collective-permute-start | bytes 1191944 | tf_op jit(solution)/shard_map/ppermute | solution.py:85
  30.8 3.6 %collective-permute-start.16 = (bf16[16,128]{1,0:T(8,128)(2,1)S(1)}, bf16[16,128]{1,0:T(8,128)(2,1)S(1)}, u32[]{:S(2)}, u32[]{:S(2)}) collective-permute-start(bf16[16,128]{1,0:T(8,128)(2,1)S(1)} %broadcast_in_dim.85), channel_id=1, source_target_pairs={{0,16},{16,0},{1,17},{17,1},{2,18},{18,2},{3,19},{19,3},{4,20},{20... | collective-permute-start | bytes 12296 | tf_op jit(solution)/shard_map/ppermute | solution.py:375
  34.4 11.8 %collective-permute-start.8 = (bf16[1552,128]{1,0:T(8,128)(2,1)S(1)}, bf16[1552,128]{1,0:T(8,128)(2,1)S(1)}, u32[]{:S(2)}, u32[]{:S(2)}) collective-permute-start(bf16[1552,128]{1,0:T(8,128)(2,1)S(1)} %collective-permute-done.refs_0_), channel_id=1, source_target_pairs={{0,1},{1,0},{2,3},{3,2},{4,5},{5,4},{6,7},{7,6},{8,9},{9,8},{10,11... | collective-permute-start | bytes 1191944 | tf_op jit(solution)/shard_map/ppermute | solution.py:91
  34.7 12.0 %collective-permute-start.12 = (bf16[1552,128]{1,0:T(8,128)(2,1)S(1)}, bf16[1552,128]{1,0:T(8,128)(2,1)S(1)}, u32[]{:S(2)}, u32[]{:S(2)}) collective-permute-start(bf16[1552,128]{1,0:T(8,128)(2,1)S(1)} %collective-permute-done.4.refs_4_), channel_id=1, source_target_pairs={{0,1},{1,0},{2,3},{3,2},{4,5},{5,4},{6,7},{7,6},{8,9},{9,8},{10,11... | collective-permute-start | bytes 1191944 | tf_op jit(solution)/shard_map/ppermute | solution.py:91
  38.4 13.0 %collective-permute-start.3 = (bf16[1552,128]{1,0:T(8,128)(2,1)S(1)}, bf16[1552,128]{1,0:T(8,128)(2,1)}, u32[]{:S(2)}, u32[]{:S(2)}) collective-permute-start(bf16[1552,128]{1,0:T(8,128)(2,1)S(1)} %collective-permute-done.1.refs_1_), channel_id=1, source_target_pairs={{0,2},{2,4},{4,6},{6,0},{1,3},{3,5},{5,7},{7,1},{8,10},{10,12},{12... | collective-permute-start | bytes 1191944 | tf_op jit(solution)/shard_map/ppermute | solution.py:87
  43.6 8.3 %collective-permute-start.7 = (bf16[1552,128]{1,0:T(8,128)(2,1)S(1)}, bf16[1552,128]{1,0:T(8,128)(2,1)}, u32[]{:S(2)}, u32[]{:S(2)}) collective-permute-start(bf16[1552,128]{1,0:T(8,128)(2,1)S(1)} %collective-permute-done.6.refs_6_), channel_id=1, source_target_pairs={{0,6},{2,0},{4,2},{6,4},{1,7},{3,1},{5,3},{7,5},{8,14},{10,8},{12,... | collective-permute-start | bytes 1191944 | tf_op jit(solution)/shard_map/ppermute | solution.py:88
  46.1 5.9 %collective-permute-start.9 = (bf16[1552,128]{1,0:T(8,128)(2,1)S(1)}, bf16[1552,128]{1,0:T(8,128)(2,1)}, u32[]{:S(2)}, u32[]{:S(2)}) collective-permute-start(bf16[1552,128]{1,0:T(8,128)(2,1)S(1)} %collective-permute-done.1.refs_1_), channel_id=1, source_target_pairs={{0,1},{1,0},{2,3},{3,2},{4,5},{5,4},{6,7},{7,6},{8,9},{9,8},{10,11... | collective-permute-start | bytes 1191944 | tf_op jit(solution)/shard_map/ppermute | solution.py:91
  46.2 8.2 %collective-permute-start.14 = (bf16[1552,128]{1,0:T(8,128)(2,1)S(1)}, bf16[1552,128]{1,0:T(8,128)(2,1)S(1)}, u32[]{:S(2)}, u32[]{:S(2)}) collective-permute-start(bf16[1552,128]{1,0:T(8,128)(2,1)S(1)} %collective-permute-done.6.refs_6_), channel_id=1, source_target_pairs={{0,1},{1,0},{2,3},{3,2},{4,5},{5,4},{6,7},{7,6},{8,9},{9,8},{10,11... | collective-permute-start | bytes 1191944 | tf_op jit(solution)/shard_map/ppermute | solution.py:91
  46.8 7.6 %collective-permute-start.10 = (bf16[1552,128]{1,0:T(8,128)(2,1)S(1)}, bf16[1552,128]{1,0:T(8,128)(2,1)S(1)}, u32[]{:S(2)}, u32[]{:S(2)}) collective-permute-start(bf16[1552,128]{1,0:T(8,128)(2,1)S(1)} %collective-permute-done.2.refs_2_), channel_id=1, source_target_pairs={{0,1},{1,0},{2,3},{3,2},{4,5},{5,4},{6,7},{7,6},{8,9},{9,8},{10,11... | collective-permute-start | bytes 1191944 | tf_op jit(solution)/shard_map/ppermute | solution.py:91
  51.4 2.9 %collective-permute-start.13 = (bf16[1552,128]{1,0:T(8,128)(2,1)S(1)}, bf16[1552,128]{1,0:T(8,128)(2,1)S(1)}, u32[]{:S(2)}, u32[]{:S(2)}) collective-permute-start(bf16[1552,128]{1,0:T(8,128)(2,1)S(1)} %collective-permute-done.5.refs_5_), channel_id=1, source_target_pairs={{0,1},{1,0},{2,3},{3,2},{4,5},{5,4},{6,7},{7,6},{8,9},{9,8},{10,11... | collective-permute-start | bytes 1191944 | tf_op jit(solution)/shard_map/ppermute | solution.py:91
  52.0 3.2 %collective-permute-start.11 = (bf16[1552,128]{1,0:T(8,128)(2,1)}, bf16[1552,128]{1,0:T(8,128)(2,1)S(1)}, u32[]{:S(2)}, u32[]{:S(2)}) collective-permute-start(bf16[1552,128]{1,0:T(8,128)(2,1)} %collective-permute-done.3.refs_3_), channel_id=1, source_target_pairs={{0,1},{1,0},{2,3},{3,2},{4,5},{5,4},{6,7},{7,6},{8,9},{9,8},{10,11... | collective-permute-start | bytes 1191944 | tf_op jit(solution)/shard_map/ppermute | solution.py:91
  52.0 4.2 %collective-permute-start.15 = (bf16[1552,128]{1,0:T(8,128)(2,1)}, bf16[1552,128]{1,0:T(8,128)(2,1)}, u32[]{:S(2)}, u32[]{:S(2)}) collective-permute-start(bf16[1552,128]{1,0:T(8,128)(2,1)} %collective-permute-done.7.refs_7_), channel_id=1, source_target_pairs={{0,1},{1,0},{2,3},{3,2},{4,5},{5,4},{6,7},{7,6},{8,9},{9,8},{10,11... | collective-permute-start | bytes 1191944 | tf_op jit(solution)/shard_map/ppermute | solution.py:91
  67.2 13.3 %collective-permute-start.17 = (bf16[1536,128]{1,0:T(8,128)(2,1)}, bf16[1536,128]{1,0:T(8,128)(2,1)S(1)}, u32[]{:S(2)}, u32[]{:S(2)}) collective-permute-start(bf16[1536,128]{1,0:T(8,128)(2,1)} %get-tuple-element.29), channel_id=1, source_target_pairs={{0,16},{16,0},{1,17},{17,1},{2,18},{18,2},{3,19},{19,3},{4,20},{20... | collective-permute-start | bytes 1179656 | tf_op jit(solution)/shard_map/ppermute | solution.py:380
  73.5 2.2 %collective-permute-start.18 = (f32[8,128]{1,0:T(8,128)}, f32[8,128]{1,0:T(8,128)S(1)}, u32[]{:S(2)}, u32[]{:S(2)}) collective-permute-start(f32[8,128]{1,0:T(8,128)} %get-tuple-element.30), channel_id=1, source_target_pairs={{0,1},{1,0},{2,3},{3,2},{4,5},{5,4},{6,7},{7,6},{8,9},{9,8},{10,11... | collective-permute-start | bytes 12296 | tf_op jit(solution)/shard_map/ppermute | solution.py:353
  76.4 4.1 %collective-permute-start.19 = (f32[8,128]{1,0:T(8,128)S(1)}, f32[8,128]{1,0:T(8,128)S(1)}, u32[]{:S(2)}, u32[]{:S(2)}) collective-permute-start(f32[8,128]{1,0:T(8,128)S(1)} %add.112), channel_id=1, source_target_pairs={{0,2},{2,0},{4,6},{6,4},{1,3},{3,1},{5,7},{7,5},{8,10},{10,8},{12,... | collective-permute-start | bytes 12296 | tf_op jit(solution)/shard_map/ppermute | solution.py:353
  81.8 30.1 %copy-start.26 = (bf16[1536,128]{1,0:T(8,128)(2,1)}, bf16[1536,128]{1,0:T(8,128)(2,1)S(1)}, u32[]{:S(2)}) copy-start(bf16[1536,128]{1,0:T(8,128)(2,1)S(1)} %add_convert_fusion.1) | copy-start | bytes 1179652
  81.8 10.9 %collective-permute-start.20 = (bf16[1536,128]{1,0:T(8,128)(2,1)S(1)}, bf16[1536,128]{1,0:T(8,128)(2,1)S(1)}, u32[]{:S(2)}, u32[]{:S(2)}) collective-permute-start(bf16[1536,128]{1,0:T(8,128)(2,1)S(1)} %add_convert_fusion.1), channel_id=1, source_target_pairs={{1,17},{0,9},{16,8},{17,24},{9,25},{8,1},{24,0},{25,16},{3,19},{2,... | collective-permute-start | bytes 1179656 | tf_op jit(solution)/shard_map/ppermute | solution.py:79
  83.2 11.6 %collective-permute-start.21 = (bf16[1536,128]{1,0:T(8,128)(2,1)S(1)}, bf16[1536,128]{1,0:T(8,128)(2,1)S(1)}, u32[]{:S(2)}, u32[]{:S(2)}) collective-permute-start(bf16[1536,128]{1,0:T(8,128)(2,1)S(1)} %add_convert_fusion.1), channel_id=1, source_target_pairs={{1,24},{0,0},{16,1},{17,17},{9,16},{8,8},{24,9},{25,25},{3,26},{2,... | collective-permute-start | bytes 1179656 | tf_op jit(solution)/shard_map/ppermute | solution.py:80
  85.1 5.2 %collective-permute-start.22 = (f32[8,128]{1,0:T(8,128)S(1)}, f32[8,128]{1,0:T(8,128)S(1)}, u32[]{:S(2)}, u32[]{:S(2)}) collective-permute-start(f32[8,128]{1,0:T(8,128)S(1)} %add.113), channel_id=1, source_target_pairs={{0,4},{2,6},{4,0},{6,2},{1,5},{3,7},{5,1},{7,3},{8,12},{10,14},{12... | collective-permute-start | bytes 12296 | tf_op jit(solution)/shard_map/ppermute | solution.py:353
  92.7 28.6 %copy-start.12 = (bf16[1536,128]{1,0:T(8,128)(2,1)}, bf16[1536,128]{1,0:T(8,128)(2,1)S(1)}, u32[]{:S(2)}) copy-start(bf16[1536,128]{1,0:T(8,128)(2,1)S(1)} %collective-permute-done.20.refs_4_) | copy-start | bytes 1179652
  94.8 26.6 %copy-start.13 = (bf16[1536,128]{1,0:T(8,128)(2,1)}, bf16[1536,128]{1,0:T(8,128)(2,1)S(1)}, u32[]{:S(2)}) copy-start(bf16[1536,128]{1,0:T(8,128)(2,1)S(1)} %collective-permute-done.21.refs_0_) | copy-start | bytes 1179652
  94.8 15.2 %collective-permute-start.23 = (bf16[1536,128]{1,0:T(8,128)(2,1)S(1)}, bf16[1536,128]{1,0:T(8,128)(2,1)S(1)}, u32[]{:S(2)}, u32[]{:S(2)}) collective-permute-start(bf16[1536,128]{1,0:T(8,128)(2,1)S(1)} %collective-permute-done.21.refs_0_), channel_id=1, source_target_pairs={{0,2},{2,4},{4,6},{6,0},{1,3},{3,5},{5,7},{7,1},{8,10},{10,12},{12... | collective-permute-start | bytes 1179656 | tf_op jit(solution)/shard_map/ppermute | solution.py:82
  96.8 13.2 %collective-permute-start.24 = (bf16[1536,128]{1,0:T(8,128)(2,1)S(1)}, bf16[1536,128]{1,0:T(8,128)(2,1)S(1)}, u32[]{:S(2)}, u32[]{:S(2)}) collective-permute-start(bf16[1536,128]{1,0:T(8,128)(2,1)S(1)} %collective-permute-done.21.refs_0_), channel_id=1, source_target_pairs={{0,6},{2,0},{4,2},{6,4},{1,7},{3,1},{5,3},{7,5},{8,14},{10,8},{12,... | collective-permute-start | bytes 1179656 | tf_op jit(solution)/shard_map/ppermute | solution.py:84
  98.0 13.6 %collective-permute-start.25 = (bf16[1536,128]{1,0:T(8,128)(2,1)S(1)}, bf16[1536,128]{1,0:T(8,128)(2,1)S(1)}, u32[]{:S(2)}, u32[]{:S(2)}) collective-permute-start(bf16[1536,128]{1,0:T(8,128)(2,1)S(1)} %collective-permute-done.20.refs_4_), channel_id=1, source_target_pairs={{0,2},{2,4},{4,6},{6,0},{1,3},{3,5},{5,7},{7,1},{8,10},{10,12},{12... | collective-permute-start | bytes 1179656 | tf_op jit(solution)/shard_map/ppermute | solution.py:85
  98.8 13.0 %collective-permute-start.26 = (bf16[1536,128]{1,0:T(8,128)(2,1)S(1)}, bf16[1536,128]{1,0:T(8,128)(2,1)S(1)}, u32[]{:S(2)}, u32[]{:S(2)}) collective-permute-start(bf16[1536,128]{1,0:T(8,128)(2,1)S(1)} %collective-permute-done.20.refs_4_), channel_id=1, source_target_pairs={{0,6},{2,0},{4,2},{6,4},{1,7},{3,1},{5,3},{7,5},{8,14},{10,8},{12,... | collective-permute-start | bytes 1179656 | tf_op jit(solution)/shard_map/ppermute | solution.py:83
  101.3 3.6 %collective-permute-start.27 = (f32[8,128]{1,0:T(8,128)S(1)}, f32[8,128]{1,0:T(8,128)S(1)}, u32[]{:S(2)}, u32[]{:S(2)}) collective-permute-start(f32[8,128]{1,0:T(8,128)S(1)} %add.115), channel_id=1, source_target_pairs={{0,16},{16,0},{1,17},{17,1},{2,18},{18,2},{3,19},{19,3},{4,20},{20... | collective-permute-start | bytes 12296 | tf_op jit(solution)/shard_map/ppermute | solution.py:353
  104.9 5.1 %collective-permute-start.28 = (f32[8,128]{1,0:T(8,128)S(1)}, f32[8,128]{1,0:T(8,128)S(1)}, u32[]{:S(2)}, u32[]{:S(2)}) collective-permute-start(f32[8,128]{1,0:T(8,128)S(1)} %add.116), channel_id=1, source_target_pairs={{0,8},{8,0},{1,9},{9,1},{2,10},{10,2},{3,11},{11,3},{4,12},{12,4},... | collective-permute-start | bytes 12296 | tf_op jit(solution)/shard_map/ppermute | solution.py:353
  112.6 9.1 %collective-permute-start.29 = (bf16[1536,128]{1,0:T(8,128)(2,1)S(1)}, bf16[1536,128]{1,0:T(8,128)(2,1)S(1)}, u32[]{:S(2)}, u32[]{:S(2)}) collective-permute-start(bf16[1536,128]{1,0:T(8,128)(2,1)S(1)} %collective-permute-done.23.refs_1_), channel_id=1, source_target_pairs={{0,2},{2,4},{4,6},{6,0},{1,3},{3,5},{5,7},{7,1},{8,10},{10,12},{12... | collective-permute-start | bytes 1179656 | tf_op jit(solution)/shard_map/ppermute | solution.py:87
  114.3 8.7 %collective-permute-start.30 = (bf16[1536,128]{1,0:T(8,128)(2,1)S(1)}, bf16[1536,128]{1,0:T(8,128)(2,1)S(1)}, u32[]{:S(2)}, u32[]{:S(2)}) collective-permute-start(bf16[1536,128]{1,0:T(8,128)(2,1)S(1)} %collective-permute-done.26.refs_6_), channel_id=1, source_target_pairs={{0,6},{2,0},{4,2},{6,4},{1,7},{3,1},{5,3},{7,5},{8,14},{10,8},{12,... | collective-permute-start | bytes 1179656 | tf_op jit(solution)/shard_map/ppermute | solution.py:88
  115.9 7.2 %collective-permute-start.31 = (bf16[1536,128]{1,0:T(8,128)(2,1)S(1)}, bf16[1536,128]{1,0:T(8,128)(2,1)S(1)}, u32[]{:S(2)}, u32[]{:S(2)}) collective-permute-start(bf16[1536,128]{1,0:T(8,128)(2,1)S(1)} %collective-permute-done.21.refs_0_), channel_id=1, source_target_pairs={{0,1},{1,0},{2,3},{3,2},{4,5},{5,4},{6,7},{7,6},{8,9},{9,8},{10,11... | collective-permute-start | bytes 1179656 | tf_op jit(solution)/shard_map/ppermute | solution.py:91
  115.9 7.8 %collective-permute-start.35 = (bf16[1536,128]{1,0:T(8,128)(2,1)S(1)}, bf16[1536,128]{1,0:T(8,128)(2,1)}, u32[]{:S(2)}, u32[]{:S(2)}) collective-permute-start(bf16[1536,128]{1,0:T(8,128)(2,1)S(1)} %collective-permute-done.20.refs_4_), channel_id=1, source_target_pairs={{0,1},{1,0},{2,3},{3,2},{4,5},{5,4},{6,7},{7,6},{8,9},{9,8},{10,11... | collective-permute-start | bytes 1179656 | tf_op jit(solution)/shard_map/ppermute | solution.py:91
  116.4 7.4 %collective-permute-start.32 = (bf16[1536,128]{1,0:T(8,128)(2,1)S(1)}, bf16[1536,128]{1,0:T(8,128)(2,1)}, u32[]{:S(2)}, u32[]{:S(2)}) collective-permute-start(bf16[1536,128]{1,0:T(8,128)(2,1)S(1)} %collective-permute-done.23.refs_1_), channel_id=1, source_target_pairs={{0,1},{1,0},{2,3},{3,2},{4,5},{5,4},{6,7},{7,6},{8,9},{9,8},{10,11... | collective-permute-start | bytes 1179656 | tf_op jit(solution)/shard_map/ppermute | solution.py:91
  121.7 3.8 %collective-permute-start.37 = (bf16[1536,128]{1,0:T(8,128)(2,1)S(1)}, bf16[1536,128]{1,0:T(8,128)(2,1)S(1)}, u32[]{:S(2)}, u32[]{:S(2)}) collective-permute-start(bf16[1536,128]{1,0:T(8,128)(2,1)S(1)} %collective-permute-done.26.refs_6_), channel_id=1, source_target_pairs={{0,1},{1,0},{2,3},{3,2},{4,5},{5,4},{6,7},{7,6},{8,9},{9,8},{10,11... | collective-permute-start | bytes 1179656 | tf_op jit(solution)/shard_map/ppermute | solution.py:91
  123.0 1.9 %collective-permute-start.33 = (bf16[1536,128]{1,0:T(8,128)(2,1)S(1)}, bf16[1536,128]{1,0:T(8,128)(2,1)S(1)}, u32[]{:S(2)}, u32[]{:S(2)}) collective-permute-start(bf16[1536,128]{1,0:T(8,128)(2,1)S(1)} %collective-permute-done.24.refs_2_), channel_id=1, source_target_pairs={{0,1},{1,0},{2,3},{3,2},{4,5},{5,4},{6,7},{7,6},{8,9},{9,8},{10,11... | collective-permute-start | bytes 1179656 | tf_op jit(solution)/shard_map/ppermute | solution.py:91
  123.2 2.3 %collective-permute-start.36 = (bf16[1536,128]{1,0:T(8,128)(2,1)S(1)}, bf16[1536,128]{1,0:T(8,128)(2,1)S(1)}, u32[]{:S(2)}, u32[]{:S(2)}) collective-permute-start(bf16[1536,128]{1,0:T(8,128)(2,1)S(1)} %collective-permute-done.25.refs_5_), channel_id=1, source_target_pairs={{0,1},{1,0},{2,3},{3,2},{4,5},{5,4},{6,7},{7,6},{8,9},{9,8},{10,11... | collective-permute-start | bytes 1179656 | tf_op jit(solution)/shard_map/ppermute | solution.py:91
  123.7 2.3 %collective-permute-start.34 = (bf16[1536,128]{1,0:T(8,128)(2,1)S(1)}, bf16[1536,128]{1,0:T(8,128)(2,1)S(1)}, u32[]{:S(2)}, u32[]{:S(2)}) collective-permute-start(bf16[1536,128]{1,0:T(8,128)(2,1)S(1)} %collective-permute-done.29.refs_3_), channel_id=1, source_target_pairs={{0,1},{1,0},{2,3},{3,2},{4,5},{5,4},{6,7},{7,6},{8,9},{9,8},{10,11... | collective-permute-start | bytes 1179656 | tf_op jit(solution)/shard_map/ppermute | solution.py:91
  123.8 2.8 %collective-permute-start.38 = (bf16[1536,128]{1,0:T(8,128)(2,1)S(1)}, bf16[1536,128]{1,0:T(8,128)(2,1)S(1)}, u32[]{:S(2)}, u32[]{:S(2)}) collective-permute-start(bf16[1536,128]{1,0:T(8,128)(2,1)S(1)} %collective-permute-done.30.refs_7_), channel_id=1, source_target_pairs={{0,1},{1,0},{2,3},{3,2},{4,5},{5,4},{6,7},{7,6},{8,9},{9,8},{10,11... | collective-permute-start | bytes 1179656 | tf_op jit(solution)/shard_map/ppermute | solution.py:91
  132.4 14.9 %collective-permute-start.39 = (bf16[1536,128]{1,0:T(8,128)(2,1)}, bf16[1536,128]{1,0:T(8,128)(2,1)S(1)}, u32[]{:S(2)}, u32[]{:S(2)}) collective-permute-start(bf16[1536,128]{1,0:T(8,128)(2,1)} %shard_map.134), channel_id=1, source_target_pairs={{0,16},{16,0},{1,17},{17,1},{2,18},{18,2},{3,19},{19,3},{4,20},{20... | collective-permute-start | bytes 1179656 | tf_op jit(solution)/shard_map/ppermute | solution.py:400
  (22 other events, 168.7 us)
Sparse Core Ops, SparseCore 0:
  11.4 48.2 all-gather.4
  61.5 43.8 all-gather.6
  112.7 42.5 all-gather.8

commit v3 on v2

--- a/solution.py
+++ b/solution.py
@@ -29,7 +29,6 @@
 LIST = COUNT_AT + 4
 RING_Y = 4
 RING_Z = 8
-WIDE = 256
 AXES = ("z", "x_lo", "x_hi", "y", "core")
 ROW = ("z", "x_lo")
 COL = ("x_hi", "y", "core")
@@ -78,15 +77,16 @@
     first, second = x_perms()
     far = lax.ppermute(tile, IN_CHIP_X, first)
     near = lax.ppermute(tile, IN_CHIP_X, second)
-    far, near = beside(0, far, near)
+    two = lax.ppermute(tile, "y", ring(RING_Y, 2))
+    far, near, two = beside(0, far, near, two)
+    far_down = lax.ppermute(far, "y", ring(RING_Y, -1))
+    far_up = lax.ppermute(far, "y", ring(RING_Y, 1))
     near_up = lax.ppermute(near, "y", ring(RING_Y, 1))
-    far_down = lax.ppermute(far, "y", ring(RING_Y, -1))
     near_down = lax.ppermute(near, "y", ring(RING_Y, -1))
-    far_up = lax.ppermute(far, "y", ring(RING_Y, 1))
-    near_up, near_down, far_up, far_down = beside(1, near_up, near_down, far_up, far_down)
-    near_two = lax.ppermute(near_up, "y", ring(RING_Y, 1))
-    far_two = lax.ppermute(far_down, "y", ring(RING_Y, -1))
-    near_two, far_two = beside(2, near_two, far_two)
+    far_two = lax.ppermute(two, IN_CHIP_X, first)
+    near_two = lax.ppermute(two, IN_CHIP_X, second)
+    moved = (near_up, near_down, near_two, far_up, far_down, far_two)
+    near_up, near_down, near_two, far_up, far_down, far_two = beside(1, *moved)
     mine = [near, near_up, near_down, near_two, far, far_up, far_down, far_two]
     theirs = [lax.ppermute(t, "core", ring(2, 1)) for t in mine]
     return mine + theirs
@@ -104,7 +104,7 @@
     from_x = (x + jnp.where(same, if_same, if_other) + 4) % 4
     from_y = (y + dy + RING_Y) % RING_Y
     order = jnp.where(same, jnp.array(IF_SAME, jnp.int32), jnp.array(IF_OTHER, jnp.int32))
-    return (from_x // 2) * RING_Y + from_y, order, same
+    return (from_x // 2) * RING_Y + from_y, order, same, from_x * RING_Y + from_y
 
 
 def block(n):
@@ -272,6 +272,31 @@
         add_trace(info, places, 0, 0, acc, energy)
 
 
+def plane_kernel(info, todo, *refs):
+    lefts, right = refs[:LEFTS], refs[LEFTS]
+    result, energy, ev, chips, part_sems = refs[LEFTS + 1 : LEFTS + 6]
+    lv, rv, acc, sems = refs[LEFTS + 6 :]
+    copies = [
+        pltpu.make_async_copy(
+            lefts[t].at[pl.ds(BODY, META)], ev.at[pl.ds(t * META, META)], part_sems.at[t]
+        )
+        for t in range(LEFTS)
+    ]
+    for copy in copies:
+        copy.start()
+    load(0, info, lefts, right, lv, rv, sems, False)
+    acc[...] = jnp.zeros_like(acc)
+    for copy in copies:
+        copy.wait()
+    for t in range(LEFTS):
+        parts = ev[t * META : (t + 1) * META, :].astype(jnp.float32)
+        chips[pl.ds(info[3, t], 1), :] = parts[0:1] + parts[1:2] + parts[2:3]
+    energy[...] = chips[0:8, :] + chips[8:16, :]
+    load(0, info, lefts, right, lv, rv, sems, True)
+    multiply(todo, lv, rv, acc)
+    result[...] = acc[0:BODY, :].astype(result.dtype)
+
+
 VMEM = pl.BlockSpec(memory_space=pltpu.VMEM)
 SMEM = pl.BlockSpec(memory_space=pltpu.SMEM)
 FAR = pl.BlockSpec(memory_space=pltpu.HBM)
@@ -336,35 +361,42 @@
     return out if trace else out[0]
 
 
-class Total:
-    steps = (
-        ("core", 2, 1),
-        ("y", RING_Y, 1),
-        ("y", RING_Y, 2),
-        ("x_lo", 2, 1),
-        ("x_hi", 2, 1),
-    )
-
-    def __init__(self, part):
-        self.part, self.done = part, 0
-
-    def advance(self, n):
-        for axis, size, hop in self.steps[self.done : self.done + n]:
-            self.part += lax.ppermute(self.part, axis, [(i, i ^ hop) for i in range(size)])
-        self.done += n
-
-    def finish(self):
-        wide = jnp.pad(self.part, ((0, WIDE - 8), (0, 0)))
-        planes = lax.all_gather(wide, "z", axis=0)
-        return jnp.sum(planes[:, :8])
+def plane_half(info, todo, lefts, right):
+    return pl.pallas_call(
+        plane_kernel,
+        out_shape=[jax.ShapeDtypeStruct((BODY, BLK), jnp.bfloat16), TRACE_SHAPE],
+        in_specs=[SMEM, SMEM] + [FAR] * (LEFTS + 1),
+        out_specs=[VMEM, VMEM],
+        scratch_shapes=[
+            pltpu.VMEM((LEFTS * META, BLK), jnp.bfloat16),
+            pltpu.VMEM((LEFTS, BLK), jnp.float32),
+            pltpu.SemaphoreType.DMA((LEFTS,)),
+        ]
+        + BLOCKS,
+        compiler_params=PARAMS,
+        cost_estimate=cost(100_000_000, 15_000_000),
+    )(info, todo, *lefts, right)
+
+
+def add_partner(part, axis, size, hop):
+    return part + lax.ppermute(part, axis, [(i, i ^ hop) for i in range(size)])
+
+
+def in_three(part):
+    rest = jnp.sum(part, axis=0, keepdims=True)
+    rows = []
+    for _ in range(3):
+        rows.append(lax.reduce_precision(rest, 8, 7))
+        rest = rest - rows[-1]
+    return jnp.pad(jnp.concatenate(rows), ((0, META - 3), (0, 0))).astype(jnp.bfloat16)
 
 
 def per_device(p_values, p_where, p_count, h_values, h_where, h_count):
     z, x_lo, x_hi, y, core = (lax.axis_index(a) for a in AXES)
     row, col = z * 2 + x_lo, (x_hi * RING_Y + y) * 2 + core
-    places, order, same = tile_table(x_hi * 2 + x_lo, y, core)
+    places, order, same, chips = tile_table(x_hi * 2 + x_lo, y, core)
     flags = jnp.stack([row == col, z * 2 + 1 - x_lo == col, same])
-    info = jnp.stack([places, order, jnp.pad(flags.astype(jnp.int32), (0, LEFTS - 3))]).astype(jnp.int32)
+    info = jnp.stack([places, order, jnp.pad(flags.astype(jnp.int32), (0, LEFTS - 3)), chips]).astype(jnp.int32)
 
     p_meta = describe(p_where, p_count, row, col)
     h_meta = describe(h_where, h_count, row, col)
@@ -379,28 +411,30 @@
     other, todo, energy, out_slots = first_half(info, p_tiles, h_line, outs)
     came = lax.ppermute(other, "x_lo", ring(2, 1))
     own, energy = later_half(1, jnp.float32, info, todo, p_tiles, h_line, out_slots, energy)
-    running = Total(energy)
-    running.advance(2)
-    came, running.part = lax.optimization_barrier((came, running.part))
-    ph = (own + came.astype(jnp.float32)).astype(jnp.bfloat16)
-
+    energy = add_partner(energy, "core", 2, 1)
+    energy = add_partner(energy, "z", RING_Z, 1)
+    came, energy = lax.optimization_barrier((came, energy))
+    f_pay = jnp.concatenate([(own + came.astype(jnp.float32)).astype(jnp.bfloat16), in_three(energy)])
+    f_pay = lax.optimization_barrier(f_pay)
     plans = []
 
     def beside(stage, *tiles):
-        if stage == 2:
-            plans.extend(plan_lists(info, p_tiles, p_line, outs))
-            *tiles, plans[:] = lax.optimization_barrier((*tiles, plans))
+        if stage == 0:
             return tiles
-        running.advance(stage + 1)
-        *tiles, running.part = lax.optimization_barrier((*tiles, running.part))
+        plans.extend(plan_lists(info, p_tiles, p_line, outs))
+        *tiles, plans[:] = lax.optimization_barrier((*tiles, plans))
         return tiles
 
-    f_tiles = spread(ph, beside)
-    other = later_half(0, jnp.bfloat16, info, plans[0], f_tiles, p_line)
+    f_tiles = spread(f_pay, beside)
+    other, energy = plane_half(info, plans[0], f_tiles, p_line)
     came = lax.ppermute(other, "x_lo", ring(2, 1))
+    energy = add_partner(energy, "z", RING_Z, 2)
     own = later_half(1, jnp.float32, info, plans[1], f_tiles, p_line)
+    own, energy = lax.optimization_barrier((own, energy))
+    energy = add_partner(energy, "z", RING_Z, 4)
     php = (own + came.astype(jnp.float32)).astype(jnp.bfloat16)
-    return ph.reshape(CAP, BLK, BLK), php.reshape(CAP, BLK, BLK), running.finish()
+    ph = f_pay[:BODY]
+    return ph.reshape(CAP, BLK, BLK), php.reshape(CAP, BLK, BLK), jnp.sum(energy)
 
 
 def solution(mesh):

time: 164 us -> 158 us (0.963)
  waiting for transfers between devices: 56 us -> 35 us
  starting transfers between devices: 49.2 us -> 62.5 us
    ppermute x9 -> x10, starting transfers between devices: 18.2 us -> 26 us  [the longest x4 11.2 us: add_partner(): return part + lax.ppermute(part, axis, [(i, i ^ hop) for i in range(size)])]
    all_gather x1 -> x0, waiting for transfers between devices: 6.07 us -> none  [finish(): planes = lax.all_gather(wide, 'z', axis=0)]
    pallas_call x0 -> x1, Pallas kernels: none -> 5.2 us  [plane_half(): pl.pallas_call(plane_kernel, out_shape=[jax.ShapeDtypeStruct((BODY, BLK),...]
    ppermute x2, waiting for transfers between devices: 4.8 us -> 0.01 us  [per_device(): came = lax.ppermute(other, 'x_lo', ring(2, 1))]
    pallas_call x3 -> x2, Pallas kernels: 15.1 us -> 10.5 us  [later_half(): pl.pallas_call(functools.partial(half_kernel, half, bool(trace)), out_sha...]
    ppermute x16, starting transfers between devices: 4.43 us -> 8.21 us  [spread(): theirs = [lax.ppermute(t, 'core', ring(2, 1)) for t in mine]]
    ppermute x2, waiting for transfers between devices: 3.45 us -> 0.01 us  [spread(): near_down = lax.ppermute(near, 'y', ring(RING_Y, -1))]
    ppermute x2, waiting for transfers between devices: 11 us -> 7.92 us  [spread(): near = lax.ppermute(tile, IN_CHIP_X, second)]
  transfers between devices with their start and end apart: 43 -> 43, of which waited for: 24 -> 22; matrix products, arithmetic and copies ran while one was open for 5% -> 5% of each run, Pallas kernels for 17% -> 15%
where the time goes in v3:
time: 158 us; the launch traced here: 157 us
  starting transfers between devices  62.5 us (40%)
  waiting for transfers between devices  35 us (22%)
  Pallas kernels  28.9 us (18%)
  between operations  15.8 us (10%)
  other arithmetic  11.7 us (7%)
  local copies, waits for them, and re-layouts  3.05 us (2%)
    ppermute x4, starting transfers between devices, add_partner(): return part + lax.ppermute(part, axis, [(i, i ^ hop) for i in range(size)])  11.2 us
    pallas_call x2, Pallas kernels, later_half(): pl.pallas_call(functools.partial(half_kernel, half, bool(trace)), out_sha...  10.5 us
    ppermute x16, starting transfers between devices, spread(): theirs = [lax.ppermute(t, 'core', ring(2, 1)) for t in mine]  8.21 us
    pallas_call x1, Pallas kernels, first_half(): pl.pallas_call(first_kernel, out_shape=[jax.ShapeDtypeStruct((BODY, BLK),...  8.14 us
    ppermute x2, waiting for transfers between devices, spread(): near = lax.ppermute(tile, IN_CHIP_X, second)  7.92 us
    ppermute x2, starting transfers between devices, spread(): near_two = lax.ppermute(two, IN_CHIP_X, second)  7.06 us
    ppermute x2, starting transfers between devices, per_device(): came = lax.ppermute(other, 'x_lo', ring(2, 1))  6.96 us
    ppermute x2, starting transfers between devices, spread(): near_down = lax.ppermute(near, 'y', ring(RING_Y, -1))  5.7 us
  transfers between devices with their start and end apart: 43, of which 22 were waited for; matrix products, arithmetic and copies ran while one was open for 5% of the time, Pallas kernels for 15%

profile of v3, /device:TPU:2, one launch (start us, length us, event | category | flops | bytes accessed | tf_op | source)
XLA Modules:
  0.0 157.0 jit_solution(9149829501792683908)
XLA Ops:
  8.6 0.8 add_bitcast_fusion.1
  9.5 1.8 %pad_maximum_fusion.1 = bf16[1552,128]{1,0:T(8,128)(2,1)} fusion(bf16[16,128]{1,0:T(8,128)(2,1)S(1)} %broadcast_in_dim.93, bf16[1536,128]{1,0:T(8,128)(2,1)} %bitcast.46), kind=kLoop, calls=%fused_computation.3 | loop fusion | flops 794624 | bytes 794624 | tf_op jit(solution)/shard_map/concatenate | solution.py:403
  11.4 1.8 %pad_maximum_fusion = bf16[1552,128]{1,0:T(8,128)(2,1)} fusion(bf16[16,128]{1,0:T(8,128)(2,1)S(1)} %broadcast_in_dim.86, bf16[1536,128]{1,0:T(8,128)(2,1)} %bitcast.47), kind=kLoop, calls=%fused_computation.2 | loop fusion | flops 794624 | bytes 794624 | tf_op jit(solution)/shard_map/concatenate | solution.py:404
  13.2 1.9 %collective-permute-start = (bf16[1552,128]{1,0:T(8,128)(2,1)}, bf16[1552,128]{1,0:T(8,128)(2,1)S(1)}, u32[]{:S(2)}, u32[]{:S(2)}) collective-permute-start(bf16[1552,128]{1,0:T(8,128)(2,1)} %pad_maximum_fusion), channel_id=1, source_target_pairs={{1,24},{0,0},{16,1},{17,17},{9,16},{8,8},{24,9},{25,25},{3,26},{2,... | collective-permute-start | bytes 1191944 | tf_op jit(solution)/shard_map/ppermute | solution.py:79
  15.1 3.3 %collective-permute-start.3 = (bf16[1552,128]{1,0:T(8,128)(2,1)}, bf16[1552,128]{1,0:T(8,128)(2,1)}, u32[]{:S(2)}, u32[]{:S(2)}) collective-permute-start(bf16[1552,128]{1,0:T(8,128)(2,1)} %pad_maximum_fusion), channel_id=1, source_target_pairs={{0,4},{2,6},{4,0},{6,2},{1,5},{3,7},{5,1},{7,3},{8,12},{10,14},{12... | collective-permute-start | bytes 1191944 | tf_op jit(solution)/shard_map/ppermute | solution.py:80
  18.4 1.1 collective-permute-start.5
  19.6 3.0 %collective-permute-done.refs_0_ = bf16[1552,128]{1,0:T(8,128)(2,1)S(1)} collective-permute-done((bf16[1552,128]{1,0:T(8,128)(2,1)}, bf16[1552,128]{1,0:T(8,128)(2,1)S(1)}, u32[]{:S(2)}, u32[]{:S(2)}) %collective-permute-start) | collective-permute-done | bytes 397344 | tf_op jit(solution)/shard_map/ppermute | solution.py:79
  22.6 1.8 %collective-permute-start.1 = (bf16[1552,128]{1,0:T(8,128)(2,1)S(1)}, bf16[1552,128]{1,0:T(8,128)(2,1)S(1)}, u32[]{:S(2)}, u32[]{:S(2)}) collective-permute-start(bf16[1552,128]{1,0:T(8,128)(2,1)S(1)} %collective-permute-done.refs_0_), channel_id=1, source_target_pairs={{0,2},{2,4},{4,6},{6,0},{1,3},{3,5},{5,7},{7,1},{8,10},{10,12},{12... | collective-permute-start | bytes 1191944 | tf_op jit(solution)/shard_map/ppermute | solution.py:84
  24.4 2.5 %collective-permute-start.2 = (bf16[1552,128]{1,0:T(8,128)(2,1)S(1)}, bf16[1552,128]{1,0:T(8,128)(2,1)S(1)}, u32[]{:S(2)}, u32[]{:S(2)}) collective-permute-start(bf16[1552,128]{1,0:T(8,128)(2,1)S(1)} %collective-permute-done.refs_0_), channel_id=1, source_target_pairs={{0,6},{2,0},{4,2},{6,4},{1,7},{3,1},{5,3},{7,5},{8,14},{10,8},{12,... | collective-permute-start | bytes 1191944 | tf_op jit(solution)/shard_map/ppermute | solution.py:85
  26.9 2.3 %collective-permute-done.3 = bf16[1552,128]{1,0:T(8,128)(2,1)} collective-permute-done((bf16[1552,128]{1,0:T(8,128)(2,1)}, bf16[1552,128]{1,0:T(8,128)(2,1)}, u32[]{:S(2)}, u32[]{:S(2)}) %collective-permute-start.3) | collective-permute-done | bytes 397344 | tf_op jit(solution)/shard_map/ppermute | solution.py:80
  29.2 3.7 %collective-permute-start.4 = (bf16[1552,128]{1,0:T(8,128)(2,1)}, bf16[1552,128]{1,0:T(8,128)(2,1)S(1)}, u32[]{:S(2)}, u32[]{:S(2)}) collective-permute-start(bf16[1552,128]{1,0:T(8,128)(2,1)} %collective-permute-done.3), channel_id=1, source_target_pairs={{1,24},{0,0},{16,1},{17,17},{9,16},{8,8},{24,9},{25,25},{3,26},{2,... | collective-permute-start | bytes 1191944 | tf_op jit(solution)/shard_map/ppermute | solution.py:87
  32.9 2.1 %collective-permute-start.6 = (bf16[1552,128]{1,0:T(8,128)(2,1)S(1)}, bf16[1552,128]{1,0:T(8,128)(2,1)S(1)}, u32[]{:S(2)}, u32[]{:S(2)}) collective-permute-start(bf16[1552,128]{1,0:T(8,128)(2,1)S(1)} %collective-permute-done.5.refs_4_), channel_id=1, source_target_pairs={{0,2},{2,4},{4,6},{6,0},{1,3},{3,5},{5,7},{7,1},{8,10},{10,12},{12... | collective-permute-start | bytes 1191944 | tf_op jit(solution)/shard_map/ppermute | solution.py:83
  35.0 3.6 %collective-permute-done.17 = bf16[16,128]{1,0:T(8,128)(2,1)S(1)} collective-permute-done((bf16[16,128]{1,0:T(8,128)(2,1)S(1)}, bf16[16,128]{1,0:T(8,128)(2,1)S(1)}, u32[]{:S(2)}, u32[]{:S(2)}) %collective-permute-start.17) | collective-permute-done | bytes 4128 | tf_op jit(solution)/shard_map/ppermute | solution.py:407
  38.6 3.1 %collective-permute-start.7 = (bf16[1552,128]{1,0:T(8,128)(2,1)S(1)}, bf16[1552,128]{1,0:T(8,128)(2,1)S(1)}, u32[]{:S(2)}, u32[]{:S(2)}) collective-permute-start(bf16[1552,128]{1,0:T(8,128)(2,1)S(1)} %collective-permute-done.5.refs_4_), channel_id=1, source_target_pairs={{0,6},{2,0},{4,2},{6,4},{1,7},{3,1},{5,3},{7,5},{8,14},{10,8},{12,... | collective-permute-start | bytes 1191944 | tf_op jit(solution)/shard_map/ppermute | solution.py:82
  41.6 2.1 %collective-permute-start.8 = (bf16[1552,128]{1,0:T(8,128)(2,1)}, bf16[1552,128]{1,0:T(8,128)(2,1)S(1)}, u32[]{:S(2)}, u32[]{:S(2)}) collective-permute-start(bf16[1552,128]{1,0:T(8,128)(2,1)} %collective-permute-done.3), channel_id=1, source_target_pairs={{1,17},{0,9},{16,8},{17,24},{9,25},{8,1},{24,0},{25,16},{3,19},{2,... | collective-permute-start | bytes 1191944 | tf_op jit(solution)/shard_map/ppermute | solution.py:86
  44.6 0.8 add_bitcast_fusion.3
  45.4 4.0 %collective-permute-done.7.refs_6_ = bf16[1552,128]{1,0:T(8,128)(2,1)S(1)} collective-permute-done((bf16[1552,128]{1,0:T(8,128)(2,1)S(1)}, bf16[1552,128]{1,0:T(8,128)(2,1)S(1)}, u32[]{:S(2)}, u32[]{:S(2)}) %collective-permute-start.7) | collective-permute-done | bytes 397344 | tf_op jit(solution)/shard_map/ppermute | solution.py:82
  49.4 4.2 %collective-permute-done.8.refs_7_ = bf16[1552,128]{1,0:T(8,128)(2,1)S(1)} collective-permute-done((bf16[1552,128]{1,0:T(8,128)(2,1)}, bf16[1552,128]{1,0:T(8,128)(2,1)S(1)}, u32[]{:S(2)}, u32[]{:S(2)}) %collective-permute-start.8) | collective-permute-done | bytes 397344 | tf_op jit(solution)/shard_map/ppermute | solution.py:86
  57.5 0.8 copy-done.14
  58.3 1.4 all-gather.3.cloned.1.call-done.refs_16_
  59.7 8.1 %shard_map.130 = (bf16[1536,128]{1,0:T(8,128)(2,1)}, s32[776]{0:T(1024)}, f32[8,128]{1,0:T(8,128)}, s32[8,128]{1,0:T(8,128)}) custom-call(s32[4,16]{1,0:T(4,128)} %pad_add_fusion.info, bf16[1552,128]{1,0:T(8,128)(2,1)} %copy-done, bf16[1552,128]{1,0:T(8,128)(2,1)} %copy-done.2, bf16[1552,128]{1,0:T(8,128)(2,1)} %copy-done.3, bf16[1552,128]{1,0:T(8,128)(2,1)} %copy-done.4, ...), custom_call_target="tpu_custom_call" | custom-call | flops 100000000 | bytes 20000000 | tf_op jit(solution)/shard_map/pallas_call | solution.py:339
  67.9 1.7 %collective-permute-start.18 = (bf16[1536,128]{1,0:T(8,128)(2,1)}, bf16[1536,128]{1,0:T(8,128)(2,1)S(1)}, u32[]{:S(2)}, u32[]{:S(2)}) collective-permute-start(bf16[1536,128]{1,0:T(8,128)(2,1)} %get-tuple-element.29), channel_id=1, source_target_pairs={{0,16},{16,0},{1,17},{17,1},{2,18},{18,2},{3,19},{19,3},{4,20},{20... | collective-permute-start | bytes 1179656 | tf_op jit(solution)/shard_map/ppermute | solution.py:412
  69.6 5.5 %shard_map.131 = (f32[1536,128]{1,0:T(8,128)}, f32[8,128]{1,0:T(8,128)}) custom-call(s32[4,16]{1,0:T(4,128)} %pad_add_fusion.info, s32[776]{0:T(1024)} %get-tuple-element.25.todo, bf16[1552,128]{1,0:T(8,128)(2,1)} %copy-done, bf16[1552,128]{1,0:T(8,128)(2,1)} %copy-done.2, bf16[1552,128]{1,0:T(8,128)(2,1)} %copy-done.3, bf16[1552,128]{1,0:T(8,128)(2,1)} %copy-done.4, ...), custom_call_target="tpu_custom_call" | custom-call | flops 100000000 | bytes 15000000 | tf_op jit(solution)/shard_map/pallas_call | solution.py:352
  75.3 1.4 collective-permute-done.19
  76.6 0.7 add.113
  77.3 2.4 %collective-permute-start.20 = (f32[8,128]{1,0:T(8,128)S(1)}, f32[8,128]{1,0:T(8,128)S(1)}, u32[]{:S(2)}, u32[]{:S(2)}) collective-permute-start(f32[8,128]{1,0:T(8,128)S(1)} %add.113), channel_id=1, source_target_pairs={{0,32},{32,0},{64,96},{96,64},{128,160},{160,128},{192,224},{224,1... | collective-permute-start | bytes 12296 | tf_op jit(solution)/shard_map/ppermute | solution.py:382
  79.7 1.6 %collective-permute-done.20 = f32[8,128]{1,0:T(8,128)S(1)} collective-permute-done((f32[8,128]{1,0:T(8,128)S(1)}, f32[8,128]{1,0:T(8,128)S(1)}, u32[]{:S(2)}, u32[]{:S(2)}) %collective-permute-start.20) | collective-permute-done | bytes 4128 | tf_op jit(solution)/shard_map/ppermute | solution.py:382
  81.3 1.2 add_convert_fusion.1
  82.6 1.9 %collective-permute-start.21 = (bf16[1552,128]{1,0:T(8,128)(2,1)S(1)}, bf16[1552,128]{1,0:T(8,128)(2,1)S(1)}, u32[]{:S(2)}, u32[]{:S(2)}) collective-permute-start(bf16[1552,128]{1,0:T(8,128)(2,1)S(1)} %pad_maximum_fusion.2), channel_id=1, source_target_pairs={{1,24},{0,0},{16,1},{17,17},{9,16},{8,8},{24,9},{25,25},{3,26},{2,... | collective-permute-start | bytes 1191944 | tf_op jit(solution)/shard_map/ppermute | solution.py:79
  84.5 2.4 %collective-permute-start.24 = (bf16[1552,128]{1,0:T(8,128)(2,1)S(1)}, bf16[1552,128]{1,0:T(8,128)(2,1)}, u32[]{:S(2)}, u32[]{:S(2)}) collective-permute-start(bf16[1552,128]{1,0:T(8,128)(2,1)S(1)} %pad_maximum_fusion.2), channel_id=1, source_target_pairs={{0,4},{2,6},{4,0},{6,2},{1,5},{3,7},{5,1},{7,3},{8,12},{10,14},{12... | collective-permute-start | bytes 1191944 | tf_op jit(solution)/shard_map/ppermute | solution.py:80
  87.1 4.9 %collective-permute-done.21.refs_0_ = bf16[1552,128]{1,0:T(8,128)(2,1)S(1)} collective-permute-done((bf16[1552,128]{1,0:T(8,128)(2,1)S(1)}, bf16[1552,128]{1,0:T(8,128)(2,1)S(1)}, u32[]{:S(2)}, u32[]{:S(2)}) %collective-permute-start.21) | collective-permute-done | bytes 397344 | tf_op jit(solution)/shard_map/ppermute | solution.py:79
  92.0 3.2 %collective-permute-start.23 = (bf16[1552,128]{1,0:T(8,128)(2,1)S(1)}, bf16[1552,128]{1,0:T(8,128)(2,1)S(1)}, u32[]{:S(2)}, u32[]{:S(2)}) collective-permute-start(bf16[1552,128]{1,0:T(8,128)(2,1)S(1)} %collective-permute-done.21.refs_0_), channel_id=1, source_target_pairs={{0,6},{2,0},{4,2},{6,4},{1,7},{3,1},{5,3},{7,5},{8,14},{10,8},{12,... | collective-permute-start | bytes 1191944 | tf_op jit(solution)/shard_map/ppermute | solution.py:85
  95.2 3.1 %collective-permute-done.24 = bf16[1552,128]{1,0:T(8,128)(2,1)} collective-permute-done((bf16[1552,128]{1,0:T(8,128)(2,1)S(1)}, bf16[1552,128]{1,0:T(8,128)(2,1)}, u32[]{:S(2)}, u32[]{:S(2)}) %collective-permute-start.24) | collective-permute-done | bytes 397344 | tf_op jit(solution)/shard_map/ppermute | solution.py:80
  98.4 3.4 %collective-permute-start.25 = (bf16[1552,128]{1,0:T(8,128)(2,1)}, bf16[1552,128]{1,0:T(8,128)(2,1)S(1)}, u32[]{:S(2)}, u32[]{:S(2)}) collective-permute-start(bf16[1552,128]{1,0:T(8,128)(2,1)} %collective-permute-done.24), channel_id=1, source_target_pairs={{1,24},{0,0},{16,1},{17,17},{9,16},{8,8},{24,9},{25,25},{3,26},{2,... | collective-permute-start | bytes 1191944 | tf_op jit(solution)/shard_map/ppermute | solution.py:87
  101.8 1.6 %collective-permute-start.27 = (bf16[1552,128]{1,0:T(8,128)(2,1)S(1)}, bf16[1552,128]{1,0:T(8,128)(2,1)S(1)}, u32[]{:S(2)}, u32[]{:S(2)}) collective-permute-start(bf16[1552,128]{1,0:T(8,128)(2,1)S(1)} %collective-permute-done.26.refs_4_), channel_id=1, source_target_pairs={{0,2},{2,4},{4,6},{6,0},{1,3},{3,5},{5,7},{7,1},{8,10},{10,12},{12... | collective-permute-start | bytes 1191944 | tf_op jit(solution)/shard_map/ppermute | solution.py:83
  103.4 1.7 %collective-permute-start.28 = (bf16[1552,128]{1,0:T(8,128)(2,1)S(1)}, bf16[1552,128]{1,0:T(8,128)(2,1)S(1)}, u32[]{:S(2)}, u32[]{:S(2)}) collective-permute-start(bf16[1552,128]{1,0:T(8,128)(2,1)S(1)} %collective-permute-done.26.refs_4_), channel_id=1, source_target_pairs={{0,6},{2,0},{4,2},{6,4},{1,7},{3,1},{5,3},{7,5},{8,14},{10,8},{12,... | collective-permute-start | bytes 1191944 | tf_op jit(solution)/shard_map/ppermute | solution.py:82
  105.1 0.9 collective-permute-done.22.refs_1_
  106.0 5.1 %shard_map.132 = (s32[776]{0:T(1024)}, s32[776]{0:T(1024)}) custom-call(s32[4,16]{1,0:T(4,128)} %pad_add_fusion.info, bf16[1552,128]{1,0:T(8,128)(2,1)} %copy-done, bf16[1552,128]{1,0:T(8,128)(2,1)} %copy-done.2, bf16[1552,128]{1,0:T(8,128)(2,1)} %copy-done.3, bf16[1552,128]{1,0:T(8,128)(2,1)} %copy-done.4, bf16[1552,128]{1,0:T(8,128)(2,1)} %copy-done.1, ...), custom_call_target="tpu_custom_call" | custom-call | flops 1000000 | bytes 10000000 | tf_op jit(solution)/shard_map/pallas_call | solution.py:327
  111.1 4.4 %collective-permute-start.30 = (bf16[1552,128]{1,0:T(8,128)(2,1)S(1)}, bf16[1552,128]{1,0:T(8,128)(2,1)S(1)}, u32[]{:S(2)}, u32[]{:S(2)}) collective-permute-start(bf16[1552,128]{1,0:T(8,128)(2,1)S(1)} %collective-permute-done.21.refs_0_), channel_id=1, source_target_pairs={{0,1},{1,0},{2,3},{3,2},{4,5},{5,4},{6,7},{7,6},{8,9},{9,8},{10,11... | collective-permute-start | bytes 1191944 | tf_op jit(solution)/shard_map/ppermute | solution.py:91
  121.1 0.8 copy-done.30
  121.8 5.2 %shard_map.134 = (bf16[1536,128]{1,0:T(8,128)(2,1)}, f32[8,128]{1,0:T(8,128)}) custom-call(s32[4,16]{1,0:T(4,128)} %pad_add_fusion.info, s32[776]{0:T(1024)} %get-tuple-element.42.todo, bf16[1552,128]{1,0:T(8,128)(2,1)} %copy-done.15, bf16[1552,128]{1,0:T(8,128)(2,1)} %copy-done.17, bf16[1552,128]{1,0:T(8,128)(2,1)} %copy-done.18, ...), custom_call_target="tpu_custom_call" | custom-call | flops 100000000 | bytes 15000000 | tf_op jit(solution)/shard_map/pallas_call | solution.py:365
  127.0 5.2 %collective-permute-start.39 = (bf16[1536,128]{1,0:T(8,128)(2,1)}, bf16[1536,128]{1,0:T(8,128)(2,1)S(1)}, u32[]{:S(2)}, u32[]{:S(2)}) collective-permute-start(bf16[1536,128]{1,0:T(8,128)(2,1)} %get-tuple-element.45), channel_id=1, source_target_pairs={{0,16},{16,0},{1,17},{17,1},{2,18},{18,2},{3,19},{19,3},{4,20},{20... | collective-permute-start | bytes 1179656 | tf_op jit(solution)/shard_map/ppermute | solution.py:430
  132.3 2.4 %collective-permute-start.38 = (f32[8,128]{1,0:T(8,128)}, f32[8,128]{1,0:T(8,128)S(1)}, u32[]{:S(2)}, u32[]{:S(2)}) collective-permute-start(f32[8,128]{1,0:T(8,128)} %get-tuple-element.43), channel_id=1, source_target_pairs={{0,64},{32,96},{64,0},{96,32},{128,192},{160,224},{192,128},{224,1... | collective-permute-start | bytes 12296 | tf_op jit(solution)/shard_map/ppermute | solution.py:382
  134.7 5.0 %shard_map.133 = f32[1536,128]{1,0:T(8,128)} custom-call(s32[4,16]{1,0:T(4,128)} %pad_add_fusion.info, s32[776]{0:T(1024)} %get-tuple-element.35.todo, bf16[1552,128]{1,0:T(8,128)(2,1)} %copy-done.15, bf16[1552,128]{1,0:T(8,128)(2,1)} %copy-done.17, bf16[1552,128]{1,0:T(8,128)(2,1)} %copy-done.18, bf16[1552,128]{1,0:T(8,128)(2,1)} %copy-done.19, ...), custom_call_target="tpu_custom_call" | custom-call | flops 100000000 | bytes 15000000 | tf_op jit(solution)/shard_map/pallas_call | solution.py:352
  139.7 6.3 %collective-permute-start.40 = (f32[8,128]{1,0:T(8,128)S(1)}, f32[8,128]{1,0:T(8,128)S(1)}, u32[]{:S(2)}, u32[]{:S(2)}) collective-permute-start(f32[8,128]{1,0:T(8,128)S(1)} %add.116), channel_id=1, source_target_pairs={{0,128},{32,160},{64,192},{96,224},{128,0},{160,32},{192,64},{224,... | collective-permute-start | bytes 12296 | tf_op jit(solution)/shard_map/ppermute | solution.py:382
  146.0 0.8 slice.20
  146.8 0.8 collective-permute-done.40
  148.2 2.0 %add_convert_fusion = bf16[1536,128]{1,0:T(8,128)(2,1)} fusion(f32[1536,128]{1,0:T(8,128)} %shard_map.133, bf16[1536,128]{1,0:T(8,128)(2,1)S(1)} %collective-permute-done.39), kind=kLoop, calls=%fused_computation | loop fusion | flops 589824 | bytes 1572864 | tf_op jit(solution)/shard_map/convert_element_type | solution.py:435
  (144 shorter events, 11.6 us)
Async XLA Ops:
  7.2 52.5 %all-gather.3.cloned.1.call-start = ((), (), s32[]{:S(2)}) async-start(), calls=%async_computation | async-start | bytes 3575808 | tf_op jit(solution)/shard_map/all_gather | solution.py:405
  11.3 94.7 %all-gather.5.cloned.1.call-start = ((), (), s32[]{:S(2)}) async-start(), calls=%async_computation.1 | async-start | bytes 3575808 | tf_op jit(solution)/shard_map/all_gather | solution.py:406
  13.2 9.3 %collective-permute-start = (bf16[1552,128]{1,0:T(8,128)(2,1)}, bf16[1552,128]{1,0:T(8,128)(2,1)S(1)}, u32[]{:S(2)}, u32[]{:S(2)}) collective-permute-start(bf16[1552,128]{1,0:T(8,128)(2,1)} %pad_maximum_fusion), channel_id=1, source_target_pairs={{1,24},{0,0},{16,1},{17,17},{9,16},{8,8},{24,9},{25,25},{3,26},{2,... | collective-permute-start | bytes 1191944 | tf_op jit(solution)/shard_map/ppermute | solution.py:79
  15.1 14.0 %collective-permute-start.3 = (bf16[1552,128]{1,0:T(8,128)(2,1)}, bf16[1552,128]{1,0:T(8,128)(2,1)}, u32[]{:S(2)}, u32[]{:S(2)}) collective-permute-start(bf16[1552,128]{1,0:T(8,128)(2,1)} %pad_maximum_fusion), channel_id=1, source_target_pairs={{0,4},{2,6},{4,0},{6,2},{1,5},{3,7},{5,1},{7,3},{8,12},{10,14},{12... | collective-permute-start | bytes 1191944 | tf_op jit(solution)/shard_map/ppermute | solution.py:80
  18.4 14.4 %collective-permute-start.5 = (bf16[1552,128]{1,0:T(8,128)(2,1)}, bf16[1552,128]{1,0:T(8,128)(2,1)S(1)}, u32[]{:S(2)}, u32[]{:S(2)}) collective-permute-start(bf16[1552,128]{1,0:T(8,128)(2,1)} %pad_maximum_fusion), channel_id=1, source_target_pairs={{1,17},{0,9},{16,8},{17,24},{9,25},{8,1},{24,0},{25,16},{3,19},{2,... | collective-permute-start | bytes 1191944 | tf_op jit(solution)/shard_map/ppermute | solution.py:78
  22.6 37.1 %copy-start = (bf16[1552,128]{1,0:T(8,128)(2,1)}, bf16[1552,128]{1,0:T(8,128)(2,1)S(1)}, u32[]{:S(2)}) copy-start(bf16[1552,128]{1,0:T(8,128)(2,1)S(1)} %collective-permute-done.refs_0_) | copy-start | bytes 1191940
  22.6 19.1 %collective-permute-start.1 = (bf16[1552,128]{1,0:T(8,128)(2,1)S(1)}, bf16[1552,128]{1,0:T(8,128)(2,1)S(1)}, u32[]{:S(2)}, u32[]{:S(2)}) collective-permute-start(bf16[1552,128]{1,0:T(8,128)(2,1)S(1)} %collective-permute-done.refs_0_), channel_id=1, source_target_pairs={{0,2},{2,4},{4,6},{6,0},{1,3},{3,5},{5,7},{7,1},{8,10},{10,12},{12... | collective-permute-start | bytes 1191944 | tf_op jit(solution)/shard_map/ppermute | solution.py:84
  24.4 19.3 %collective-permute-start.2 = (bf16[1552,128]{1,0:T(8,128)(2,1)S(1)}, bf16[1552,128]{1,0:T(8,128)(2,1)S(1)}, u32[]{:S(2)}, u32[]{:S(2)}) collective-permute-start(bf16[1552,128]{1,0:T(8,128)(2,1)S(1)} %collective-permute-done.refs_0_), channel_id=1, source_target_pairs={{0,6},{2,0},{4,2},{6,4},{1,7},{3,1},{5,3},{7,5},{8,14},{10,8},{12,... | collective-permute-start | bytes 1191944 | tf_op jit(solution)/shard_map/ppermute | solution.py:85
  29.2 14.5 %collective-permute-start.4 = (bf16[1552,128]{1,0:T(8,128)(2,1)}, bf16[1552,128]{1,0:T(8,128)(2,1)S(1)}, u32[]{:S(2)}, u32[]{:S(2)}) collective-permute-start(bf16[1552,128]{1,0:T(8,128)(2,1)} %collective-permute-done.3), channel_id=1, source_target_pairs={{1,24},{0,0},{16,1},{17,17},{9,16},{8,8},{24,9},{25,25},{3,26},{2,... | collective-permute-start | bytes 1191944 | tf_op jit(solution)/shard_map/ppermute | solution.py:87
  32.9 26.8 %copy-start.1 = (bf16[1552,128]{1,0:T(8,128)(2,1)}, bf16[1552,128]{1,0:T(8,128)(2,1)S(1)}, u32[]{:S(2)}) copy-start(bf16[1552,128]{1,0:T(8,128)(2,1)S(1)} %collective-permute-done.5.refs_4_) | copy-start | bytes 1191940
  32.9 11.7 %collective-permute-start.6 = (bf16[1552,128]{1,0:T(8,128)(2,1)S(1)}, bf16[1552,128]{1,0:T(8,128)(2,1)S(1)}, u32[]{:S(2)}, u32[]{:S(2)}) collective-permute-start(bf16[1552,128]{1,0:T(8,128)(2,1)S(1)} %collective-permute-done.5.refs_4_), channel_id=1, source_target_pairs={{0,2},{2,4},{4,6},{6,0},{1,3},{3,5},{5,7},{7,1},{8,10},{10,12},{12... | collective-permute-start | bytes 1191944 | tf_op jit(solution)/shard_map/ppermute | solution.py:83
  35.0 3.6 %collective-permute-start.17 = (bf16[16,128]{1,0:T(8,128)(2,1)S(1)}, bf16[16,128]{1,0:T(8,128)(2,1)S(1)}, u32[]{:S(2)}, u32[]{:S(2)}) collective-permute-start(bf16[16,128]{1,0:T(8,128)(2,1)S(1)} %broadcast_in_dim.86), channel_id=1, source_target_pairs={{0,16},{16,0},{1,17},{17,1},{2,18},{18,2},{3,19},{19,3},{4,20},{20... | collective-permute-start | bytes 12296 | tf_op jit(solution)/shard_map/ppermute | solution.py:407
  38.6 10.8 %collective-permute-start.7 = (bf16[1552,128]{1,0:T(8,128)(2,1)S(1)}, bf16[1552,128]{1,0:T(8,128)(2,1)S(1)}, u32[]{:S(2)}, u32[]{:S(2)}) collective-permute-start(bf16[1552,128]{1,0:T(8,128)(2,1)S(1)} %collective-permute-done.5.refs_4_), channel_id=1, source_target_pairs={{0,6},{2,0},{4,2},{6,4},{1,7},{3,1},{5,3},{7,5},{8,14},{10,8},{12,... | collective-permute-start | bytes 1191944 | tf_op jit(solution)/shard_map/ppermute | solution.py:82
  41.6 18.1 %copy-start.2 = (bf16[1552,128]{1,0:T(8,128)(2,1)}, bf16[1552,128]{1,0:T(8,128)(2,1)S(1)}, u32[]{:S(2)}) copy-start(bf16[1552,128]{1,0:T(8,128)(2,1)S(1)} %collective-permute-done.1.refs_1_) | copy-start | bytes 1191940
  41.6 11.9 %collective-permute-start.8 = (bf16[1552,128]{1,0:T(8,128)(2,1)}, bf16[1552,128]{1,0:T(8,128)(2,1)S(1)}, u32[]{:S(2)}, u32[]{:S(2)}) collective-permute-start(bf16[1552,128]{1,0:T(8,128)(2,1)} %collective-permute-done.3), channel_id=1, source_target_pairs={{1,17},{0,9},{16,8},{17,24},{9,25},{8,1},{24,0},{25,16},{3,19},{2,... | collective-permute-start | bytes 1191944 | tf_op jit(solution)/shard_map/ppermute | solution.py:86
  43.7 9.8 %collective-permute-start.9 = (bf16[1552,128]{1,0:T(8,128)(2,1)S(1)}, bf16[1552,128]{1,0:T(8,128)(2,1)S(1)}, u32[]{:S(2)}, u32[]{:S(2)}) collective-permute-start(bf16[1552,128]{1,0:T(8,128)(2,1)S(1)} %collective-permute-done.refs_0_), channel_id=1, source_target_pairs={{0,1},{1,0},{2,3},{3,2},{4,5},{5,4},{6,7},{7,6},{8,9},{9,8},{10,11... | collective-permute-start | bytes 1191944 | tf_op jit(solution)/shard_map/ppermute | solution.py:91
  43.8 10.3 %collective-permute-start.13 = (bf16[1552,128]{1,0:T(8,128)(2,1)S(1)}, bf16[1552,128]{1,0:T(8,128)(2,1)S(1)}, u32[]{:S(2)}, u32[]{:S(2)}) collective-permute-start(bf16[1552,128]{1,0:T(8,128)(2,1)S(1)} %collective-permute-done.5.refs_4_), channel_id=1, source_target_pairs={{0,1},{1,0},{2,3},{3,2},{4,5},{5,4},{6,7},{7,6},{8,9},{9,8},{10,11... | collective-permute-start | bytes 1191944 | tf_op jit(solution)/shard_map/ppermute | solution.py:91
  44.6 9.6 %collective-permute-start.10 = (bf16[1552,128]{1,0:T(8,128)(2,1)S(1)}, bf16[1552,128]{1,0:T(8,128)(2,1)S(1)}, u32[]{:S(2)}, u32[]{:S(2)}) collective-permute-start(bf16[1552,128]{1,0:T(8,128)(2,1)S(1)} %collective-permute-done.1.refs_1_), channel_id=1, source_target_pairs={{0,1},{1,0},{2,3},{3,2},{4,5},{5,4},{6,7},{7,6},{8,9},{9,8},{10,11... | collective-permute-start | bytes 1191944 | tf_op jit(solution)/shard_map/ppermute | solution.py:91
  49.4 7.1 %collective-permute-start.11 = (bf16[1552,128]{1,0:T(8,128)(2,1)S(1)}, bf16[1552,128]{1,0:T(8,128)(2,1)S(1)}, u32[]{:S(2)}, u32[]{:S(2)}) collective-permute-start(bf16[1552,128]{1,0:T(8,128)(2,1)S(1)} %collective-permute-done.2.refs_2_), channel_id=1, source_target_pairs={{0,1},{1,0},{2,3},{3,2},{4,5},{5,4},{6,7},{7,6},{8,9},{9,8},{10,11... | collective-permute-start | bytes 1191944 | tf_op jit(solution)/shard_map/ppermute | solution.py:91
  53.6 2.9 %collective-permute-start.12 = (bf16[1552,128]{1,0:T(8,128)(2,1)S(1)}, bf16[1552,128]{1,0:T(8,128)(2,1)S(1)}, u32[]{:S(2)}, u32[]{:S(2)}) collective-permute-start(bf16[1552,128]{1,0:T(8,128)(2,1)S(1)} %collective-permute-done.4.refs_3_), channel_id=1, source_target_pairs={{0,1},{1,0},{2,3},{3,2},{4,5},{5,4},{6,7},{7,6},{8,9},{9,8},{10,11... | collective-permute-start | bytes 1191944 | tf_op jit(solution)/shard_map/ppermute | solution.py:91
  53.6 2.9 %collective-permute-start.14 = (bf16[1552,128]{1,0:T(8,128)(2,1)S(1)}, bf16[1552,128]{1,0:T(8,128)(2,1)S(1)}, u32[]{:S(2)}, u32[]{:S(2)}) collective-permute-start(bf16[1552,128]{1,0:T(8,128)(2,1)S(1)} %collective-permute-done.6.refs_5_), channel_id=1, source_target_pairs={{0,1},{1,0},{2,3},{3,2},{4,5},{5,4},{6,7},{7,6},{8,9},{9,8},{10,11... | collective-permute-start | bytes 1191944 | tf_op jit(solution)/shard_map/ppermute | solution.py:91
  54.1 2.9 %collective-permute-start.15 = (bf16[1552,128]{1,0:T(8,128)(2,1)S(1)}, bf16[1552,128]{1,0:T(8,128)(2,1)S(1)}, u32[]{:S(2)}, u32[]{:S(2)}) collective-permute-start(bf16[1552,128]{1,0:T(8,128)(2,1)S(1)} %collective-permute-done.7.refs_6_), channel_id=1, source_target_pairs={{0,1},{1,0},{2,3},{3,2},{4,5},{5,4},{6,7},{7,6},{8,9},{9,8},{10,11... | collective-permute-start | bytes 1191944 | tf_op jit(solution)/shard_map/ppermute | solution.py:91
  54.2 4.1 %collective-permute-start.16 = (bf16[1552,128]{1,0:T(8,128)(2,1)S(1)}, bf16[1552,128]{1,0:T(8,128)(2,1)}, u32[]{:S(2)}, u32[]{:S(2)}) collective-permute-start(bf16[1552,128]{1,0:T(8,128)(2,1)S(1)} %collective-permute-done.8.refs_7_), channel_id=1, source_target_pairs={{0,1},{1,0},{2,3},{3,2},{4,5},{5,4},{6,7},{7,6},{8,9},{9,8},{10,11... | collective-permute-start | bytes 1191944 | tf_op jit(solution)/shard_map/ppermute | solution.py:91
  67.9 13.4 %collective-permute-start.18 = (bf16[1536,128]{1,0:T(8,128)(2,1)}, bf16[1536,128]{1,0:T(8,128)(2,1)S(1)}, u32[]{:S(2)}, u32[]{:S(2)}) collective-permute-start(bf16[1536,128]{1,0:T(8,128)(2,1)} %get-tuple-element.29), channel_id=1, source_target_pairs={{0,16},{16,0},{1,17},{17,1},{2,18},{18,2},{3,19},{19,3},{4,20},{20... | collective-permute-start | bytes 1179656 | tf_op jit(solution)/shard_map/ppermute | solution.py:412
  75.2 1.5 collective-permute-start.19
  77.3 4.0 %collective-permute-start.20 = (f32[8,128]{1,0:T(8,128)S(1)}, f32[8,128]{1,0:T(8,128)S(1)}, u32[]{:S(2)}, u32[]{:S(2)}) collective-permute-start(f32[8,128]{1,0:T(8,128)S(1)} %add.113), channel_id=1, source_target_pairs={{0,32},{32,0},{64,96},{96,64},{128,160},{160,128},{192,224},{224,1... | collective-permute-start | bytes 12296 | tf_op jit(solution)/shard_map/ppermute | solution.py:382
  82.6 23.4 %copy-start.31 = (bf16[1552,128]{1,0:T(8,128)(2,1)}, bf16[1552,128]{1,0:T(8,128)(2,1)S(1)}, u32[]{:S(2)}) copy-start(bf16[1552,128]{1,0:T(8,128)(2,1)S(1)} %pad_maximum_fusion.2) | copy-start | bytes 1191940
  82.6 9.4 %collective-permute-start.21 = (bf16[1552,128]{1,0:T(8,128)(2,1)S(1)}, bf16[1552,128]{1,0:T(8,128)(2,1)S(1)}, u32[]{:S(2)}, u32[]{:S(2)}) collective-permute-start(bf16[1552,128]{1,0:T(8,128)(2,1)S(1)} %pad_maximum_fusion.2), channel_id=1, source_target_pairs={{1,24},{0,0},{16,1},{17,17},{9,16},{8,8},{24,9},{25,25},{3,26},{2,... | collective-permute-start | bytes 1191944 | tf_op jit(solution)/shard_map/ppermute | solution.py:79
  84.5 13.8 %collective-permute-start.24 = (bf16[1552,128]{1,0:T(8,128)(2,1)S(1)}, bf16[1552,128]{1,0:T(8,128)(2,1)}, u32[]{:S(2)}, u32[]{:S(2)}) collective-permute-start(bf16[1552,128]{1,0:T(8,128)(2,1)S(1)} %pad_maximum_fusion.2), channel_id=1, source_target_pairs={{0,4},{2,6},{4,0},{6,2},{1,5},{3,7},{5,1},{7,3},{8,12},{10,14},{12... | collective-permute-start | bytes 1191944 | tf_op jit(solution)/shard_map/ppermute | solution.py:80
  86.9 14.9 %collective-permute-start.26 = (bf16[1552,128]{1,0:T(8,128)(2,1)S(1)}, bf16[1552,128]{1,0:T(8,128)(2,1)S(1)}, u32[]{:S(2)}, u32[]{:S(2)}) collective-permute-start(bf16[1552,128]{1,0:T(8,128)(2,1)S(1)} %pad_maximum_fusion.2), channel_id=1, source_target_pairs={{1,17},{0,9},{16,8},{17,24},{9,25},{8,1},{24,0},{25,16},{3,19},{2,... | collective-permute-start | bytes 1191944 | tf_op jit(solution)/shard_map/ppermute | solution.py:78
  92.0 19.1 %copy-start.15 = (bf16[1552,128]{1,0:T(8,128)(2,1)}, bf16[1552,128]{1,0:T(8,128)(2,1)S(1)}, u32[]{:S(2)}) copy-start(bf16[1552,128]{1,0:T(8,128)(2,1)S(1)} %collective-permute-done.21.refs_0_) | copy-start | bytes 1191940
  92.0 14.0 %collective-permute-start.22 = (bf16[1552,128]{1,0:T(8,128)(2,1)S(1)}, bf16[1552,128]{1,0:T(8,128)(2,1)S(1)}, u32[]{:S(2)}, u32[]{:S(2)}) collective-permute-start(bf16[1552,128]{1,0:T(8,128)(2,1)S(1)} %collective-permute-done.21.refs_0_), channel_id=1, source_target_pairs={{0,2},{2,4},{4,6},{6,0},{1,3},{3,5},{5,7},{7,1},{8,10},{10,12},{12... | collective-permute-start | bytes 1191944 | tf_op jit(solution)/shard_map/ppermute | solution.py:84
  92.0 19.1 %collective-permute-start.23 = (bf16[1552,128]{1,0:T(8,128)(2,1)S(1)}, bf16[1552,128]{1,0:T(8,128)(2,1)S(1)}, u32[]{:S(2)}, u32[]{:S(2)}) collective-permute-start(bf16[1552,128]{1,0:T(8,128)(2,1)S(1)} %collective-permute-done.21.refs_0_), channel_id=1, source_target_pairs={{0,6},{2,0},{4,2},{6,4},{1,7},{3,1},{5,3},{7,5},{8,14},{10,8},{12,... | collective-permute-start | bytes 1191944 | tf_op jit(solution)/shard_map/ppermute | solution.py:85
  98.4 17.2 %collective-permute-start.25 = (bf16[1552,128]{1,0:T(8,128)(2,1)}, bf16[1552,128]{1,0:T(8,128)(2,1)S(1)}, u32[]{:S(2)}, u32[]{:S(2)}) collective-permute-start(bf16[1552,128]{1,0:T(8,128)(2,1)} %collective-permute-done.24), channel_id=1, source_target_pairs={{1,24},{0,0},{16,1},{17,17},{9,16},{8,8},{24,9},{25,25},{3,26},{2,... | collective-permute-start | bytes 1191944 | tf_op jit(solution)/shard_map/ppermute | solution.py:87
  101.8 13.9 %collective-permute-start.27 = (bf16[1552,128]{1,0:T(8,128)(2,1)S(1)}, bf16[1552,128]{1,0:T(8,128)(2,1)S(1)}, u32[]{:S(2)}, u32[]{:S(2)}) collective-permute-start(bf16[1552,128]{1,0:T(8,128)(2,1)S(1)} %collective-permute-done.26.refs_4_), channel_id=1, source_target_pairs={{0,2},{2,4},{4,6},{6,0},{1,3},{3,5},{5,7},{7,1},{8,10},{10,12},{12... | collective-permute-start | bytes 1191944 | tf_op jit(solution)/shard_map/ppermute | solution.py:83
  103.4 12.3 %collective-permute-start.28 = (bf16[1552,128]{1,0:T(8,128)(2,1)S(1)}, bf16[1552,128]{1,0:T(8,128)(2,1)S(1)}, u32[]{:S(2)}, u32[]{:S(2)}) collective-permute-start(bf16[1552,128]{1,0:T(8,128)(2,1)S(1)} %collective-permute-done.26.refs_4_), channel_id=1, source_target_pairs={{0,6},{2,0},{4,2},{6,4},{1,7},{3,1},{5,3},{7,5},{8,14},{10,8},{12,... | collective-permute-start | bytes 1191944 | tf_op jit(solution)/shard_map/ppermute | solution.py:82
  106.0 9.7 %collective-permute-start.29 = (bf16[1552,128]{1,0:T(8,128)(2,1)}, bf16[1552,128]{1,0:T(8,128)(2,1)S(1)}, u32[]{:S(2)}, u32[]{:S(2)}) collective-permute-start(bf16[1552,128]{1,0:T(8,128)(2,1)} %collective-permute-done.24), channel_id=1, source_target_pairs={{1,17},{0,9},{16,8},{17,24},{9,25},{8,1},{24,0},{25,16},{3,19},{2,... | collective-permute-start | bytes 1191944 | tf_op jit(solution)/shard_map/ppermute | solution.py:86
  111.1 5.7 %collective-permute-start.30 = (bf16[1552,128]{1,0:T(8,128)(2,1)S(1)}, bf16[1552,128]{1,0:T(8,128)(2,1)S(1)}, u32[]{:S(2)}, u32[]{:S(2)}) collective-permute-start(bf16[1552,128]{1,0:T(8,128)(2,1)S(1)} %collective-permute-done.21.refs_0_), channel_id=1, source_target_pairs={{0,1},{1,0},{2,3},{3,2},{4,5},{5,4},{6,7},{7,6},{8,9},{9,8},{10,11... | collective-permute-start | bytes 1191944 | tf_op jit(solution)/shard_map/ppermute | solution.py:91
  115.5 1.9 %collective-permute-start.34 = (bf16[1552,128]{1,0:T(8,128)(2,1)S(1)}, bf16[1552,128]{1,0:T(8,128)(2,1)S(1)}, u32[]{:S(2)}, u32[]{:S(2)}) collective-permute-start(bf16[1552,128]{1,0:T(8,128)(2,1)S(1)} %collective-permute-done.26.refs_4_), channel_id=1, source_target_pairs={{0,1},{1,0},{2,3},{3,2},{4,5},{5,4},{6,7},{7,6},{8,9},{9,8},{10,11... | collective-permute-start | bytes 1191944 | tf_op jit(solution)/shard_map/ppermute | solution.py:91
  115.7 2.3 %collective-permute-start.31 = (bf16[1552,128]{1,0:T(8,128)(2,1)S(1)}, bf16[1552,128]{1,0:T(8,128)(2,1)S(1)}, u32[]{:S(2)}, u32[]{:S(2)}) collective-permute-start(bf16[1552,128]{1,0:T(8,128)(2,1)S(1)} %collective-permute-done.22.refs_1_), channel_id=1, source_target_pairs={{0,1},{1,0},{2,3},{3,2},{4,5},{5,4},{6,7},{7,6},{8,9},{9,8},{10,11... | collective-permute-start | bytes 1191944 | tf_op jit(solution)/shard_map/ppermute | solution.py:91
  116.3 2.3 %collective-permute-start.32 = (bf16[1552,128]{1,0:T(8,128)(2,1)S(1)}, bf16[1552,128]{1,0:T(8,128)(2,1)S(1)}, u32[]{:S(2)}, u32[]{:S(2)}) collective-permute-start(bf16[1552,128]{1,0:T(8,128)(2,1)S(1)} %collective-permute-done.23.refs_2_), channel_id=1, source_target_pairs={{0,1},{1,0},{2,3},{3,2},{4,5},{5,4},{6,7},{7,6},{8,9},{9,8},{10,11... | collective-permute-start | bytes 1191944 | tf_op jit(solution)/shard_map/ppermute | solution.py:91
  116.4 2.8 %collective-permute-start.33 = (bf16[1552,128]{1,0:T(8,128)(2,1)S(1)}, bf16[1552,128]{1,0:T(8,128)(2,1)S(1)}, u32[]{:S(2)}, u32[]{:S(2)}) collective-permute-start(bf16[1552,128]{1,0:T(8,128)(2,1)S(1)} %collective-permute-done.25.refs_3_), channel_id=1, source_target_pairs={{0,1},{1,0},{2,3},{3,2},{4,5},{5,4},{6,7},{7,6},{8,9},{9,8},{10,11... | collective-permute-start | bytes 1191944 | tf_op jit(solution)/shard_map/ppermute | solution.py:91
  116.9 2.8 %collective-permute-start.35 = (bf16[1552,128]{1,0:T(8,128)(2,1)S(1)}, bf16[1552,128]{1,0:T(8,128)(2,1)S(1)}, u32[]{:S(2)}, u32[]{:S(2)}) collective-permute-start(bf16[1552,128]{1,0:T(8,128)(2,1)S(1)} %collective-permute-done.27.refs_5_), channel_id=1, source_target_pairs={{0,1},{1,0},{2,3},{3,2},{4,5},{5,4},{6,7},{7,6},{8,9},{9,8},{10,11... | collective-permute-start | bytes 1191944 | tf_op jit(solution)/shard_map/ppermute | solution.py:91
  117.5 2.8 %collective-permute-start.36 = (bf16[1552,128]{1,0:T(8,128)(2,1)S(1)}, bf16[1552,128]{1,0:T(8,128)(2,1)S(1)}, u32[]{:S(2)}, u32[]{:S(2)}) collective-permute-start(bf16[1552,128]{1,0:T(8,128)(2,1)S(1)} %collective-permute-done.28.refs_6_), channel_id=1, source_target_pairs={{0,1},{1,0},{2,3},{3,2},{4,5},{5,4},{6,7},{7,6},{8,9},{9,8},{10,11... | collective-permute-start | bytes 1191944 | tf_op jit(solution)/shard_map/ppermute | solution.py:91
  118.0 2.8 %collective-permute-start.37 = (bf16[1552,128]{1,0:T(8,128)(2,1)S(1)}, bf16[1552,128]{1,0:T(8,128)(2,1)S(1)}, u32[]{:S(2)}, u32[]{:S(2)}) collective-permute-start(bf16[1552,128]{1,0:T(8,128)(2,1)S(1)} %collective-permute-done.29.refs_7_), channel_id=1, source_target_pairs={{0,1},{1,0},{2,3},{3,2},{4,5},{5,4},{6,7},{7,6},{8,9},{9,8},{10,11... | collective-permute-start | bytes 1191944 | tf_op jit(solution)/shard_map/ppermute | solution.py:91
  127.0 21.2 %collective-permute-start.39 = (bf16[1536,128]{1,0:T(8,128)(2,1)}, bf16[1536,128]{1,0:T(8,128)(2,1)S(1)}, u32[]{:S(2)}, u32[]{:S(2)}) collective-permute-start(bf16[1536,128]{1,0:T(8,128)(2,1)} %get-tuple-element.45), channel_id=1, source_target_pairs={{0,16},{16,0},{1,17},{17,1},{2,18},{18,2},{3,19},{19,3},{4,20},{20... | collective-permute-start | bytes 1179656 | tf_op jit(solution)/shard_map/ppermute | solution.py:430
  132.3 7.4 %collective-permute-start.38 = (f32[8,128]{1,0:T(8,128)}, f32[8,128]{1,0:T(8,128)S(1)}, u32[]{:S(2)}, u32[]{:S(2)}) collective-permute-start(f32[8,128]{1,0:T(8,128)} %get-tuple-element.43), channel_id=1, source_target_pairs={{0,64},{32,96},{64,0},{96,32},{128,192},{160,224},{192,128},{224,1... | collective-permute-start | bytes 12296 | tf_op jit(solution)/shard_map/ppermute | solution.py:382
  139.7 7.8 %collective-permute-start.40 = (f32[8,128]{1,0:T(8,128)S(1)}, f32[8,128]{1,0:T(8,128)S(1)}, u32[]{:S(2)}, u32[]{:S(2)}) collective-permute-start(f32[8,128]{1,0:T(8,128)S(1)} %add.116), channel_id=1, source_target_pairs={{0,128},{32,160},{64,192},{96,224},{128,0},{160,32},{192,64},{224,... | collective-permute-start | bytes 12296 | tf_op jit(solution)/shard_map/ppermute | solution.py:382
  (29 other events, 166.1 us)
Sparse Core Ops, SparseCore 0:
  11.4 48.2 all-gather.2
  61.5 43.8 all-gather.4

commit v4 on v3

--- a/solution.py
+++ b/solution.py
@@ -416,25 +416,25 @@
     came, energy = lax.optimization_barrier((came, energy))
     f_pay = jnp.concatenate([(own + came.astype(jnp.float32)).astype(jnp.bfloat16), in_three(energy)])
     f_pay = lax.optimization_barrier(f_pay)
+    ph = f_pay[:BODY]
     plans = []
 
     def beside(stage, *tiles):
         if stage == 0:
             return tiles
-        plans.extend(plan_lists(info, p_tiles, p_line, outs))
+        plans.extend([*plan_lists(info, p_tiles, p_line, outs), ph])
         *tiles, plans[:] = lax.optimization_barrier((*tiles, plans))
         return tiles
 
     f_tiles = spread(f_pay, beside)
     other, energy = plane_half(info, plans[0], f_tiles, p_line)
     came = lax.ppermute(other, "x_lo", ring(2, 1))
-    energy = add_partner(energy, "z", RING_Z, 2)
+    energy = add_partner(energy, "z", RING_Z, 4)
     own = later_half(1, jnp.float32, info, plans[1], f_tiles, p_line)
     own, energy = lax.optimization_barrier((own, energy))
-    energy = add_partner(energy, "z", RING_Z, 4)
+    energy = add_partner(energy, "z", RING_Z, 2)
     php = (own + came.astype(jnp.float32)).astype(jnp.bfloat16)
-    ph = f_pay[:BODY]
-    return ph.reshape(CAP, BLK, BLK), php.reshape(CAP, BLK, BLK), jnp.sum(energy)
+    return plans[2].reshape(CAP, BLK, BLK), php.reshape(CAP, BLK, BLK), jnp.sum(energy)
 
 
 def solution(mesh):

time: 158 us -> 160 us (1.013)
  waiting for transfers between devices: 35 us -> 37.5 us
    ppermute x4, waiting for transfers between devices: 3.76 us -> 7.11 us  [add_partner(): return part + lax.ppermute(part, axis, [(i, i ^ hop) for i in range(size)])]
    ppermute x2, starting transfers between devices: 6.96 us -> 4.98 us  [per_device(): came = lax.ppermute(other, 'x_lo', ring(2, 1))]
  transfers between devices with their start and end apart: 43 -> 43, of which waited for: 22 -> 23; matrix products, arithmetic and copies ran while one was open for 5% -> 5% of each run, Pallas kernels for 15% -> 15%
where the time goes in v4:
time: 160 us; the launch traced here: 159 us
  starting transfers between devices  61.1 us (38%)
  waiting for transfers between devices  37.5 us (23%)
  Pallas kernels  29.7 us (19%)
  between operations  15.8 us (10%)
  other arithmetic  11.7 us (7%)
  local copies, waits for them, and re-layouts  3.05 us (2%)
    ppermute x4, starting transfers between devices, add_partner(): return part + lax.ppermute(part, axis, [(i, i ^ hop) for i in range(size)])  10.7 us
    pallas_call x2, Pallas kernels, later_half(): pl.pallas_call(functools.partial(half_kernel, half, bool(trace)), out_sha...  10.7 us
    pallas_call x1, Pallas kernels, first_half(): pl.pallas_call(first_kernel, out_shape=[jax.ShapeDtypeStruct((BODY, BLK),...  8.83 us
    ppermute x16, starting transfers between devices, spread(): theirs = [lax.ppermute(t, 'core', ring(2, 1)) for t in mine]  8.57 us
    ppermute x2, starting transfers between devices, spread(): near_two = lax.ppermute(two, IN_CHIP_X, second)  7.45 us
    ppermute x2, waiting for transfers between devices, spread(): near = lax.ppermute(tile, IN_CHIP_X, second)  7.24 us
    ppermute x4, waiting for transfers between devices, add_partner(): return part + lax.ppermute(part, axis, [(i, i ^ hop) for i in range(size)])  7.11 us
    ppermute x2, starting transfers between devices, spread(): two = lax.ppermute(tile, 'y', ring(RING_Y, 2))  5.95 us
  transfers between devices with their start and end apart: 43, of which 23 were waited for; matrix products, arithmetic and copies ran while one was open for 5% of the time, Pallas kernels for 15%

profile of v4, /device:TPU:2, one launch (start us, length us, event | category | flops | bytes accessed | tf_op | source)
XLA Modules:
  0.0 158.9 jit_solution(697353538755209227)
XLA Ops:
  8.6 0.8 add_bitcast_fusion.1
  9.5 1.8 %pad_maximum_fusion.1 = bf16[1552,128]{1,0:T(8,128)(2,1)} fusion(bf16[16,128]{1,0:T(8,128)(2,1)S(1)} %broadcast_in_dim.93, bf16[1536,128]{1,0:T(8,128)(2,1)} %bitcast.46), kind=kLoop, calls=%fused_computation.3 | loop fusion | flops 794624 | bytes 794624 | tf_op jit(solution)/shard_map/concatenate | solution.py:403
  11.4 1.8 %pad_maximum_fusion = bf16[1552,128]{1,0:T(8,128)(2,1)} fusion(bf16[16,128]{1,0:T(8,128)(2,1)S(1)} %broadcast_in_dim.86, bf16[1536,128]{1,0:T(8,128)(2,1)} %bitcast.47), kind=kLoop, calls=%fused_computation.2 | loop fusion | flops 794624 | bytes 794624 | tf_op jit(solution)/shard_map/concatenate | solution.py:404
  13.2 1.9 %collective-permute-start = (bf16[1552,128]{1,0:T(8,128)(2,1)}, bf16[1552,128]{1,0:T(8,128)(2,1)S(1)}, u32[]{:S(2)}, u32[]{:S(2)}) collective-permute-start(bf16[1552,128]{1,0:T(8,128)(2,1)} %pad_maximum_fusion), channel_id=1, source_target_pairs={{1,24},{0,0},{16,1},{17,17},{9,16},{8,8},{24,9},{25,25},{3,26},{2,... | collective-permute-start | bytes 1191944 | tf_op jit(solution)/shard_map/ppermute | solution.py:79
  15.1 3.3 %collective-permute-start.3 = (bf16[1552,128]{1,0:T(8,128)(2,1)}, bf16[1552,128]{1,0:T(8,128)(2,1)}, u32[]{:S(2)}, u32[]{:S(2)}) collective-permute-start(bf16[1552,128]{1,0:T(8,128)(2,1)} %pad_maximum_fusion), channel_id=1, source_target_pairs={{0,4},{2,6},{4,0},{6,2},{1,5},{3,7},{5,1},{7,3},{8,12},{10,14},{12... | collective-permute-start | bytes 1191944 | tf_op jit(solution)/shard_map/ppermute | solution.py:80
  18.4 1.1 collective-permute-start.5
  19.6 3.0 %collective-permute-done.refs_0_ = bf16[1552,128]{1,0:T(8,128)(2,1)S(1)} collective-permute-done((bf16[1552,128]{1,0:T(8,128)(2,1)}, bf16[1552,128]{1,0:T(8,128)(2,1)S(1)}, u32[]{:S(2)}, u32[]{:S(2)}) %collective-permute-start) | collective-permute-done | bytes 397344 | tf_op jit(solution)/shard_map/ppermute | solution.py:79
  22.6 1.8 %collective-permute-start.1 = (bf16[1552,128]{1,0:T(8,128)(2,1)S(1)}, bf16[1552,128]{1,0:T(8,128)(2,1)S(1)}, u32[]{:S(2)}, u32[]{:S(2)}) collective-permute-start(bf16[1552,128]{1,0:T(8,128)(2,1)S(1)} %collective-permute-done.refs_0_), channel_id=1, source_target_pairs={{0,2},{2,4},{4,6},{6,0},{1,3},{3,5},{5,7},{7,1},{8,10},{10,12},{12... | collective-permute-start | bytes 1191944 | tf_op jit(solution)/shard_map/ppermute | solution.py:84
  24.4 2.5 %collective-permute-start.2 = (bf16[1552,128]{1,0:T(8,128)(2,1)S(1)}, bf16[1552,128]{1,0:T(8,128)(2,1)S(1)}, u32[]{:S(2)}, u32[]{:S(2)}) collective-permute-start(bf16[1552,128]{1,0:T(8,128)(2,1)S(1)} %collective-permute-done.refs_0_), channel_id=1, source_target_pairs={{0,6},{2,0},{4,2},{6,4},{1,7},{3,1},{5,3},{7,5},{8,14},{10,8},{12,... | collective-permute-start | bytes 1191944 | tf_op jit(solution)/shard_map/ppermute | solution.py:85
  26.9 2.3 %collective-permute-done.3 = bf16[1552,128]{1,0:T(8,128)(2,1)} collective-permute-done((bf16[1552,128]{1,0:T(8,128)(2,1)}, bf16[1552,128]{1,0:T(8,128)(2,1)}, u32[]{:S(2)}, u32[]{:S(2)}) %collective-permute-start.3) | collective-permute-done | bytes 397344 | tf_op jit(solution)/shard_map/ppermute | solution.py:80
  29.2 3.7 %collective-permute-start.4 = (bf16[1552,128]{1,0:T(8,128)(2,1)}, bf16[1552,128]{1,0:T(8,128)(2,1)S(1)}, u32[]{:S(2)}, u32[]{:S(2)}) collective-permute-start(bf16[1552,128]{1,0:T(8,128)(2,1)} %collective-permute-done.3), channel_id=1, source_target_pairs={{1,24},{0,0},{16,1},{17,17},{9,16},{8,8},{24,9},{25,25},{3,26},{2,... | collective-permute-start | bytes 1191944 | tf_op jit(solution)/shard_map/ppermute | solution.py:87
  32.9 2.1 %collective-permute-start.6 = (bf16[1552,128]{1,0:T(8,128)(2,1)S(1)}, bf16[1552,128]{1,0:T(8,128)(2,1)S(1)}, u32[]{:S(2)}, u32[]{:S(2)}) collective-permute-start(bf16[1552,128]{1,0:T(8,128)(2,1)S(1)} %collective-permute-done.5.refs_4_), channel_id=1, source_target_pairs={{0,2},{2,4},{4,6},{6,0},{1,3},{3,5},{5,7},{7,1},{8,10},{10,12},{12... | collective-permute-start | bytes 1191944 | tf_op jit(solution)/shard_map/ppermute | solution.py:83
  35.0 3.6 %collective-permute-done.17 = bf16[16,128]{1,0:T(8,128)(2,1)S(1)} collective-permute-done((bf16[16,128]{1,0:T(8,128)(2,1)S(1)}, bf16[16,128]{1,0:T(8,128)(2,1)S(1)}, u32[]{:S(2)}, u32[]{:S(2)}) %collective-permute-start.17) | collective-permute-done | bytes 4128 | tf_op jit(solution)/shard_map/ppermute | solution.py:407
  38.6 3.1 %collective-permute-start.7 = (bf16[1552,128]{1,0:T(8,128)(2,1)S(1)}, bf16[1552,128]{1,0:T(8,128)(2,1)S(1)}, u32[]{:S(2)}, u32[]{:S(2)}) collective-permute-start(bf16[1552,128]{1,0:T(8,128)(2,1)S(1)} %collective-permute-done.5.refs_4_), channel_id=1, source_target_pairs={{0,6},{2,0},{4,2},{6,4},{1,7},{3,1},{5,3},{7,5},{8,14},{10,8},{12,... | collective-permute-start | bytes 1191944 | tf_op jit(solution)/shard_map/ppermute | solution.py:82
  41.6 2.1 %collective-permute-start.8 = (bf16[1552,128]{1,0:T(8,128)(2,1)}, bf16[1552,128]{1,0:T(8,128)(2,1)S(1)}, u32[]{:S(2)}, u32[]{:S(2)}) collective-permute-start(bf16[1552,128]{1,0:T(8,128)(2,1)} %collective-permute-done.3), channel_id=1, source_target_pairs={{1,17},{0,9},{16,8},{17,24},{9,25},{8,1},{24,0},{25,16},{3,19},{2,... | collective-permute-start | bytes 1191944 | tf_op jit(solution)/shard_map/ppermute | solution.py:86
  44.6 0.8 add_bitcast_fusion.3
  45.4 4.0 %collective-permute-done.7.refs_6_ = bf16[1552,128]{1,0:T(8,128)(2,1)S(1)} collective-permute-done((bf16[1552,128]{1,0:T(8,128)(2,1)S(1)}, bf16[1552,128]{1,0:T(8,128)(2,1)S(1)}, u32[]{:S(2)}, u32[]{:S(2)}) %collective-permute-start.7) | collective-permute-done | bytes 397344 | tf_op jit(solution)/shard_map/ppermute | solution.py:82
  49.4 4.2 %collective-permute-done.8.refs_7_ = bf16[1552,128]{1,0:T(8,128)(2,1)S(1)} collective-permute-done((bf16[1552,128]{1,0:T(8,128)(2,1)}, bf16[1552,128]{1,0:T(8,128)(2,1)S(1)}, u32[]{:S(2)}, u32[]{:S(2)}) %collective-permute-start.8) | collective-permute-done | bytes 397344 | tf_op jit(solution)/shard_map/ppermute | solution.py:86
  54.6 0.7 fusion.15
  57.5 0.8 copy-done.14
  58.3 1.4 all-gather.3.cloned.1.call-done.refs_16_
  59.7 8.8 %shard_map.130 = (bf16[1536,128]{1,0:T(8,128)(2,1)}, s32[776]{0:T(1024)}, f32[8,128]{1,0:T(8,128)}, s32[8,128]{1,0:T(8,128)}) custom-call(s32[4,16]{1,0:T(4,128)} %pad_add_fusion.info, bf16[1552,128]{1,0:T(8,128)(2,1)} %copy-done, bf16[1552,128]{1,0:T(8,128)(2,1)} %copy-done.2, bf16[1552,128]{1,0:T(8,128)(2,1)} %copy-done.3, bf16[1552,128]{1,0:T(8,128)(2,1)} %copy-done.4, ...), custom_call_target="tpu_custom_call" | custom-call | flops 100000000 | bytes 20000000 | tf_op jit(solution)/shard_map/pallas_call | solution.py:339
  69.0 5.5 %shard_map.131 = (f32[1536,128]{1,0:T(8,128)}, f32[8,128]{1,0:T(8,128)}) custom-call(s32[4,16]{1,0:T(4,128)} %pad_add_fusion.info, s32[776]{0:T(1024)} %get-tuple-element.26.todo, bf16[1552,128]{1,0:T(8,128)(2,1)} %copy-done, bf16[1552,128]{1,0:T(8,128)(2,1)} %copy-done.2, bf16[1552,128]{1,0:T(8,128)(2,1)} %copy-done.3, bf16[1552,128]{1,0:T(8,128)(2,1)} %copy-done.4, ...), custom_call_target="tpu_custom_call" | custom-call | flops 100000000 | bytes 15000000 | tf_op jit(solution)/shard_map/pallas_call | solution.py:352
  74.5 0.6 collective-permute-start.19
  75.2 1.0 collective-permute-done.19
  76.2 0.7 add.113
  76.9 2.3 %collective-permute-start.20 = (f32[8,128]{1,0:T(8,128)S(1)}, f32[8,128]{1,0:T(8,128)S(1)}, u32[]{:S(2)}, u32[]{:S(2)}) collective-permute-start(f32[8,128]{1,0:T(8,128)S(1)} %add.113), channel_id=1, source_target_pairs={{0,32},{32,0},{64,96},{96,64},{128,160},{160,128},{192,224},{224,1... | collective-permute-start | bytes 12296 | tf_op jit(solution)/shard_map/ppermute | solution.py:382
  79.2 1.6 collective-permute-done.20
  80.8 1.2 add_convert_fusion.1
  82.1 2.2 %collective-permute-start.21 = (bf16[1552,128]{1,0:T(8,128)(2,1)S(1)}, bf16[1552,128]{1,0:T(8,128)(2,1)S(1)}, u32[]{:S(2)}, u32[]{:S(2)}) collective-permute-start(bf16[1552,128]{1,0:T(8,128)(2,1)S(1)} %pad_maximum_fusion.2), channel_id=1, source_target_pairs={{1,24},{0,0},{16,1},{17,17},{9,16},{8,8},{24,9},{25,25},{3,26},{2,... | collective-permute-start | bytes 1191944 | tf_op jit(solution)/shard_map/ppermute | solution.py:79
  84.3 2.7 %collective-permute-start.24 = (bf16[1552,128]{1,0:T(8,128)(2,1)S(1)}, bf16[1552,128]{1,0:T(8,128)(2,1)}, u32[]{:S(2)}, u32[]{:S(2)}) collective-permute-start(bf16[1552,128]{1,0:T(8,128)(2,1)S(1)} %pad_maximum_fusion.2), channel_id=1, source_target_pairs={{0,4},{2,6},{4,0},{6,2},{1,5},{3,7},{5,1},{7,3},{8,12},{10,14},{12... | collective-permute-start | bytes 1191944 | tf_op jit(solution)/shard_map/ppermute | solution.py:80
  87.0 4.2 %collective-permute-done.21.refs_0_ = bf16[1552,128]{1,0:T(8,128)(2,1)S(1)} collective-permute-done((bf16[1552,128]{1,0:T(8,128)(2,1)S(1)}, bf16[1552,128]{1,0:T(8,128)(2,1)S(1)}, u32[]{:S(2)}, u32[]{:S(2)}) %collective-permute-start.21) | collective-permute-done | bytes 397344 | tf_op jit(solution)/shard_map/ppermute | solution.py:79
  91.2 0.7 collective-permute-start.22
  91.9 2.5 %collective-permute-start.23 = (bf16[1552,128]{1,0:T(8,128)(2,1)S(1)}, bf16[1552,128]{1,0:T(8,128)(2,1)S(1)}, u32[]{:S(2)}, u32[]{:S(2)}) collective-permute-start(bf16[1552,128]{1,0:T(8,128)(2,1)S(1)} %collective-permute-done.21.refs_0_), channel_id=1, source_target_pairs={{0,6},{2,0},{4,2},{6,4},{1,7},{3,1},{5,3},{7,5},{8,14},{10,8},{12,... | collective-permute-start | bytes 1191944 | tf_op jit(solution)/shard_map/ppermute | solution.py:85
  94.4 3.2 %collective-permute-done.24 = bf16[1552,128]{1,0:T(8,128)(2,1)} collective-permute-done((bf16[1552,128]{1,0:T(8,128)(2,1)S(1)}, bf16[1552,128]{1,0:T(8,128)(2,1)}, u32[]{:S(2)}, u32[]{:S(2)}) %collective-permute-start.24) | collective-permute-done | bytes 397344 | tf_op jit(solution)/shard_map/ppermute | solution.py:80
  97.6 3.8 %collective-permute-start.25 = (bf16[1552,128]{1,0:T(8,128)(2,1)}, bf16[1552,128]{1,0:T(8,128)(2,1)S(1)}, u32[]{:S(2)}, u32[]{:S(2)}) collective-permute-start(bf16[1552,128]{1,0:T(8,128)(2,1)} %collective-permute-done.24), channel_id=1, source_target_pairs={{1,24},{0,0},{16,1},{17,17},{9,16},{8,8},{24,9},{25,25},{3,26},{2,... | collective-permute-start | bytes 1191944 | tf_op jit(solution)/shard_map/ppermute | solution.py:87
  101.5 1.9 %collective-permute-start.27 = (bf16[1552,128]{1,0:T(8,128)(2,1)S(1)}, bf16[1552,128]{1,0:T(8,128)(2,1)S(1)}, u32[]{:S(2)}, u32[]{:S(2)}) collective-permute-start(bf16[1552,128]{1,0:T(8,128)(2,1)S(1)} %collective-permute-done.26.refs_4_), channel_id=1, source_target_pairs={{0,2},{2,4},{4,6},{6,0},{1,3},{3,5},{5,7},{7,1},{8,10},{10,12},{12... | collective-permute-start | bytes 1191944 | tf_op jit(solution)/shard_map/ppermute | solution.py:83
  103.4 1.4 collective-permute-start.28
  105.4 5.0 %shard_map.132 = (s32[776]{0:T(1024)}, s32[776]{0:T(1024)}) custom-call(s32[4,16]{1,0:T(4,128)} %pad_add_fusion.info, bf16[1552,128]{1,0:T(8,128)(2,1)} %copy-done, bf16[1552,128]{1,0:T(8,128)(2,1)} %copy-done.2, bf16[1552,128]{1,0:T(8,128)(2,1)} %copy-done.3, bf16[1552,128]{1,0:T(8,128)(2,1)} %copy-done.4, bf16[1552,128]{1,0:T(8,128)(2,1)} %copy-done.1, ...), custom_call_target="tpu_custom_call" | custom-call | flops 1000000 | bytes 10000000 | tf_op jit(solution)/shard_map/pallas_call | solution.py:327
  110.4 0.8 slice.20
  111.2 4.8 %collective-permute-start.30 = (bf16[1552,128]{1,0:T(8,128)(2,1)S(1)}, bf16[1552,128]{1,0:T(8,128)(2,1)S(1)}, u32[]{:S(2)}, u32[]{:S(2)}) collective-permute-start(bf16[1552,128]{1,0:T(8,128)(2,1)S(1)} %collective-permute-done.21.refs_0_), channel_id=1, source_target_pairs={{0,1},{1,0},{2,3},{3,2},{4,5},{5,4},{6,7},{7,6},{8,9},{9,8},{10,11... | collective-permute-start | bytes 1191944 | tf_op jit(solution)/shard_map/ppermute | solution.py:91
  121.5 0.7 copy-done.30
  122.3 5.2 %shard_map.134 = (bf16[1536,128]{1,0:T(8,128)(2,1)}, f32[8,128]{1,0:T(8,128)}) custom-call(s32[4,16]{1,0:T(4,128)} %pad_add_fusion.info, s32[776]{0:T(1024)} %get-tuple-element.44.todo, bf16[1552,128]{1,0:T(8,128)(2,1)} %copy-done.15, bf16[1552,128]{1,0:T(8,128)(2,1)} %copy-done.17, bf16[1552,128]{1,0:T(8,128)(2,1)} %copy-done.18, ...), custom_call_target="tpu_custom_call" | custom-call | flops 100000000 | bytes 15000000 | tf_op jit(solution)/shard_map/pallas_call | solution.py:365
  127.5 4.6 %collective-permute-start.39 = (bf16[1536,128]{1,0:T(8,128)(2,1)}, bf16[1536,128]{1,0:T(8,128)(2,1)S(1)}, u32[]{:S(2)}, u32[]{:S(2)}) collective-permute-start(bf16[1536,128]{1,0:T(8,128)(2,1)} %get-tuple-element.47), channel_id=1, source_target_pairs={{0,16},{16,0},{1,17},{17,1},{2,18},{18,2},{3,19},{19,3},{4,20},{20... | collective-permute-start | bytes 1179656 | tf_op jit(solution)/shard_map/ppermute | solution.py:431
  132.0 7.7 %collective-permute-start.38 = (f32[8,128]{1,0:T(8,128)}, f32[8,128]{1,0:T(8,128)S(1)}, u32[]{:S(2)}, u32[]{:S(2)}) collective-permute-start(f32[8,128]{1,0:T(8,128)} %get-tuple-element.45), channel_id=1, source_target_pairs={{0,128},{32,160},{64,192},{96,224},{128,0},{160,32},{192,64},{224,... | collective-permute-start | bytes 12296 | tf_op jit(solution)/shard_map/ppermute | solution.py:382
  139.8 5.2 %shard_map.133 = f32[1536,128]{1,0:T(8,128)} custom-call(s32[4,16]{1,0:T(4,128)} %pad_add_fusion.info, s32[776]{0:T(1024)} %get-tuple-element.37.todo, bf16[1552,128]{1,0:T(8,128)(2,1)} %copy-done.15, bf16[1552,128]{1,0:T(8,128)(2,1)} %copy-done.17, bf16[1552,128]{1,0:T(8,128)(2,1)} %copy-done.18, bf16[1552,128]{1,0:T(8,128)(2,1)} %copy-done.19, ...), custom_call_target="tpu_custom_call" | custom-call | flops 100000000 | bytes 15000000 | tf_op jit(solution)/shard_map/pallas_call | solution.py:352
  145.0 4.5 %collective-permute-done.40 = f32[8,128]{1,0:T(8,128)S(1)} collective-permute-done((f32[8,128]{1,0:T(8,128)S(1)}, f32[8,128]{1,0:T(8,128)S(1)}, u32[]{:S(2)}, u32[]{:S(2)}) %collective-permute-start.40) | collective-permute-done | bytes 4128 | tf_op jit(solution)/shard_map/ppermute | solution.py:382
  150.1 2.0 %add_convert_fusion = bf16[1536,128]{1,0:T(8,128)(2,1)} fusion(f32[1536,128]{1,0:T(8,128)} %shard_map.133, bf16[1536,128]{1,0:T(8,128)(2,1)S(1)} %collective-permute-done.39), kind=kLoop, calls=%fused_computation | loop fusion | flops 589824 | bytes 1572864 | tf_op jit(solution)/shard_map/convert_element_type | solution.py:436
  (144 shorter events, 11.8 us)
Async XLA Ops:
  7.2 52.5 %all-gather.3.cloned.1.call-start = ((), (), s32[]{:S(2)}) async-start(), calls=%async_computation | async-start | bytes 3575808 | tf_op jit(solution)/shard_map/all_gather | solution.py:405
  11.3 94.1 %all-gather.5.cloned.1.call-start = ((), (), s32[]{:S(2)}) async-start(), calls=%async_computation.1 | async-start | bytes 3575808 | tf_op jit(solution)/shard_map/all_gather | solution.py:406
  13.2 9.3 %collective-permute-start = (bf16[1552,128]{1,0:T(8,128)(2,1)}, bf16[1552,128]{1,0:T(8,128)(2,1)S(1)}, u32[]{:S(2)}, u32[]{:S(2)}) collective-permute-start(bf16[1552,128]{1,0:T(8,128)(2,1)} %pad_maximum_fusion), channel_id=1, source_target_pairs={{1,24},{0,0},{16,1},{17,17},{9,16},{8,8},{24,9},{25,25},{3,26},{2,... | collective-permute-start | bytes 1191944 | tf_op jit(solution)/shard_map/ppermute | solution.py:79
  15.1 14.0 %collective-permute-start.3 = (bf16[1552,128]{1,0:T(8,128)(2,1)}, bf16[1552,128]{1,0:T(8,128)(2,1)}, u32[]{:S(2)}, u32[]{:S(2)}) collective-permute-start(bf16[1552,128]{1,0:T(8,128)(2,1)} %pad_maximum_fusion), channel_id=1, source_target_pairs={{0,4},{2,6},{4,0},{6,2},{1,5},{3,7},{5,1},{7,3},{8,12},{10,14},{12... | collective-permute-start | bytes 1191944 | tf_op jit(solution)/shard_map/ppermute | solution.py:80
  18.4 14.4 %collective-permute-start.5 = (bf16[1552,128]{1,0:T(8,128)(2,1)}, bf16[1552,128]{1,0:T(8,128)(2,1)S(1)}, u32[]{:S(2)}, u32[]{:S(2)}) collective-permute-start(bf16[1552,128]{1,0:T(8,128)(2,1)} %pad_maximum_fusion), channel_id=1, source_target_pairs={{1,17},{0,9},{16,8},{17,24},{9,25},{8,1},{24,0},{25,16},{3,19},{2,... | collective-permute-start | bytes 1191944 | tf_op jit(solution)/shard_map/ppermute | solution.py:78
  22.6 37.1 %copy-start = (bf16[1552,128]{1,0:T(8,128)(2,1)}, bf16[1552,128]{1,0:T(8,128)(2,1)S(1)}, u32[]{:S(2)}) copy-start(bf16[1552,128]{1,0:T(8,128)(2,1)S(1)} %collective-permute-done.refs_0_) | copy-start | bytes 1191940
  22.6 19.1 %collective-permute-start.1 = (bf16[1552,128]{1,0:T(8,128)(2,1)S(1)}, bf16[1552,128]{1,0:T(8,128)(2,1)S(1)}, u32[]{:S(2)}, u32[]{:S(2)}) collective-permute-start(bf16[1552,128]{1,0:T(8,128)(2,1)S(1)} %collective-permute-done.refs_0_), channel_id=1, source_target_pairs={{0,2},{2,4},{4,6},{6,0},{1,3},{3,5},{5,7},{7,1},{8,10},{10,12},{12... | collective-permute-start | bytes 1191944 | tf_op jit(solution)/shard_map/ppermute | solution.py:84
  24.4 19.3 %collective-permute-start.2 = (bf16[1552,128]{1,0:T(8,128)(2,1)S(1)}, bf16[1552,128]{1,0:T(8,128)(2,1)S(1)}, u32[]{:S(2)}, u32[]{:S(2)}) collective-permute-start(bf16[1552,128]{1,0:T(8,128)(2,1)S(1)} %collective-permute-done.refs_0_), channel_id=1, source_target_pairs={{0,6},{2,0},{4,2},{6,4},{1,7},{3,1},{5,3},{7,5},{8,14},{10,8},{12,... | collective-permute-start | bytes 1191944 | tf_op jit(solution)/shard_map/ppermute | solution.py:85
  29.2 14.5 %collective-permute-start.4 = (bf16[1552,128]{1,0:T(8,128)(2,1)}, bf16[1552,128]{1,0:T(8,128)(2,1)S(1)}, u32[]{:S(2)}, u32[]{:S(2)}) collective-permute-start(bf16[1552,128]{1,0:T(8,128)(2,1)} %collective-permute-done.3), channel_id=1, source_target_pairs={{1,24},{0,0},{16,1},{17,17},{9,16},{8,8},{24,9},{25,25},{3,26},{2,... | collective-permute-start | bytes 1191944 | tf_op jit(solution)/shard_map/ppermute | solution.py:87
  32.9 26.8 %copy-start.1 = (bf16[1552,128]{1,0:T(8,128)(2,1)}, bf16[1552,128]{1,0:T(8,128)(2,1)S(1)}, u32[]{:S(2)}) copy-start(bf16[1552,128]{1,0:T(8,128)(2,1)S(1)} %collective-permute-done.5.refs_4_) | copy-start | bytes 1191940
  32.9 11.7 %collective-permute-start.6 = (bf16[1552,128]{1,0:T(8,128)(2,1)S(1)}, bf16[1552,128]{1,0:T(8,128)(2,1)S(1)}, u32[]{:S(2)}, u32[]{:S(2)}) collective-permute-start(bf16[1552,128]{1,0:T(8,128)(2,1)S(1)} %collective-permute-done.5.refs_4_), channel_id=1, source_target_pairs={{0,2},{2,4},{4,6},{6,0},{1,3},{3,5},{5,7},{7,1},{8,10},{10,12},{12... | collective-permute-start | bytes 1191944 | tf_op jit(solution)/shard_map/ppermute | solution.py:83
  35.0 3.6 %collective-permute-start.17 = (bf16[16,128]{1,0:T(8,128)(2,1)S(1)}, bf16[16,128]{1,0:T(8,128)(2,1)S(1)}, u32[]{:S(2)}, u32[]{:S(2)}) collective-permute-start(bf16[16,128]{1,0:T(8,128)(2,1)S(1)} %broadcast_in_dim.86), channel_id=1, source_target_pairs={{0,16},{16,0},{1,17},{17,1},{2,18},{18,2},{3,19},{19,3},{4,20},{20... | collective-permute-start | bytes 12296 | tf_op jit(solution)/shard_map/ppermute | solution.py:407
  38.6 10.8 %collective-permute-start.7 = (bf16[1552,128]{1,0:T(8,128)(2,1)S(1)}, bf16[1552,128]{1,0:T(8,128)(2,1)S(1)}, u32[]{:S(2)}, u32[]{:S(2)}) collective-permute-start(bf16[1552,128]{1,0:T(8,128)(2,1)S(1)} %collective-permute-done.5.refs_4_), channel_id=1, source_target_pairs={{0,6},{2,0},{4,2},{6,4},{1,7},{3,1},{5,3},{7,5},{8,14},{10,8},{12,... | collective-permute-start | bytes 1191944 | tf_op jit(solution)/shard_map/ppermute | solution.py:82
  41.6 18.1 %copy-start.2 = (bf16[1552,128]{1,0:T(8,128)(2,1)}, bf16[1552,128]{1,0:T(8,128)(2,1)S(1)}, u32[]{:S(2)}) copy-start(bf16[1552,128]{1,0:T(8,128)(2,1)S(1)} %collective-permute-done.1.refs_1_) | copy-start | bytes 1191940
  41.6 11.9 %collective-permute-start.8 = (bf16[1552,128]{1,0:T(8,128)(2,1)}, bf16[1552,128]{1,0:T(8,128)(2,1)S(1)}, u32[]{:S(2)}, u32[]{:S(2)}) collective-permute-start(bf16[1552,128]{1,0:T(8,128)(2,1)} %collective-permute-done.3), channel_id=1, source_target_pairs={{1,17},{0,9},{16,8},{17,24},{9,25},{8,1},{24,0},{25,16},{3,19},{2,... | collective-permute-start | bytes 1191944 | tf_op jit(solution)/shard_map/ppermute | solution.py:86
  43.7 9.8 %collective-permute-start.9 = (bf16[1552,128]{1,0:T(8,128)(2,1)S(1)}, bf16[1552,128]{1,0:T(8,128)(2,1)S(1)}, u32[]{:S(2)}, u32[]{:S(2)}) collective-permute-start(bf16[1552,128]{1,0:T(8,128)(2,1)S(1)} %collective-permute-done.refs_0_), channel_id=1, source_target_pairs={{0,1},{1,0},{2,3},{3,2},{4,5},{5,4},{6,7},{7,6},{8,9},{9,8},{10,11... | collective-permute-start | bytes 1191944 | tf_op jit(solution)/shard_map/ppermute | solution.py:91
  43.8 10.3 %collective-permute-start.13 = (bf16[1552,128]{1,0:T(8,128)(2,1)S(1)}, bf16[1552,128]{1,0:T(8,128)(2,1)S(1)}, u32[]{:S(2)}, u32[]{:S(2)}) collective-permute-start(bf16[1552,128]{1,0:T(8,128)(2,1)S(1)} %collective-permute-done.5.refs_4_), channel_id=1, source_target_pairs={{0,1},{1,0},{2,3},{3,2},{4,5},{5,4},{6,7},{7,6},{8,9},{9,8},{10,11... | collective-permute-start | bytes 1191944 | tf_op jit(solution)/shard_map/ppermute | solution.py:91
  44.6 9.6 %collective-permute-start.10 = (bf16[1552,128]{1,0:T(8,128)(2,1)S(1)}, bf16[1552,128]{1,0:T(8,128)(2,1)S(1)}, u32[]{:S(2)}, u32[]{:S(2)}) collective-permute-start(bf16[1552,128]{1,0:T(8,128)(2,1)S(1)} %collective-permute-done.1.refs_1_), channel_id=1, source_target_pairs={{0,1},{1,0},{2,3},{3,2},{4,5},{5,4},{6,7},{7,6},{8,9},{9,8},{10,11... | collective-permute-start | bytes 1191944 | tf_op jit(solution)/shard_map/ppermute | solution.py:91
  49.4 7.1 %collective-permute-start.11 = (bf16[1552,128]{1,0:T(8,128)(2,1)S(1)}, bf16[1552,128]{1,0:T(8,128)(2,1)S(1)}, u32[]{:S(2)}, u32[]{:S(2)}) collective-permute-start(bf16[1552,128]{1,0:T(8,128)(2,1)S(1)} %collective-permute-done.2.refs_2_), channel_id=1, source_target_pairs={{0,1},{1,0},{2,3},{3,2},{4,5},{5,4},{6,7},{7,6},{8,9},{9,8},{10,11... | collective-permute-start | bytes 1191944 | tf_op jit(solution)/shard_map/ppermute | solution.py:91
  53.6 2.9 %collective-permute-start.12 = (bf16[1552,128]{1,0:T(8,128)(2,1)S(1)}, bf16[1552,128]{1,0:T(8,128)(2,1)S(1)}, u32[]{:S(2)}, u32[]{:S(2)}) collective-permute-start(bf16[1552,128]{1,0:T(8,128)(2,1)S(1)} %collective-permute-done.4.refs_3_), channel_id=1, source_target_pairs={{0,1},{1,0},{2,3},{3,2},{4,5},{5,4},{6,7},{7,6},{8,9},{9,8},{10,11... | collective-permute-start | bytes 1191944 | tf_op jit(solution)/shard_map/ppermute | solution.py:91
  53.6 2.9 %collective-permute-start.14 = (bf16[1552,128]{1,0:T(8,128)(2,1)S(1)}, bf16[1552,128]{1,0:T(8,128)(2,1)S(1)}, u32[]{:S(2)}, u32[]{:S(2)}) collective-permute-start(bf16[1552,128]{1,0:T(8,128)(2,1)S(1)} %collective-permute-done.6.refs_5_), channel_id=1, source_target_pairs={{0,1},{1,0},{2,3},{3,2},{4,5},{5,4},{6,7},{7,6},{8,9},{9,8},{10,11... | collective-permute-start | bytes 1191944 | tf_op jit(solution)/shard_map/ppermute | solution.py:91
  54.1 2.9 %collective-permute-start.15 = (bf16[1552,128]{1,0:T(8,128)(2,1)S(1)}, bf16[1552,128]{1,0:T(8,128)(2,1)S(1)}, u32[]{:S(2)}, u32[]{:S(2)}) collective-permute-start(bf16[1552,128]{1,0:T(8,128)(2,1)S(1)} %collective-permute-done.7.refs_6_), channel_id=1, source_target_pairs={{0,1},{1,0},{2,3},{3,2},{4,5},{5,4},{6,7},{7,6},{8,9},{9,8},{10,11... | collective-permute-start | bytes 1191944 | tf_op jit(solution)/shard_map/ppermute | solution.py:91
  54.2 4.1 %collective-permute-start.16 = (bf16[1552,128]{1,0:T(8,128)(2,1)S(1)}, bf16[1552,128]{1,0:T(8,128)(2,1)}, u32[]{:S(2)}, u32[]{:S(2)}) collective-permute-start(bf16[1552,128]{1,0:T(8,128)(2,1)S(1)} %collective-permute-done.8.refs_7_), channel_id=1, source_target_pairs={{0,1},{1,0},{2,3},{3,2},{4,5},{5,4},{6,7},{7,6},{8,9},{9,8},{10,11... | collective-permute-start | bytes 1191944 | tf_op jit(solution)/shard_map/ppermute | solution.py:91
  68.6 12.2 %collective-permute-start.18 = (bf16[1536,128]{1,0:T(8,128)(2,1)}, bf16[1536,128]{1,0:T(8,128)(2,1)S(1)}, u32[]{:S(2)}, u32[]{:S(2)}) collective-permute-start(bf16[1536,128]{1,0:T(8,128)(2,1)} %get-tuple-element.30), channel_id=1, source_target_pairs={{0,16},{16,0},{1,17},{17,1},{2,18},{18,2},{3,19},{19,3},{4,20},{20... | collective-permute-start | bytes 1179656 | tf_op jit(solution)/shard_map/ppermute | solution.py:412
  74.5 1.7 %collective-permute-start.19 = (f32[8,128]{1,0:T(8,128)}, f32[8,128]{1,0:T(8,128)S(1)}, u32[]{:S(2)}, u32[]{:S(2)}) collective-permute-start(f32[8,128]{1,0:T(8,128)} %get-tuple-element.31), channel_id=1, source_target_pairs={{0,1},{1,0},{2,3},{3,2},{4,5},{5,4},{6,7},{7,6},{8,9},{9,8},{10,11... | collective-permute-start | bytes 12296 | tf_op jit(solution)/shard_map/ppermute | solution.py:382
  76.9 3.8 %collective-permute-start.20 = (f32[8,128]{1,0:T(8,128)S(1)}, f32[8,128]{1,0:T(8,128)S(1)}, u32[]{:S(2)}, u32[]{:S(2)}) collective-permute-start(f32[8,128]{1,0:T(8,128)S(1)} %add.113), channel_id=1, source_target_pairs={{0,32},{32,0},{64,96},{96,64},{128,160},{160,128},{192,224},{224,1... | collective-permute-start | bytes 12296 | tf_op jit(solution)/shard_map/ppermute | solution.py:382
  82.0 23.3 %copy-start.31 = (bf16[1552,128]{1,0:T(8,128)(2,1)}, bf16[1552,128]{1,0:T(8,128)(2,1)S(1)}, u32[]{:S(2)}) copy-start(bf16[1552,128]{1,0:T(8,128)(2,1)S(1)} %pad_maximum_fusion.2) | copy-start | bytes 1191940
  82.1 9.1 %collective-permute-start.21 = (bf16[1552,128]{1,0:T(8,128)(2,1)S(1)}, bf16[1552,128]{1,0:T(8,128)(2,1)S(1)}, u32[]{:S(2)}, u32[]{:S(2)}) collective-permute-start(bf16[1552,128]{1,0:T(8,128)(2,1)S(1)} %pad_maximum_fusion.2), channel_id=1, source_target_pairs={{1,24},{0,0},{16,1},{17,17},{9,16},{8,8},{24,9},{25,25},{3,26},{2,... | collective-permute-start | bytes 1191944 | tf_op jit(solution)/shard_map/ppermute | solution.py:79
  84.3 13.4 %collective-permute-start.24 = (bf16[1552,128]{1,0:T(8,128)(2,1)S(1)}, bf16[1552,128]{1,0:T(8,128)(2,1)}, u32[]{:S(2)}, u32[]{:S(2)}) collective-permute-start(bf16[1552,128]{1,0:T(8,128)(2,1)S(1)} %pad_maximum_fusion.2), channel_id=1, source_target_pairs={{0,4},{2,6},{4,0},{6,2},{1,5},{3,7},{5,1},{7,3},{8,12},{10,14},{12... | collective-permute-start | bytes 1191944 | tf_op jit(solution)/shard_map/ppermute | solution.py:80
  87.0 14.5 %collective-permute-start.26 = (bf16[1552,128]{1,0:T(8,128)(2,1)S(1)}, bf16[1552,128]{1,0:T(8,128)(2,1)S(1)}, u32[]{:S(2)}, u32[]{:S(2)}) collective-permute-start(bf16[1552,128]{1,0:T(8,128)(2,1)S(1)} %pad_maximum_fusion.2), channel_id=1, source_target_pairs={{1,17},{0,9},{16,8},{17,24},{9,25},{8,1},{24,0},{25,16},{3,19},{2,... | collective-permute-start | bytes 1191944 | tf_op jit(solution)/shard_map/ppermute | solution.py:78
  91.2 20.0 %copy-start.15 = (bf16[1552,128]{1,0:T(8,128)(2,1)}, bf16[1552,128]{1,0:T(8,128)(2,1)S(1)}, u32[]{:S(2)}) copy-start(bf16[1552,128]{1,0:T(8,128)(2,1)S(1)} %collective-permute-done.21.refs_0_) | copy-start | bytes 1191940
  91.2 14.1 %collective-permute-start.22 = (bf16[1552,128]{1,0:T(8,128)(2,1)S(1)}, bf16[1552,128]{1,0:T(8,128)(2,1)S(1)}, u32[]{:S(2)}, u32[]{:S(2)}) collective-permute-start(bf16[1552,128]{1,0:T(8,128)(2,1)S(1)} %collective-permute-done.21.refs_0_), channel_id=1, source_target_pairs={{0,2},{2,4},{4,6},{6,0},{1,3},{3,5},{5,7},{7,1},{8,10},{10,12},{12... | collective-permute-start | bytes 1191944 | tf_op jit(solution)/shard_map/ppermute | solution.py:84
  91.9 19.3 %collective-permute-start.23 = (bf16[1552,128]{1,0:T(8,128)(2,1)S(1)}, bf16[1552,128]{1,0:T(8,128)(2,1)S(1)}, u32[]{:S(2)}, u32[]{:S(2)}) collective-permute-start(bf16[1552,128]{1,0:T(8,128)(2,1)S(1)} %collective-permute-done.21.refs_0_), channel_id=1, source_target_pairs={{0,6},{2,0},{4,2},{6,4},{1,7},{3,1},{5,3},{7,5},{8,14},{10,8},{12,... | collective-permute-start | bytes 1191944 | tf_op jit(solution)/shard_map/ppermute | solution.py:85
  97.6 18.3 %collective-permute-start.25 = (bf16[1552,128]{1,0:T(8,128)(2,1)}, bf16[1552,128]{1,0:T(8,128)(2,1)S(1)}, u32[]{:S(2)}, u32[]{:S(2)}) collective-permute-start(bf16[1552,128]{1,0:T(8,128)(2,1)} %collective-permute-done.24), channel_id=1, source_target_pairs={{1,24},{0,0},{16,1},{17,17},{9,16},{8,8},{24,9},{25,25},{3,26},{2,... | collective-permute-start | bytes 1191944 | tf_op jit(solution)/shard_map/ppermute | solution.py:87
  101.5 14.7 %collective-permute-start.27 = (bf16[1552,128]{1,0:T(8,128)(2,1)S(1)}, bf16[1552,128]{1,0:T(8,128)(2,1)S(1)}, u32[]{:S(2)}, u32[]{:S(2)}) collective-permute-start(bf16[1552,128]{1,0:T(8,128)(2,1)S(1)} %collective-permute-done.26.refs_4_), channel_id=1, source_target_pairs={{0,2},{2,4},{4,6},{6,0},{1,3},{3,5},{5,7},{7,1},{8,10},{10,12},{12... | collective-permute-start | bytes 1191944 | tf_op jit(solution)/shard_map/ppermute | solution.py:83
  103.4 12.7 %collective-permute-start.28 = (bf16[1552,128]{1,0:T(8,128)(2,1)S(1)}, bf16[1552,128]{1,0:T(8,128)(2,1)S(1)}, u32[]{:S(2)}, u32[]{:S(2)}) collective-permute-start(bf16[1552,128]{1,0:T(8,128)(2,1)S(1)} %collective-permute-done.26.refs_4_), channel_id=1, source_target_pairs={{0,6},{2,0},{4,2},{6,4},{1,7},{3,1},{5,3},{7,5},{8,14},{10,8},{12,... | collective-permute-start | bytes 1191944 | tf_op jit(solution)/shard_map/ppermute | solution.py:82
  105.3 10.8 %collective-permute-start.29 = (bf16[1552,128]{1,0:T(8,128)(2,1)}, bf16[1552,128]{1,0:T(8,128)(2,1)S(1)}, u32[]{:S(2)}, u32[]{:S(2)}) collective-permute-start(bf16[1552,128]{1,0:T(8,128)(2,1)} %collective-permute-done.24), channel_id=1, source_target_pairs={{1,17},{0,9},{16,8},{17,24},{9,25},{8,1},{24,0},{25,16},{3,19},{2,... | collective-permute-start | bytes 1191944 | tf_op jit(solution)/shard_map/ppermute | solution.py:86
  111.2 6.1 %collective-permute-start.30 = (bf16[1552,128]{1,0:T(8,128)(2,1)S(1)}, bf16[1552,128]{1,0:T(8,128)(2,1)S(1)}, u32[]{:S(2)}, u32[]{:S(2)}) collective-permute-start(bf16[1552,128]{1,0:T(8,128)(2,1)S(1)} %collective-permute-done.21.refs_0_), channel_id=1, source_target_pairs={{0,1},{1,0},{2,3},{3,2},{4,5},{5,4},{6,7},{7,6},{8,9},{9,8},{10,11... | collective-permute-start | bytes 1191944 | tf_op jit(solution)/shard_map/ppermute | solution.py:91
  116.0 1.9 %collective-permute-start.34 = (bf16[1552,128]{1,0:T(8,128)(2,1)S(1)}, bf16[1552,128]{1,0:T(8,128)(2,1)S(1)}, u32[]{:S(2)}, u32[]{:S(2)}) collective-permute-start(bf16[1552,128]{1,0:T(8,128)(2,1)S(1)} %collective-permute-done.26.refs_4_), channel_id=1, source_target_pairs={{0,1},{1,0},{2,3},{3,2},{4,5},{5,4},{6,7},{7,6},{8,9},{9,8},{10,11... | collective-permute-start | bytes 1191944 | tf_op jit(solution)/shard_map/ppermute | solution.py:91
  116.2 2.3 %collective-permute-start.31 = (bf16[1552,128]{1,0:T(8,128)(2,1)S(1)}, bf16[1552,128]{1,0:T(8,128)(2,1)S(1)}, u32[]{:S(2)}, u32[]{:S(2)}) collective-permute-start(bf16[1552,128]{1,0:T(8,128)(2,1)S(1)} %collective-permute-done.22.refs_1_), channel_id=1, source_target_pairs={{0,1},{1,0},{2,3},{3,2},{4,5},{5,4},{6,7},{7,6},{8,9},{9,8},{10,11... | collective-permute-start | bytes 1191944 | tf_op jit(solution)/shard_map/ppermute | solution.py:91
  116.7 2.3 %collective-permute-start.32 = (bf16[1552,128]{1,0:T(8,128)(2,1)S(1)}, bf16[1552,128]{1,0:T(8,128)(2,1)S(1)}, u32[]{:S(2)}, u32[]{:S(2)}) collective-permute-start(bf16[1552,128]{1,0:T(8,128)(2,1)S(1)} %collective-permute-done.23.refs_2_), channel_id=1, source_target_pairs={{0,1},{1,0},{2,3},{3,2},{4,5},{5,4},{6,7},{7,6},{8,9},{9,8},{10,11... | collective-permute-start | bytes 1191944 | tf_op jit(solution)/shard_map/ppermute | solution.py:91
  116.8 2.8 %collective-permute-start.33 = (bf16[1552,128]{1,0:T(8,128)(2,1)S(1)}, bf16[1552,128]{1,0:T(8,128)(2,1)S(1)}, u32[]{:S(2)}, u32[]{:S(2)}) collective-permute-start(bf16[1552,128]{1,0:T(8,128)(2,1)S(1)} %collective-permute-done.25.refs_3_), channel_id=1, source_target_pairs={{0,1},{1,0},{2,3},{3,2},{4,5},{5,4},{6,7},{7,6},{8,9},{9,8},{10,11... | collective-permute-start | bytes 1191944 | tf_op jit(solution)/shard_map/ppermute | solution.py:91
  117.3 2.8 %collective-permute-start.35 = (bf16[1552,128]{1,0:T(8,128)(2,1)S(1)}, bf16[1552,128]{1,0:T(8,128)(2,1)S(1)}, u32[]{:S(2)}, u32[]{:S(2)}) collective-permute-start(bf16[1552,128]{1,0:T(8,128)(2,1)S(1)} %collective-permute-done.27.refs_5_), channel_id=1, source_target_pairs={{0,1},{1,0},{2,3},{3,2},{4,5},{5,4},{6,7},{7,6},{8,9},{9,8},{10,11... | collective-permute-start | bytes 1191944 | tf_op jit(solution)/shard_map/ppermute | solution.py:91
  117.9 2.8 %collective-permute-start.36 = (bf16[1552,128]{1,0:T(8,128)(2,1)S(1)}, bf16[1552,128]{1,0:T(8,128)(2,1)S(1)}, u32[]{:S(2)}, u32[]{:S(2)}) collective-permute-start(bf16[1552,128]{1,0:T(8,128)(2,1)S(1)} %collective-permute-done.28.refs_6_), channel_id=1, source_target_pairs={{0,1},{1,0},{2,3},{3,2},{4,5},{5,4},{6,7},{7,6},{8,9},{9,8},{10,11... | collective-permute-start | bytes 1191944 | tf_op jit(solution)/shard_map/ppermute | solution.py:91
  118.5 2.8 %collective-permute-start.37 = (bf16[1552,128]{1,0:T(8,128)(2,1)S(1)}, bf16[1552,128]{1,0:T(8,128)(2,1)S(1)}, u32[]{:S(2)}, u32[]{:S(2)}) collective-permute-start(bf16[1552,128]{1,0:T(8,128)(2,1)S(1)} %collective-permute-done.29.refs_7_), channel_id=1, source_target_pairs={{0,1},{1,0},{2,3},{3,2},{4,5},{5,4},{6,7},{7,6},{8,9},{9,8},{10,11... | collective-permute-start | bytes 1191944 | tf_op jit(solution)/shard_map/ppermute | solution.py:91
  127.5 22.7 %collective-permute-start.39 = (bf16[1536,128]{1,0:T(8,128)(2,1)}, bf16[1536,128]{1,0:T(8,128)(2,1)S(1)}, u32[]{:S(2)}, u32[]{:S(2)}) collective-permute-start(bf16[1536,128]{1,0:T(8,128)(2,1)} %get-tuple-element.47), channel_id=1, source_target_pairs={{0,16},{16,0},{1,17},{17,1},{2,18},{18,2},{3,19},{19,3},{4,20},{20... | collective-permute-start | bytes 1179656 | tf_op jit(solution)/shard_map/ppermute | solution.py:431
  132.0 12.9 %collective-permute-start.38 = (f32[8,128]{1,0:T(8,128)}, f32[8,128]{1,0:T(8,128)S(1)}, u32[]{:S(2)}, u32[]{:S(2)}) collective-permute-start(f32[8,128]{1,0:T(8,128)} %get-tuple-element.45), channel_id=1, source_target_pairs={{0,128},{32,160},{64,192},{96,224},{128,0},{160,32},{192,64},{224,... | collective-permute-start | bytes 12296 | tf_op jit(solution)/shard_map/ppermute | solution.py:382
  144.9 4.6 %collective-permute-start.40 = (f32[8,128]{1,0:T(8,128)S(1)}, f32[8,128]{1,0:T(8,128)S(1)}, u32[]{:S(2)}, u32[]{:S(2)}) collective-permute-start(f32[8,128]{1,0:T(8,128)S(1)} %add.116), channel_id=1, source_target_pairs={{0,64},{32,96},{64,0},{96,32},{128,192},{160,224},{192,128},{224,1... | collective-permute-start | bytes 12296 | tf_op jit(solution)/shard_map/ppermute | solution.py:382
  (29 other events, 165.2 us)
Sparse Core Ops, SparseCore 0:
  11.4 48.2 all-gather.2
  61.5 43.8 all-gather.4
